TPU v7x, 512 devices: a whole 4x8x8 slice. The times are simulated.
512 devices in a mesh: slab: 8 (over z_lo, core), subj: 32 (over x, y), comp: 2 (over z_hi).
Axes of the slice: x: 4, y: 8, z: 8 (z_hi: 2, z_lo: 4; z = z_hi * 4 + z_lo), core: 2. Of those that a mesh axis runs over, the one named last changes fastest.
Arguments:
- scans: bfloat16 [14336, 8, 32, 128], P('subj', 'slab'), may hold values from -6 to 6
- maps: bfloat16 [256, 8, 32, 128], P('comp', 'slab'), may hold values from -4 to 4
- gram_old: float32 [256, 256], P('comp'), may hold values from -0.04 to 2, as said below
- stats_old: float32 [256, 8, 32, 128], P('comp', 'slab', 'subj'), may hold values from -6 to 6
- kept: int32 [32], P('subj'), may hold values from 224 to 448, as said below
Outputs:
- maps_new: bfloat16 [256, 8, 32, 128], P('comp', 'slab', 'subj')
- stats_new: float32 [256, 8, 32, 128], P('comp', 'slab', 'subj')
- gram_new: float32 [256, 256], P('comp')
- codes: float32 [14336, 256], P('subj', 'comp')
Inputs may be any that keep to these rules, and one draw needn't show every extreme that they name: Subject s uses its volumes 0 to kept[s] - 1 in the statistics; some subject keeps all 448. `gram_old`: Symmetric, with a diagonal of 0.5 or more.
All inputs are finite; a program needn't handle non-finite values.
Results may differ from a plain program's by a relative error of at most 0.017.
Values may be sent and summed in bfloat16 or wider, within the bound.
No kernel may reach another device: no remote copies, remote signals or barrier semaphores. Data moves between devices by JAX's collectives and lax.ppermute only.
A program may use at most 64 MiB of HBM per device.

v0:
```python
import math

import jax
import jax.numpy as jnp
from jax import lax
from jax.sharding import PartitionSpec as P

COMPONENTS = 256
ITERS = 12


def padded_2(block, sides, width):
    for axis, dim in sides:
        count = lax.axis_size(axis)
        forward = [(i, i + 1) for i in range(count - 1)]
        backward = [(target, source) for source, target in forward]
        low = lax.ppermute(
            lax.slice_in_dim(block, block.shape[dim] - width, None, axis=dim), axis, forward
        )
        high = lax.ppermute(lax.slice_in_dim(block, 0, width, axis=dim), axis, backward)
        block = jnp.concatenate([low, block, high], axis=dim)
    return block


def share_codes(codes):
    return lax.all_gather(codes.astype(jnp.bfloat16), "comp", axis=1, tiled=True).astype(
        codes.dtype
    )


def on_device(scans, maps, gram_old, stats_old, kept):
    highest = lax.Precision.HIGHEST
    volumes = scans.shape[0]
    own_count = maps.shape[0]
    planes, lines_all, width_x = (maps.shape[1], maps.shape[2], maps.shape[3])
    lines_own = stats_old.shape[2]
    voxel_total = planes * lax.axis_size("slab") * lines_all * width_x
    total_rows = volumes * lax.axis_size("subj")
    inv_root = 1.0 / math.sqrt(voxel_total)
    comp_index = lax.axis_index("comp")
    flat_scans = scans.reshape(volumes, -1)
    flat_own = maps.reshape(own_count, -1)
    full_maps = lax.all_gather(maps, "comp", axis=0, tiled=True)
    flat_full = full_maps.reshape(COMPONENTS, -1)
    proj_part = jnp.dot(flat_scans, flat_own.T, preferred_element_type=jnp.float32) * inv_root
    gram_part = jnp.dot(flat_full, flat_own.T, preferred_element_type=jnp.float32) * (
        1.0 / voxel_total
    )
    proj, gram_cols = lax.psum((proj_part, gram_part), "slab")
    codes = 0.1 * proj
    for step in range(ITERS - 1):
        whole = share_codes(codes)
        codes = codes + 0.1 * (proj - jnp.dot(whole, gram_cols, precision=highest) - 0.2 * codes)
    whole = share_codes(codes)
    live = (lax.iota(jnp.int32, volumes) < kept[0]).astype(jnp.float32)
    weighted = codes * live[:, None]
    gram_term = 0.5 / total_rows * jnp.dot(weighted.T, whole, precision=highest)
    gram_new = 0.5 * gram_old + lax.psum(gram_term.astype(jnp.bfloat16), "subj").astype(jnp.float32)
    weighted_low = weighted.astype(jnp.bfloat16)
    stats_scale = 0.5 / math.sqrt(total_rows)
    term = jnp.einsum("rzyx,rk->ykzx", scans, weighted_low, preferred_element_type=jnp.float32)
    summed = lax.psum_scatter(
        (term * stats_scale).astype(jnp.bfloat16), "subj", scatter_dimension=0, tiled=True
    ).astype(jnp.float32)
    stats_new = 0.5 * stats_old + jnp.transpose(summed, (1, 2, 0, 3))
    line_start = lax.axis_index("subj") * lines_own
    full_piece = lax.dynamic_slice_in_dim(full_maps, line_start, lines_own, 2).astype(jnp.float32)
    own_piece = lax.dynamic_slice_in_dim(maps, line_start, lines_own, 2).astype(jnp.float32)
    diag_block = lax.dynamic_slice_in_dim(gram_new, comp_index * own_count, own_count, 1)
    diag = jnp.diagonal(diag_block)
    coupled = jnp.dot(gram_new, full_piece.reshape(COMPONENTS, -1), precision=highest).reshape(
        own_piece.shape
    )
    updated = own_piece + (stats_new - coupled) / diag[:, None, None, None]
    padded = padded_2(updated, (("slab", 1), ("subj", 2)), 1)
    lap_z = padded[:, 2:, 1:-1, :] + padded[:, :-2, 1:-1, :] - 2.0 * updated
    lap_y = padded[:, 1:-1, 2:, :] + padded[:, 1:-1, :-2, :] - 2.0 * updated
    side_x = jnp.pad(updated, ((0, 0), (0, 0), (0, 0), (1, 1)))
    lap_x = side_x[:, :, :, 2:] + side_x[:, :, :, :-2] - 2.0 * updated
    maps_new = (updated + 0.24 * lap_z + 0.18 * lap_y + 0.12 * lap_x).astype(jnp.bfloat16)
    return (maps_new, stats_new, gram_new, codes)


def solution(mesh):
    in_specs = (
        P("subj", "slab", None, None),
        P("comp", "slab", None, None),
        P("comp", None),
        P("comp", "slab", "subj", None),
        P("subj"),
    )
    out_specs = (
        P("comp", "slab", "subj", None),
        P("comp", "slab", "subj", None),
        P("comp", None),
        P("subj", "comp"),
    )
    return jax.shard_map(
        on_device, mesh=mesh, in_specs=in_specs, out_specs=out_specs, check_vma=False
    )
```

profile of v0, /device:TPU:1, one launch (start us, length us, event | category | flops | bytes accessed | tf_op | source)
XLA Modules:
  0.0 687.0 jit_solution(10921568269107471022)
XLA Ops:
  7.2 2.6 copy.18
  9.9 4.5 fusion.47
  14.4 69.5 %all-gather.2.cloned.1.call-done = bf16[256,1,32,128]{3,0,2,1:T(8,128)(2,1)} async-done(((bf16[128,1,32,128]{3,0,2,1:T(8,128)(2,1)}), bf16[256,1,32,128]{3,0,2,1:T(8,128)(2,1)}) %all-gather.2.cloned.1.call-update) | async-done | bytes 2097168 | tf_op jit(solution)/shard_map/all_gather | solution.py:43
  83.9 3.0 fusion.53
  87.6 71.2 %all-reduce.7.cloned.1.call-done = (f32[448,128]{1,0:T(8,128)}, f32[256,128]{1,0:T(8,128)}) async-done(((f32[448,128]{1,0:T(8,128)}, f32[256,128]{1,0:T(8,128)}), (f32[448,128]{1,0:T(8,128)}, f32[256,128]{1,0:T(8,128)})) %all-reduce.7.cloned.1.call-update) | async-done | bytes 360464 | tf_op jit(solution)/shard_map/psum | solution.py:49
  159.8 8.3 %all_gather.39 = bf16[448,256]{1,0:T(8,128)(2,1)S(1)} all-gather(bf16[448,128]{1,0:T(8,128)(2,1)S(1)} %multiply_convert_fusion.2), channel_id=1, replica_groups=mesh['slab'=8,'subj'=32,'comp'=2] {'comp'}, dimensions={1}, use_global_device_ids=true | all-gather | bytes 344064 | tf_op jit(solution)/shard_map/all_gather | solution.py:26
  168.2 1.4 fusion.79
  169.5 8.3 %all_gather.41 = bf16[448,256]{1,0:T(8,128)(2,1)S(1)} all-gather(bf16[448,128]{1,0:T(8,128)(2,1)S(1)} %get-tuple-element.14), channel_id=1, replica_groups=mesh['slab'=8,'subj'=32,'comp'=2] {'comp'}, dimensions={1}, use_global_device_ids=true | all-gather | bytes 344064 | tf_op jit(solution)/shard_map/all_gather | solution.py:26
  177.8 1.4 fusion.80
  179.2 8.2 %all_gather.42 = bf16[448,256]{1,0:T(8,128)(2,1)S(1)} all-gather(bf16[448,128]{1,0:T(8,128)(2,1)S(1)} %get-tuple-element.16), channel_id=1, replica_groups=mesh['slab'=8,'subj'=32,'comp'=2] {'comp'}, dimensions={1}, use_global_device_ids=true | all-gather | bytes 344064 | tf_op jit(solution)/shard_map/all_gather | solution.py:26
  187.4 1.4 fusion.81
  188.8 8.2 %all_gather.43 = bf16[448,256]{1,0:T(8,128)(2,1)S(1)} all-gather(bf16[448,128]{1,0:T(8,128)(2,1)S(1)} %get-tuple-element.18), channel_id=1, replica_groups=mesh['slab'=8,'subj'=32,'comp'=2] {'comp'}, dimensions={1}, use_global_device_ids=true | all-gather | bytes 344064 | tf_op jit(solution)/shard_map/all_gather | solution.py:26
  197.4 9.8 %all_gather.44 = bf16[448,256]{1,0:T(8,128)(2,1)S(1)} all-gather(bf16[448,128]{1,0:T(8,128)(2,1)S(1)} %get-tuple-element.20), channel_id=1, replica_groups=mesh['slab'=8,'subj'=32,'comp'=2] {'comp'}, dimensions={1}, use_global_device_ids=true | all-gather | bytes 344064 | tf_op jit(solution)/shard_map/all_gather | solution.py:26
  207.6 8.9 %all_gather.45 = bf16[448,256]{1,0:T(8,128)(2,1)S(1)} all-gather(bf16[448,128]{1,0:T(8,128)(2,1)S(1)} %get-tuple-element.22), channel_id=1, replica_groups=mesh['slab'=8,'subj'=32,'comp'=2] {'comp'}, dimensions={1}, use_global_device_ids=true | all-gather | bytes 344064 | tf_op jit(solution)/shard_map/all_gather | solution.py:26
  216.8 8.5 %all_gather.46 = bf16[448,256]{1,0:T(8,128)(2,1)S(1)} all-gather(bf16[448,128]{1,0:T(8,128)(2,1)S(1)} %get-tuple-element.24), channel_id=1, replica_groups=mesh['slab'=8,'subj'=32,'comp'=2] {'comp'}, dimensions={1}, use_global_device_ids=true | all-gather | bytes 344064 | tf_op jit(solution)/shard_map/all_gather | solution.py:26
  225.7 9.4 %all_gather.47 = bf16[448,256]{1,0:T(8,128)(2,1)S(1)} all-gather(bf16[448,128]{1,0:T(8,128)(2,1)S(1)} %get-tuple-element.26), channel_id=1, replica_groups=mesh['slab'=8,'subj'=32,'comp'=2] {'comp'}, dimensions={1}, use_global_device_ids=true | all-gather | bytes 344064 | tf_op jit(solution)/shard_map/all_gather | solution.py:26
  235.5 9.5 %all_gather.48 = bf16[448,256]{1,0:T(8,128)(2,1)S(1)} all-gather(bf16[448,128]{1,0:T(8,128)(2,1)S(1)} %get-tuple-element.28), channel_id=1, replica_groups=mesh['slab'=8,'subj'=32,'comp'=2] {'comp'}, dimensions={1}, use_global_device_ids=true | all-gather | bytes 344064 | tf_op jit(solution)/shard_map/all_gather | solution.py:26
  245.3 9.5 %all_gather.49 = bf16[448,256]{1,0:T(8,128)(2,1)S(1)} all-gather(bf16[448,128]{1,0:T(8,128)(2,1)S(1)} %get-tuple-element.30), channel_id=1, replica_groups=mesh['slab'=8,'subj'=32,'comp'=2] {'comp'}, dimensions={1}, use_global_device_ids=true | all-gather | bytes 344064 | tf_op jit(solution)/shard_map/all_gather | solution.py:26
  255.1 9.5 %all_gather.50 = bf16[448,256]{1,0:T(8,128)(2,1)S(1)} all-gather(bf16[448,128]{1,0:T(8,128)(2,1)S(1)} %get-tuple-element.32), channel_id=1, replica_groups=mesh['slab'=8,'subj'=32,'comp'=2] {'comp'}, dimensions={1}, use_global_device_ids=true | all-gather | bytes 344064 | tf_op jit(solution)/shard_map/all_gather | solution.py:26
  265.0 9.5 %all_gather.51 = bf16[448,256]{1,0:T(8,128)(2,1)S(1)} all-gather(bf16[448,128]{1,0:T(8,128)(2,1)S(1)} %get-tuple-element.34), channel_id=1, replica_groups=mesh['slab'=8,'subj'=32,'comp'=2] {'comp'}, dimensions={1}, use_global_device_ids=true | all-gather | bytes 344064 | tf_op jit(solution)/shard_map/all_gather | solution.py:26
  274.5 1.1 fusion.56
  275.7 4.5 fusion.8
  280.2 152.9 %all-reduce.5.cloned.1.call-done = bf16[128,256]{1,0:T(8,128)(2,1)} async-done(((bf16[128,256]{1,0:T(8,128)(2,1)}), bf16[128,256]{1,0:T(8,128)(2,1)}) %all-reduce.5.cloned.1.call-update) | async-done | bytes 65552 | tf_op jit(solution)/shard_map/psum | solution.py:58
  434.1 1.2 gather_fusion
  435.3 219.8 %reduce-scatter.2.cloned.1.call-done = bf16[1,128,1,128]{3,1,0,2:T(8,128)(2,1)} async-done(((bf16[32,128,1,128]{3,1,0,2:T(8,128)(2,1)}), bf16[1,128,1,128]{3,1,0,2:T(8,128)(2,1)}) %reduce-scatter.2.cloned.1.call-update) | async-done | bytes 32784 | tf_op jit(solution)/shard_map/reduce_scatter | solution.py:62
  657.0 7.7 %collective-permute-start = (f32[128,1,1,128]{3,0,2,1:T(8,128)S(1)}, f32[128,1,1,128]{3,0,2,1:T(8,128)S(1)}, u32[]{:S(2)}, u32[]{:S(2)}) collective-permute-start(f32[128,1,1,128]{3,0,2,1:T(8,128)S(1)} %fusion.59), channel_id=1, source_target_pairs={{64,0},{128,64},{192,128},{256,192},{320,256},{384,320},{448,384},... | collective-permute-start | bytes 196616 | tf_op jit(solution)/shard_map/ppermute | solution.py:20
  664.6 3.1 collective-permute-start.1
  667.8 1.3 collective-permute-done.1
  669.1 2.2 collective-permute-start.3
  671.3 1.3 collective-permute-start.2
  672.6 2.7 collective-permute-done.3
  675.3 4.4 collective-permute-done.2
  (42 shorter events, 7.7 us)
Async XLA Ops:
  7.2 76.7 %all-gather.2.cloned.1.call-start = ((), (), s32[]{:S(2)}) async-start(), calls=%async_computation.1 | async-start | bytes 3145728 | tf_op jit(solution)/shard_map/all_gather | solution.py:43
  9.9 148.9 %all-reduce.7.cloned.1.call-start = ((), (), s32[]{:S(2)}) async-start(), calls=%async_computation.4 | async-start | bytes 720896 | tf_op jit(solution)/shard_map/psum | solution.py:49
  9.9 74.0 %copy-start.3 = (bf16[128,1,32,128]{3,2,1,0:T(8,128)(2,1)S(1)}, bf16[128,1,32,128]{3,2,1,0:T(8,128)(2,1)}, u32[]{:S(2)}) copy-start(bf16[128,1,32,128]{3,2,1,0:T(8,128)(2,1)} %param.6) | copy-start | bytes 3145732
  86.9 346.3 %all-reduce.5.cloned.1.call-start = ((), (), s32[]{:S(2)}) async-start(), calls=%async_computation.3 | async-start | bytes 131072 | tf_op jit(solution)/shard_map/psum | solution.py:58
  158.8 38.2 %copy-start = (f32[448,128]{1,0:T(8,128)S(1)}, f32[448,128]{1,0:T(8,128)}, u32[]{:S(2)}) copy-start(f32[448,128]{1,0:T(8,128)} %get-tuple-element.12) | copy-start | bytes 688132
  158.8 38.2 %copy-start.1 = (f32[256,128]{1,0:T(8,128)S(1)}, f32[256,128]{1,0:T(8,128)}, u32[]{:S(2)}) copy-start(f32[256,128]{1,0:T(8,128)} %get-tuple-element.13) | copy-start | bytes 393220
  265.0 169.1 %copy-start.2 = (f32[448,128]{1,0:T(8,128)}, f32[448,128]{1,0:T(8,128)S(1)}, u32[]{:S(2)}) copy-start(f32[448,128]{1,0:T(8,128)S(1)} %get-tuple-element.35) | copy-start | bytes 688132
  265.0 168.2 %copy-start.6 = (f32[128,256]{1,0:T(8,128)S(1)}, f32[128,256]{1,0:T(8,128)}, u32[]{:S(2)}) copy-start(f32[128,256]{1,0:T(8,128)} %param.7) | copy-start | bytes 393220
  275.6 379.5 %copy-start.7 = (f32[128,1,1,128]{3,2,1,0:T(1,128)S(1)}, f32[128,1,1,128]{3,2,1,0:T(1,128)}, u32[]{:S(2)}) copy-start(f32[128,1,1,128]{3,2,1,0:T(1,128)} %param.8) | copy-start | bytes 196612
  275.6 379.5 %reduce-scatter.2.cloned.1.call-start = ((), (), s32[]{:S(2)}) async-start(), calls=%async_computation.2 | async-start | bytes 1081344 | tf_op jit(solution)/shard_map/reduce_scatter | solution.py:62
  434.1 246.4 %copy-start.4 = (f32[128,256]{1,0:T(8,128)}, f32[128,256]{1,0:T(8,128)S(1)}, u32[]{:S(2)}) copy-start(f32[128,256]{1,0:T(8,128)S(1)} %convert_add_fusion) | copy-start | bytes 393220
  655.9 24.6 %copy-start.5 = (f32[128,1,1,128]{3,0,2,1:T(8,128)}, f32[128,1,1,128]{3,0,2,1:T(8,128)S(1)}, u32[]{:S(2)}) copy-start(f32[128,1,1,128]{3,0,2,1:T(8,128)S(1)} %convert_add_fusion.1) | copy-start | bytes 196612
  657.0 10.8 %collective-permute-start = (f32[128,1,1,128]{3,0,2,1:T(8,128)S(1)}, f32[128,1,1,128]{3,0,2,1:T(8,128)S(1)}, u32[]{:S(2)}, u32[]{:S(2)}) collective-permute-start(f32[128,1,1,128]{3,0,2,1:T(8,128)S(1)} %fusion.59), channel_id=1, source_target_pairs={{64,0},{128,64},{192,128},{256,192},{320,256},{384,320},{448,384},... | collective-permute-start | bytes 196616 | tf_op jit(solution)/shard_map/ppermute | solution.py:20
  664.6 4.5 collective-permute-start.1
  669.1 6.2 collective-permute-start.3
  671.3 8.4 %collective-permute-start.2 = (f32[128,3,1,128]{3,0,2,1:T(8,128)S(1)}, f32[128,3,1,128]{3,0,2,1:T(8,128)S(1)}, u32[]{:S(2)}, u32[]{:S(2)}) collective-permute-start(f32[128,3,1,128]{3,0,2,1:T(8,128)S(1)} %pad_maximum_fusion), channel_id=1, source_target_pairs={{2,0},{4,2},{6,4},{8,6},{10,8},{12,10},{14,12},{16,14},{18,16},{20... | collective-permute-start | bytes 589832 | tf_op jit(solution)/shard_map/ppermute | solution.py:20
Sparse Core Ops, SparseCore 0:
  10.1 73.7 all-gather.1
  87.4 71.3 all-reduce.6
  275.7 157.4 all-reduce.4
  438.1 217.0 reduce-scatter.1
where the time goes:
time: 689 us; the launch traced here: 687 us
  waiting for transfers between devices  522 us (76%)
  blocking collectives  108 us (16%)
  matrix products  21.2 us (3%)
  between operations  14.6 us (2%)
  starting transfers between devices  14.5 us (2%)
    reduce_scatter x1, waiting for transfers between devices, on_device(): lax.psum_scatter((term * stats_scale).astype(jnp.bfloat16), 'subj', scatt...  220 us
    psum x1, waiting for transfers between devices, on_device(): lax.psum(gram_term.astype(jnp.bfloat16), 'subj').astype(jnp.float32)  153 us
    all_gather x12, blocking collectives, share_codes(): lax.all_gather(codes.astype(jnp.bfloat16), 'comp', axis=1, tiled=True)  108 us
    psum x1, waiting for transfers between devices, on_device(): proj, gram_cols = lax.psum((proj_part, gram_part), 'slab')  71.2 us
    all_gather x1, waiting for transfers between devices, on_device(): full_maps = lax.all_gather(maps, 'comp', axis=0, tiled=True)  69.5 us
  transfers between devices with their start and end apart: 8, of which 7 were waited for; matrix products, arithmetic and copies ran while one was open for 2% of the time, Pallas kernels for 0%

commit v1 on v0

v1 whole, which is shorter than its diff:
```python
import math

import jax
import jax.numpy as jnp
from jax import lax
from jax.sharding import PartitionSpec as P

COMPONENTS = 256
ITERS = 12
X_SIZE = 4
Y_SIZE = 8
LOW = jnp.bfloat16
WIDE = jnp.float32


def power_sum(gram):
    dot = lambda a, b: jnp.dot(a, b, precision=lax.Precision.HIGHEST)
    eye = jnp.eye(COMPONENTS, dtype=WIDE)
    first = 0.98 * eye - 0.1 * gram
    second = dot(first, first)
    third = dot(second, first)
    sum3 = eye + first + second
    sum6 = sum3 + dot(third, sum3)
    sixth = dot(third, third)
    return 0.1 * (sum6 + dot(sixth, sum6))


def on_device(scans, maps, gram_old, stats_old, kept):
    highest = lax.Precision.HIGHEST
    slabs = lax.axis_size("slab")
    subjects = lax.axis_size("subj")
    volumes = scans.shape[0]
    own_count, _, lines, width = maps.shape
    voxel_total = slabs * lines * width
    total_rows = volumes * subjects
    slab, subj, comp = lax.axis_index("slab"), lax.axis_index("subj"), lax.axis_index("comp")
    at_x = subj // Y_SIZE
    ring = slabs * X_SIZE * 2
    ring_groups = [
        [(s * subjects + x * Y_SIZE + y) * 2 + c for s in range(slabs) for x in range(X_SIZE) for c in range(2)]
        for y in range(Y_SIZE)
    ]
    x_groups = [[x * Y_SIZE + y for x in range(X_SIZE)] for y in range(Y_SIZE)]
    y_groups = [[x * Y_SIZE + y for y in range(Y_SIZE)] for x in range(X_SIZE)]
    whole_axes = ("slab", "subj", "comp")

    scans3 = scans.reshape(volumes, lines, width)
    maps3 = maps.reshape(own_count, lines, width)
    half = Y_SIZE // 2
    own_line = lax.dynamic_slice_in_dim(maps3, subj, 1, 1)
    to_partner = lax.dynamic_slice_in_dim(maps3, at_x * Y_SIZE + (1 - comp) * half, half, 1)
    got = lax.ppermute(jnp.concatenate([to_partner, own_line], axis=1), "comp", [(0, 1), (1, 0)])

    proj_part = jnp.einsum("ryx,kyx->rk", scans3, maps3, preferred_element_type=WIDE)
    proj_part = (proj_part * (1.0 / math.sqrt(voxel_total))).astype(LOW)

    quarter = lax.dynamic_slice_in_dim(maps3, at_x * Y_SIZE, Y_SIZE, 1)
    own_half = lax.dynamic_slice_in_dim(maps3, at_x * Y_SIZE + comp * half, half, 1)
    gram_own = jnp.einsum("ayx,byx->ab", quarter, quarter, preferred_element_type=WIDE)
    first = jnp.where(comp == 0, own_half, got[:, :half])
    second = jnp.where(comp == 0, got[:, :half], own_half)
    gram_cross = jnp.einsum("ayx,byx->ab", first, second, preferred_element_type=WIDE)
    gram_parts = jnp.concatenate(
        [gram_own.reshape(ring, -1, own_count), gram_cross.reshape(ring, -1, own_count)], axis=1
    )
    gram_parts = (gram_parts * (1.0 / voxel_total)).astype(LOW)

    pieces = volumes // 8
    proj_sent = jnp.pad(proj_part.reshape(pieces, 8, own_count), ((0, ring - pieces), (0, 0), (0, 0)))
    sent = jnp.concatenate([proj_sent, jnp.pad(gram_parts, ((0, 0), (0, 4), (0, 0)))], axis=1)
    taken = lax.all_to_all(sent, whole_axes, 0, 0, axis_index_groups=ring_groups)
    taken = taken.reshape(slabs, X_SIZE, 2, 16, own_count).astype(WIDE)
    slab_sum = taken.sum(0)
    proj_rows = slab_sum[:, :, :8].reshape(X_SIZE, 16, own_count)
    gram_rows = slab_sum[:, :, 8:12].sum(0)
    shared = jnp.concatenate([gram_rows[:, :2].reshape(4, own_count), gram_rows[:, 2:].sum(0)], axis=0)
    shared = jnp.pad(shared, ((0, 2), (0, 0)))
    back = jnp.concatenate([proj_rows, jnp.broadcast_to(shared, (X_SIZE, 8, own_count))], axis=1).astype(LOW)
    back = jnp.broadcast_to(back[None, :, None], (slabs, X_SIZE, 2, 24, own_count)).reshape(ring, 24, own_count)
    back = lax.all_to_all(back, whole_axes, 0, 0, axis_index_groups=ring_groups)
    proj = jnp.concatenate(
        [back[:pieces, :8].reshape(volumes, own_count), back[:pieces, 8:16].reshape(volumes, own_count)], axis=1
    )
    low_block = back[:, 16:18].reshape(own_count, own_count)
    high_block = back[:, 18:20].reshape(own_count, own_count)
    cross = back[:, 20:22].reshape(own_count, own_count)
    gram = jnp.concatenate(
        [jnp.concatenate([low_block, cross], axis=1), jnp.concatenate([cross.T, high_block], axis=1)], axis=0
    ).astype(WIDE)

    whole = jnp.dot(proj.astype(WIDE), power_sum(gram), precision=highest)
    codes = lax.dynamic_slice_in_dim(whole, comp * own_count, own_count, 1)
    live = (lax.iota(jnp.int32, volumes) < kept[0]).astype(WIDE)
    weighted_low = (codes * live[:, None]).astype(LOW)

    term = jnp.einsum("rk,ryx->ykx", weighted_low, scans3, preferred_element_type=WIDE)
    term = (term * (0.5 / math.sqrt(total_rows))).astype(LOW).reshape(X_SIZE, Y_SIZE * own_count, width)
    product = jnp.dot(weighted_low.T, whole.astype(LOW), preferred_element_type=WIDE) * (0.5 / total_rows)
    share = own_count // slabs
    mine = lax.dynamic_slice_in_dim(product, slab * share, share, 0).astype(LOW)
    mine = jnp.concatenate([mine[:, :own_count], mine[:, own_count:]], axis=0)
    sent = jnp.concatenate([term, jnp.broadcast_to(mine, (X_SIZE, 2 * share, width))], axis=1)
    taken = lax.all_to_all(sent, "subj", 0, 0, axis_index_groups=x_groups).astype(WIDE).sum(0).astype(LOW)
    sent = jnp.concatenate(
        [
            taken[: Y_SIZE * own_count].reshape(Y_SIZE, own_count, width),
            jnp.broadcast_to(taken[Y_SIZE * own_count :], (Y_SIZE, 2 * share, width)),
        ],
        axis=1,
    )
    summed = lax.all_to_all(sent, "subj", 0, 0, axis_index_groups=y_groups).astype(WIDE).sum(0)
    stats_line = 0.5 * stats_old.reshape(own_count, width) + summed[:own_count]
    mine = jnp.broadcast_to(summed[own_count:].astype(LOW), (slabs, 2 * share, width))
    product = lax.all_to_all(mine, "slab", 0, 0).astype(WIDE)
    product = jnp.concatenate(
        [product[:, :share].reshape(own_count, own_count), product[:, share:].reshape(own_count, own_count)], axis=1
    )
    gram_new = 0.5 * gram_old + product

    own_piece = own_line.reshape(own_count, width)
    other_piece = got[:, half]
    piece = jnp.where(
        comp == 0,
        jnp.concatenate([own_piece, other_piece], axis=0),
        jnp.concatenate([other_piece, own_piece], axis=0),
    ).astype(WIDE)
    block = lax.dynamic_slice_in_dim(gram_new, comp * own_count, own_count, 1)
    diag = jnp.sum(block * jnp.eye(own_count, dtype=WIDE), axis=1, keepdims=True)
    coupled = jnp.dot(gram_new, piece, precision=highest)
    updated = own_piece.astype(WIDE) + (stats_line - coupled) / diag
    edge = updated.astype(LOW)
    sides = []
    for axis in ("slab", "subj"):
        count = lax.axis_size(axis)
        up = [(i, i + 1) for i in range(count - 1)]
        sides.append(lax.ppermute(edge, axis, up) + 0.0)
        sides.append(lax.ppermute(edge, axis, [(b, a) for a, b in up]) + 0.0)
    z_low, z_high, y_low, y_high = [side.astype(WIDE) for side in sides]
    side_x = jnp.pad(updated, ((0, 0), (1, 1)))
    lap_x = side_x[:, 2:] + side_x[:, :-2] - 2.0 * updated
    lap_z = z_low + z_high - 2.0 * updated
    lap_y = y_low + y_high - 2.0 * updated
    maps_new = (updated + 0.24 * lap_z + 0.18 * lap_y + 0.12 * lap_x).astype(LOW)
    return (
        maps_new.reshape(own_count, 1, 1, width),
        stats_line.reshape(own_count, 1, 1, width),
        gram_new,
        codes,
    )


def solution(mesh):
    in_specs = (
        P("subj", "slab", None, None),
        P("comp", "slab", None, None),
        P("comp", None),
        P("comp", "slab", "subj", None),
        P("subj"),
    )
    out_specs = (
        P("comp", "slab", "subj", None),
        P("comp", "slab", "subj", None),
        P("comp", None),
        P("subj", "comp"),
    )
    return jax.shard_map(
        on_device, mesh=mesh, in_specs=in_specs, out_specs=out_specs, check_vma=False
    )
```

time: 689 us -> 136 us (0.20)
  waiting for transfers between devices: 522 us -> 29.6 us
  blocking collectives: 108 us -> 42.8 us
  starting transfers between devices: 14.5 us -> 43.2 us
  between operations: 14.6 us -> 1.82 us
  matrix products: 21.2 us -> 8.65 us
    psum x2 -> x0, waiting for transfers between devices: 224 us -> none  [the longest x1 153 us: on_device(): lax.psum(gram_term.astype(jnp.bfloat16), 'subj').astype(jnp.float32)]
    reduce_scatter x1 -> x0, waiting for transfers between devices: 220 us -> none  [on_device(): lax.psum_scatter((term * stats_scale).astype(jnp.bfloat16), 'subj', scatt...]
    all_gather x12 -> x0, blocking collectives: 108 us -> none  [share_codes(): lax.all_gather(codes.astype(jnp.bfloat16), 'comp', axis=1, tiled=True)]
    all_gather x1 -> x0, waiting for transfers between devices: 69.5 us -> none  [on_device(): full_maps = lax.all_gather(maps, 'comp', axis=0, tiled=True)]
    all_to_all x0 -> x2, blocking collectives: none -> 42.8 us  [the longest x1 26.1 us: on_device(): lax.all_to_all(sent, whole_axes, 0, 0, axis_index_groups=ring_groups)]
    all_to_all x0 -> x3, waiting for transfers between devices: none -> 29.4 us  [the longest x1 14.4 us: on_device(): back = lax.all_to_all(back, whole_axes, 0, 0, axis_index_groups=ring_groups)]
    all_to_all x0 -> x3, starting transfers between devices: none -> 20.8 us  [the longest x1 8.65 us: on_device(): product = lax.all_to_all(mine, 'slab', 0, 0).astype(WIDE)]
    dot_general x16 -> x12, matrix products: 21.2 us -> 8.65 us  [the longest x1 3.68 us: on_device(): jnp.einsum('ryx,kyx->rk', scans3, maps3, preferred_element_type=WIDE)]
  transfers between devices with their start and end apart: 8 -> 8, of which waited for: 7 -> 4; matrix products, arithmetic and copies ran while one was open for 2% -> 4% of each run, Pallas kernels for 0% -> 0%
where the time goes in v1:
time: 136 us; the launch traced here: 135 us
  starting transfers between devices  43.2 us (32%)
  blocking collectives  42.8 us (31%)
  waiting for transfers between devices  29.6 us (22%)
  matrix products  8.65 us (6%)
  local copies, waits for them, and re-layouts  7.69 us (6%)
  between operations  1.82 us (1%)
  other arithmetic  1.5 us (1%)
    all_to_all x1, blocking collectives, on_device(): lax.all_to_all(sent, whole_axes, 0, 0, axis_index_groups=ring_groups)  26.1 us
    all_to_all x1, blocking collectives, on_device(): lax.all_to_all(sent, 'subj', 0, 0, axis_index_groups=x_groups).astype(WIDE)  16.7 us
    all_to_all x1, waiting for transfers between devices, on_device(): back = lax.all_to_all(back, whole_axes, 0, 0, axis_index_groups=ring_groups)  14.4 us
    ppermute x1, starting transfers between devices, on_device(): lax.ppermute(jnp.concatenate([to_partner, own_line], axis=1), 'comp', [(0...  11.5 us
    all_to_all x1, waiting for transfers between devices, on_device(): lax.all_to_all(sent, 'subj', 0, 0, axis_index_groups=y_groups).astype(WIDE)  9.97 us
    all_to_all x1, starting transfers between devices, on_device(): product = lax.all_to_all(mine, 'slab', 0, 0).astype(WIDE)  8.65 us
    all_to_all x1, starting transfers between devices, on_device(): lax.all_to_all(sent, 'subj', 0, 0, axis_index_groups=y_groups).astype(WIDE)  6.81 us
    ppermute x2, starting transfers between devices, on_device(): sides.append(lax.ppermute(edge, axis, up) + 0.0)  6.25 us
  transfers between devices with their start and end apart: 8, of which 4 were waited for; matrix products, arithmetic and copies ran while one was open for 4% of the time, Pallas kernels for 0%

profile of v1, /device:TPU:1, one launch (start us, length us, event | category | flops | bytes accessed | tf_op | source)
XLA Modules:
  0.0 135.3 jit_solution(13991895289856931511)
XLA Ops:
  0.7 1.0 constant_dynamic-slice_fusion.4
  1.8 1.2 constant_dynamic-slice_fusion.1
  3.2 11.5 %collective-permute-start = (bf16[128,5,128]{0,2,1:T(8,128)(2,1)S(1)}, bf16[128,5,128]{0,2,1:T(8,128)(2,1)S(1)}, u32[]{:S(2)}, u32[]{:S(2)}) collective-permute-start(bf16[128,5,128]{0,2,1:T(8,128)(2,1)S(1)} %pad_maximum_fusion.2), channel_id=1, source_target_pairs={{0,1},{1,0},{2,3},{3,2},{4,5},{5,4},{6,7},{7,6},{8,9},{9,8},{10,11... | collective-permute-start | bytes 491528 | tf_op jit(solution)/shard_map/ppermute | solution.py:52
  14.7 3.7 %fusion.16 = bf16[56,8,128]{2,1,0:T(8,128)(2,1)S(1)} fusion(bf16[448,32,128]{2,1,0:T(8,128)(2,1)} %bitcast.81, bf16[128,32,128]{2,1,0:T(8,128)(2,1)} %bitcast.86), kind=kOutput, calls=%fused_computation.11 | convolution fusion | flops 469876736 | bytes 4833280 | tf_op jit(solution)/shard_map/ryx,kyx->rk/dot_general | solution.py:54
  18.3 1.0 constant_dynamic-slice_fusion.3
  20.3 26.1 %all_to_all.25 = bf16[64,16,128]{2,1,0:T(8,128)(2,1)S(1)} all-to-all(bf16[64,16,128]{2,1,0:T(8,128)(2,1)S(1)} %copy.143), channel_id=1, replica_groups={{0,1,16,17,32,33,48,49,64,65,80,81,96,97,112,113,128,129,144,145,160,16..., dimensions={0} | all-to-all | bytes 524288 | tf_op jit(solution)/shard_map/all_to_all | solution.py:71
  46.6 0.8 broadcast_in_dim.21
  47.4 5.4 %all-to-all-start.1 = ((bf16[64,24,128]{2,1,0:T(8,128)(2,1)}), bf16[64,24,128]{2,1,0:T(8,128)(2,1)S(1)}, u32[]{:S(2)}, u32[]{:S(2)}) async-start(bf16[64,24,128]{2,1,0:T(8,128)(2,1)} %bitcast.20), calls=%async_computation.1 | async-start | bytes 786432 | tf_op jit(solution)/shard_map/all_to_all | solution.py:80
  53.4 14.4 %all-to-all-done.1 = bf16[64,24,128]{2,1,0:T(8,128)(2,1)S(1)} async-done(((bf16[64,24,128]{2,1,0:T(8,128)(2,1)}), bf16[64,24,128]{2,1,0:T(8,128)(2,1)S(1)}, u32[]{:S(2)}, u32[]{:S(2)}) %all-to-all-start.1) | async-done | bytes 393248 | tf_op jit(solution)/shard_map/all_to_all | solution.py:80
  68.1 0.4 fusion.31
  68.5 0.4 fusion.30
  68.9 0.4 convolution_add_fusion.1
  69.4 0.4 fusion.84
  69.8 0.4 fusion.6
  70.2 0.4 fusion.32
  70.6 0.3 fusion.36
  70.9 0.5 copy-done
  71.4 1.5 %multiply_convert_fusion = bf16[128,32,128]{2,0,1:T(8,128)(2,1)S(1)} fusion(bf16[448,32,128]{2,1,0:T(8,128)(2,1)S(1)} %bitcast.82, f32[448,128]{1,0:T(8,128)S(1)} %constant_dynamic-slice_fusion, f32[448]{0:T(512)S(1)} %fusion.67), kind=kOutput, calls=%fused_computation.4 | convolution fusion | flops 470925312 | bytes 4949760 | tf_op jit(solution)/shard_map/rk,ryx->ykx/dot_general | solution.py:96
  73.1 16.7 %all_to_all.26 = bf16[4,1056,128]{2,1,0:T(8,128)(2,1)S(1)} all-to-all(bf16[4,1056,128]{2,1,0:T(8,128)(2,1)S(1)} %pad_maximum_fusion), channel_id=1, replica_groups={{0,16,32,48},{2,18,34,50},{4,20,36,52},{6,22,38,54},{8,24,40,56},{10,26..., dimensions={0} | all-to-all | bytes 2162688 | tf_op jit(solution)/shard_map/all_to_all | solution.py:103
  89.8 0.3 reduce_sum.60
  90.1 0.7 pad_maximum_fusion.1
  90.9 6.8 %all-to-all-start.3 = ((bf16[8,160,128]{2,1,0:T(8,128)(2,1)}), bf16[8,160,128]{2,1,0:T(8,128)(2,1)S(1)}, u32[]{:S(2)}, u32[]{:S(2)}) async-start(bf16[8,160,128]{2,1,0:T(8,128)(2,1)} %pad_maximum_fusion.1), calls=%async_computation.3 | async-start | bytes 655360 | tf_op jit(solution)/shard_map/all_to_all | solution.py:111
  97.8 10.0 %all-to-all-done.3 = bf16[8,160,128]{2,1,0:T(8,128)(2,1)S(1)} async-done(((bf16[8,160,128]{2,1,0:T(8,128)(2,1)}), bf16[8,160,128]{2,1,0:T(8,128)(2,1)S(1)}, u32[]{:S(2)}, u32[]{:S(2)}) %all-to-all-start.3) | async-done | bytes 327712 | tf_op jit(solution)/shard_map/all_to_all | solution.py:111
  107.8 0.6 broadcast_in_dim.24
  108.5 8.7 %all-to-all-start.4 = ((bf16[8,32,128]{2,1,0:T(8,128)(2,1)}), bf16[8,32,128]{2,1,0:T(8,128)(2,1)S(1)}, u32[]{:S(2)}, u32[]{:S(2)}) async-start(bf16[8,32,128]{2,1,0:T(8,128)(2,1)} %broadcast_in_dim.24), calls=%async_computation.4 | async-start | bytes 131072 | tf_op jit(solution)/shard_map/all_to_all | solution.py:114
  117.2 5.0 %all-to-all-done.4 = bf16[8,32,128]{2,1,0:T(8,128)(2,1)S(1)} async-done(((bf16[8,32,128]{2,1,0:T(8,128)(2,1)}), bf16[8,32,128]{2,1,0:T(8,128)(2,1)S(1)}, u32[]{:S(2)}, u32[]{:S(2)}) %all-to-all-start.4) | async-done | bytes 65568 | tf_op jit(solution)/shard_map/all_to_all | solution.py:114
  122.6 1.3 collective-permute-start.4
  123.9 4.0 %collective-permute-start.3 = (bf16[128,128]{0,1:T(8,128)(2,1)S(1)}, bf16[128,128]{0,1:T(8,128)(2,1)S(1)}, u32[]{:S(2)}, u32[]{:S(2)}) collective-permute-start(bf16[128,128]{0,1:T(8,128)(2,1)S(1)} %get-tuple-element.43), channel_id=1, source_target_pairs={{0,2},{2,4},{4,6},{6,8},{8,10},{10,12},{12,14},{14,16},{16,18},{18... | collective-permute-start | bytes 98312 | tf_op jit(solution)/shard_map/ppermute | solution.py:136
  127.9 3.3 %collective-permute-start.2 = (bf16[128,128]{0,1:T(8,128)(2,1)S(1)}, bf16[128,128]{0,1:T(8,128)(2,1)S(1)}, u32[]{:S(2)}, u32[]{:S(2)}) collective-permute-start(bf16[128,128]{0,1:T(8,128)(2,1)S(1)} %get-tuple-element.43), channel_id=1, source_target_pairs={{64,0},{128,64},{192,128},{256,192},{320,256},{384,320},{448,384},... | collective-permute-start | bytes 98312 | tf_op jit(solution)/shard_map/ppermute | solution.py:137
  131.2 2.3 %collective-permute-start.1 = (bf16[128,128]{0,1:T(8,128)(2,1)S(1)}, bf16[128,128]{0,1:T(8,128)(2,1)S(1)}, u32[]{:S(2)}, u32[]{:S(2)}) collective-permute-start(bf16[128,128]{0,1:T(8,128)(2,1)S(1)} %get-tuple-element.43), channel_id=1, source_target_pairs={{0,64},{64,128},{128,192},{192,256},{256,320},{320,384},{384,448},... | collective-permute-start | bytes 98312 | tf_op jit(solution)/shard_map/ppermute | solution.py:136
  133.5 0.7 copy.151
  134.6 0.7 copy.150
  (63 shorter events, 2.6 us)
Async XLA Ops:
  3.2 16.6 %collective-permute-start = (bf16[128,5,128]{0,2,1:T(8,128)(2,1)S(1)}, bf16[128,5,128]{0,2,1:T(8,128)(2,1)S(1)}, u32[]{:S(2)}, u32[]{:S(2)}) collective-permute-start(bf16[128,5,128]{0,2,1:T(8,128)(2,1)S(1)} %pad_maximum_fusion.2), channel_id=1, source_target_pairs={{0,1},{1,0},{2,3},{3,2},{4,5},{5,4},{6,7},{7,6},{8,9},{9,8},{10,11... | collective-permute-start | bytes 491528 | tf_op jit(solution)/shard_map/ppermute | solution.py:52
  47.4 20.5 %all-to-all-start.1 = ((bf16[64,24,128]{2,1,0:T(8,128)(2,1)}), bf16[64,24,128]{2,1,0:T(8,128)(2,1)S(1)}, u32[]{:S(2)}, u32[]{:S(2)}) async-start(bf16[64,24,128]{2,1,0:T(8,128)(2,1)} %bitcast.20), calls=%async_computation.1 | async-start | bytes 786432 | tf_op jit(solution)/shard_map/all_to_all | solution.py:80
  69.3 2.0 %copy-start = (bf16[448,1,32,128]{3,2,1,0:T(8,128)(2,1)S(1)}, bf16[448,1,32,128]{3,2,1,0:T(8,128)(2,1)}, u32[]{:S(2)}) copy-start(bf16[448,1,32,128]{3,2,1,0:T(8,128)(2,1)} %param.5) | copy-start | bytes 11010052
  70.6 2.4 %copy-start.1 = (f32[448,128]{1,0:T(8,128)}, f32[448,128]{1,0:T(8,128)S(1)}, u32[]{:S(2)}) copy-start(f32[448,128]{1,0:T(8,128)S(1)} %constant_dynamic-slice_fusion) | copy-start | bytes 688132
  89.8 7.9 %copy-start.4 = (f32[128,1,1,128]{3,2,1,0:T(1,128)S(1)}, f32[128,1,1,128]{3,2,1,0:T(1,128)}, u32[]{:S(2)}) copy-start(f32[128,1,1,128]{3,2,1,0:T(1,128)} %param.8) | copy-start | bytes 196612
  89.8 32.4 %copy-start.3 = (f32[128,256]{1,0:T(8,128)S(1)}, f32[128,256]{1,0:T(8,128)}, u32[]{:S(2)}) copy-start(f32[128,256]{1,0:T(8,128)} %param.7) | copy-start | bytes 393220
  90.9 16.9 %all-to-all-start.3 = ((bf16[8,160,128]{2,1,0:T(8,128)(2,1)}), bf16[8,160,128]{2,1,0:T(8,128)(2,1)S(1)}, u32[]{:S(2)}, u32[]{:S(2)}) async-start(bf16[8,160,128]{2,1,0:T(8,128)(2,1)} %pad_maximum_fusion.1), calls=%async_computation.3 | async-start | bytes 655360 | tf_op jit(solution)/shard_map/all_to_all | solution.py:111
  108.5 13.7 %all-to-all-start.4 = ((bf16[8,32,128]{2,1,0:T(8,128)(2,1)}), bf16[8,32,128]{2,1,0:T(8,128)(2,1)S(1)}, u32[]{:S(2)}, u32[]{:S(2)}) async-start(bf16[8,32,128]{2,1,0:T(8,128)(2,1)} %broadcast_in_dim.24), calls=%async_computation.4 | async-start | bytes 131072 | tf_op jit(solution)/shard_map/all_to_all | solution.py:114
  122.2 13.0 %copy-start.2 = (f32[128,256]{1,0:T(8,128)}, f32[128,256]{1,0:T(8,128)S(1)}, u32[]{:S(2)}) copy-start(f32[128,256]{1,0:T(8,128)S(1)} %maximum_add_fusion) | copy-start | bytes 393220
  122.6 11.6 %collective-permute-start.4 = (bf16[128,128]{0,1:T(8,128)(2,1)S(1)}, bf16[128,128]{0,1:T(8,128)(2,1)S(1)}, u32[]{:S(2)}, u32[]{:S(2)}) collective-permute-start(bf16[128,128]{0,1:T(8,128)(2,1)S(1)} %get-tuple-element.43), channel_id=1, source_target_pairs={{2,0},{4,2},{6,4},{8,6},{10,8},{12,10},{14,12},{16,14},{18,16},{20... | collective-permute-start | bytes 98312 | tf_op jit(solution)/shard_map/ppermute | solution.py:137
  123.9 10.3 %collective-permute-start.3 = (bf16[128,128]{0,1:T(8,128)(2,1)S(1)}, bf16[128,128]{0,1:T(8,128)(2,1)S(1)}, u32[]{:S(2)}, u32[]{:S(2)}) collective-permute-start(bf16[128,128]{0,1:T(8,128)(2,1)S(1)} %get-tuple-element.43), channel_id=1, source_target_pairs={{0,2},{2,4},{4,6},{6,8},{8,10},{10,12},{12,14},{14,16},{16,18},{18... | collective-permute-start | bytes 98312 | tf_op jit(solution)/shard_map/ppermute | solution.py:136
  127.9 6.4 %collective-permute-start.2 = (bf16[128,128]{0,1:T(8,128)(2,1)S(1)}, bf16[128,128]{0,1:T(8,128)(2,1)S(1)}, u32[]{:S(2)}, u32[]{:S(2)}) collective-permute-start(bf16[128,128]{0,1:T(8,128)(2,1)S(1)} %get-tuple-element.43), channel_id=1, source_target_pairs={{64,0},{128,64},{192,128},{256,192},{320,256},{384,320},{448,384},... | collective-permute-start | bytes 98312 | tf_op jit(solution)/shard_map/ppermute | solution.py:137
  131.2 3.3 %collective-permute-start.1 = (bf16[128,128]{0,1:T(8,128)(2,1)S(1)}, bf16[128,128]{0,1:T(8,128)(2,1)S(1)}, u32[]{:S(2)}, u32[]{:S(2)}) collective-permute-start(bf16[128,128]{0,1:T(8,128)(2,1)S(1)} %get-tuple-element.43), channel_id=1, source_target_pairs={{0,64},{64,128},{128,192},{192,256},{256,320},{320,384},{384,448},... | collective-permute-start | bytes 98312 | tf_op jit(solution)/shard_map/ppermute | solution.py:136

commit v2 on v1

--- a/solution.py
+++ b/solution.py
@@ -78,6 +78,7 @@
     back = jnp.concatenate([proj_rows, jnp.broadcast_to(shared, (X_SIZE, 8, own_count))], axis=1).astype(LOW)
     back = jnp.broadcast_to(back[None, :, None], (slabs, X_SIZE, 2, 24, own_count)).reshape(ring, 24, own_count)
     back = lax.all_to_all(back, whole_axes, 0, 0, axis_index_groups=ring_groups)
+    back, kept, scans3 = lax.optimization_barrier((back, kept, scans3))
     proj = jnp.concatenate(
         [back[:pieces, :8].reshape(volumes, own_count), back[:pieces, 8:16].reshape(volumes, own_count)], axis=1
     )
@@ -108,14 +109,18 @@
         ],
         axis=1,
     )
-    summed = lax.all_to_all(sent, "subj", 0, 0, axis_index_groups=y_groups).astype(WIDE).sum(0)
-    stats_line = 0.5 * stats_old.reshape(own_count, width) + summed[:own_count]
+    summed = lax.all_to_all(sent, "subj", 0, 0, axis_index_groups=y_groups)
+    summed, stats_old, gram_old = lax.optimization_barrier((summed, stats_old, gram_old))
+    summed = summed.astype(WIDE).sum(0)
     mine = jnp.broadcast_to(summed[own_count:].astype(LOW), (slabs, 2 * share, width))
-    product = lax.all_to_all(mine, "slab", 0, 0).astype(WIDE)
+    product = lax.all_to_all(mine, "slab", 0, 0)
+    product, summed, stats_old, got, own_line = lax.optimization_barrier((product, summed, stats_old, got, own_line))
+    product = product.astype(WIDE)
     product = jnp.concatenate(
         [product[:, :share].reshape(own_count, own_count), product[:, share:].reshape(own_count, own_count)], axis=1
     )
     gram_new = 0.5 * gram_old + product
+    stats_line = 0.5 * stats_old.reshape(own_count, width) + summed[:own_count]
 
     own_piece = own_line.reshape(own_count, width)
     other_piece = got[:, half]

time: 136 us -> 134 us (0.985)
  blocking collectives: 42.8 us -> 73 us
  starting transfers between devices: 43.2 us -> 27.7 us
  waiting for transfers between devices: 29.6 us -> 14.7 us
    all_to_all x0 -> x2, blocking collectives: none -> 30.2 us  [the longest x1 16.5 us: on_device(): summed = lax.all_to_all(sent, 'subj', 0, 0, axis_index_groups=y_groups)]
    all_to_all x2 -> x0, starting transfers between devices: 15.5 us -> none  [the longest x1 8.65 us: on_device(): product = lax.all_to_all(mine, 'slab', 0, 0).astype(WIDE)]
    all_to_all x2 -> x0, waiting for transfers between devices: 14.9 us -> none  [the longest x1 9.97 us: on_device(): lax.all_to_all(sent, 'subj', 0, 0, axis_index_groups=y_groups).astype(WIDE)]
  transfers between devices with their start and end apart: 8 -> 6, of which waited for: 4 -> 2; matrix products, arithmetic and copies ran while one was open for 4% -> 4% of each run, Pallas kernels for 0% -> 0%
where the time goes in v2:
time: 134 us
  blocking collectives  73 us (54%)
  starting transfers between devices  27.7 us (21%)
  waiting for transfers between devices  14.7 us (11%)
  matrix products  8.64 us (6%)
  local copies, waits for them, and re-layouts  7.05 us (5%)
  between operations  1.83 us (1%)
    all_to_all x1, blocking collectives, on_device(): lax.all_to_all(sent, whole_axes, 0, 0, axis_index_groups=ring_groups)  26.1 us
    all_to_all x1, blocking collectives, on_device(): lax.all_to_all(sent, 'subj', 0, 0, axis_index_groups=x_groups).astype(WIDE)  16.7 us
    all_to_all x1, blocking collectives, on_device(): summed = lax.all_to_all(sent, 'subj', 0, 0, axis_index_groups=y_groups)  16.5 us
    all_to_all x1, waiting for transfers between devices, on_device(): back = lax.all_to_all(back, whole_axes, 0, 0, axis_index_groups=ring_groups)  14.4 us
    all_to_all x1, blocking collectives, on_device(): product = lax.all_to_all(mine, 'slab', 0, 0)  13.7 us
    ppermute x1, starting transfers between devices, on_device(): lax.ppermute(jnp.concatenate([to_partner, own_line], axis=1), 'comp', [(0...  11.5 us
    ppermute x2, starting transfers between devices, on_device(): sides.append(lax.ppermute(edge, axis, up) + 0.0)  6.25 us
    all_to_all x1, starting transfers between devices, on_device(): back = lax.all_to_all(back, whole_axes, 0, 0, axis_index_groups=ring_groups)  5.38 us
  transfers between devices with their start and end apart: 6, of which 2 were waited for; matrix products, arithmetic and copies ran while one was open for 4% of the time, Pallas kernels for 0%

profile of v2, /device:TPU:1, one launch (start us, length us, event | category | flops | bytes accessed | tf_op | source)
XLA Modules:
  0.0 133.7 jit_solution(6252280194864400254)
XLA Ops:
  0.7 1.0 constant_dynamic-slice_fusion.1
  1.8 1.2 constant_dynamic-slice_fusion.2
  3.2 11.5 %collective-permute-start = (bf16[128,5,128]{0,2,1:T(8,128)(2,1)S(1)}, bf16[128,5,128]{0,2,1:T(8,128)(2,1)S(1)}, u32[]{:S(2)}, u32[]{:S(2)}) collective-permute-start(bf16[128,5,128]{0,2,1:T(8,128)(2,1)S(1)} %pad_maximum_fusion.2), channel_id=1, source_target_pairs={{0,1},{1,0},{2,3},{3,2},{4,5},{5,4},{6,7},{7,6},{8,9},{9,8},{10,11... | collective-permute-start | bytes 491528 | tf_op jit(solution)/shard_map/ppermute | solution.py:52
  14.7 3.7 %fusion.16 = bf16[56,8,128]{2,1,0:T(8,128)(2,1)S(1)} fusion(bf16[448,32,128]{2,1,0:T(8,128)(2,1)} %bitcast.106, bf16[128,32,128]{2,1,0:T(8,128)(2,1)} %bitcast.84), kind=kOutput, calls=%fused_computation.11 | convolution fusion | flops 469876736 | bytes 4833280 | tf_op jit(solution)/shard_map/ryx,kyx->rk/dot_general | solution.py:54
  18.3 1.0 constant_dynamic-slice_fusion.4
  19.5 0.2 convolution_bitcast_fusion
  19.8 0.2 fusion.38
  20.3 26.1 %all_to_all.25 = bf16[64,16,128]{2,1,0:T(8,128)(2,1)S(1)} all-to-all(bf16[64,16,128]{2,1,0:T(8,128)(2,1)S(1)} %copy.135), channel_id=1, replica_groups={{0,1,16,17,32,33,48,49,64,65,80,81,96,97,112,113,128,129,144,145,160,16..., dimensions={0} | all-to-all | bytes 524288 | tf_op jit(solution)/shard_map/all_to_all | solution.py:71
  46.6 0.8 broadcast_in_dim.21
  47.4 5.4 %all-to-all-start.1 = ((bf16[64,24,128]{2,1,0:T(8,128)(2,1)}), bf16[64,24,128]{2,1,0:T(8,128)(2,1)S(1)}, u32[]{:S(2)}, u32[]{:S(2)}) async-start(bf16[64,24,128]{2,1,0:T(8,128)(2,1)} %bitcast.18), calls=%async_computation.1 | async-start | bytes 786432 | tf_op jit(solution)/shard_map/all_to_all | solution.py:80
  53.4 14.4 %all-to-all-done.1 = bf16[64,24,128]{2,1,0:T(8,128)(2,1)S(1)} async-done(((bf16[64,24,128]{2,1,0:T(8,128)(2,1)}), bf16[64,24,128]{2,1,0:T(8,128)(2,1)S(1)}, u32[]{:S(2)}, u32[]{:S(2)}) %all-to-all-start.1) | async-done | bytes 393248 | tf_op jit(solution)/shard_map/all_to_all | solution.py:80
  68.1 0.4 fusion.30
  68.5 0.4 fusion.29
  68.9 0.4 convolution_add_fusion.1
  69.4 0.4 fusion.83
  69.8 0.4 fusion.6
  70.1 0.4 fusion.31
  70.6 0.3 fusion.35
  71.0 0.5 copy-done.4
  71.4 1.5 %multiply_convert_fusion = bf16[32,128,128]{1,2,0:T(8,128)(2,1)S(1)} fusion(bf16[448,32,128]{2,1,0:T(8,128)(2,1)S(1)} %bitcast.107, f32[448,128]{1,0:T(8,128)S(1)} %constant_dynamic-slice_fusion, f32[448]{0:T(512)S(1)} %fusion.66), kind=kOutput, calls=%fused_computation.4 | convolution fusion | flops 470925312 | bytes 4949760 | tf_op jit(solution)/shard_map/rk,ryx->ykx/dot_general | solution.py:97
  73.1 16.7 %all_to_all.26 = bf16[4,1056,128]{2,1,0:T(8,128)(2,1)S(1)} all-to-all(bf16[4,1056,128]{2,1,0:T(8,128)(2,1)S(1)} %pad_maximum_fusion), channel_id=1, replica_groups={{0,16,32,48},{2,18,34,50},{4,20,36,52},{6,22,38,54},{8,24,40,56},{10,26..., dimensions={0} | all-to-all | bytes 2162688 | tf_op jit(solution)/shard_map/all_to_all | solution.py:104
  89.8 0.3 reduce_sum.60
  90.1 16.5 %all_to_all.27 = bf16[8,160,128]{2,1,0:T(8,128)(2,1)S(1)} all-to-all(bf16[8,160,128]{2,1,0:T(8,128)(2,1)S(1)} %pad_maximum_fusion.1), channel_id=1, replica_groups={{0,2,4,6,8,10,12,14},{16,18,20,22,24,26,28,30},{32,34,36,38,40,42,44,46..., dimensions={0} | all-to-all | bytes 655360 | tf_op jit(solution)/shard_map/all_to_all | solution.py:112
  106.7 13.7 %all_to_all.28 = bf16[8,32,128]{2,1,0:T(8,128)(2,1)S(1)} all-to-all(bf16[8,32,128]{2,1,0:T(8,128)(2,1)S(1)} %broadcast_in_dim.24), channel_id=1, replica_groups=mesh['slab'=8,'subj'=32,'comp'=2] {'slab'}, dimensions={0} | all-to-all | bytes 131072 | tf_op jit(solution)/shard_map/all_to_all | solution.py:116
  120.8 0.2 fusion.82
  121.0 1.3 collective-permute-start.4
  122.3 4.0 %collective-permute-start.3 = (bf16[128,128]{0,1:T(8,128)(2,1)S(1)}, bf16[128,128]{0,1:T(8,128)(2,1)S(1)}, u32[]{:S(2)}, u32[]{:S(2)}) collective-permute-start(bf16[128,128]{0,1:T(8,128)(2,1)S(1)} %get-tuple-element.65), channel_id=1, source_target_pairs={{0,2},{2,4},{4,6},{6,8},{8,10},{10,12},{12,14},{14,16},{16,18},{18... | collective-permute-start | bytes 98312 | tf_op jit(solution)/shard_map/ppermute | solution.py:141
  126.3 3.3 %collective-permute-start.2 = (bf16[128,128]{0,1:T(8,128)(2,1)S(1)}, bf16[128,128]{0,1:T(8,128)(2,1)S(1)}, u32[]{:S(2)}, u32[]{:S(2)}) collective-permute-start(bf16[128,128]{0,1:T(8,128)(2,1)S(1)} %get-tuple-element.65), channel_id=1, source_target_pairs={{64,0},{128,64},{192,128},{256,192},{320,256},{384,320},{448,384},... | collective-permute-start | bytes 98312 | tf_op jit(solution)/shard_map/ppermute | solution.py:142
  129.7 2.3 %collective-permute-start.1 = (bf16[128,128]{0,1:T(8,128)(2,1)S(1)}, bf16[128,128]{0,1:T(8,128)(2,1)S(1)}, u32[]{:S(2)}, u32[]{:S(2)}) collective-permute-start(bf16[128,128]{0,1:T(8,128)(2,1)S(1)} %get-tuple-element.65), channel_id=1, source_target_pairs={{0,64},{64,128},{128,192},{192,256},{256,320},{320,384},{384,448},... | collective-permute-start | bytes 98312 | tf_op jit(solution)/shard_map/ppermute | solution.py:141
  132.0 0.7 copy.144
  132.7 0.2 collective-permute-done.1
  133.0 0.7 copy.143
  (60 shorter events, 1.7 us)
Async XLA Ops:
  3.2 16.6 %collective-permute-start = (bf16[128,5,128]{0,2,1:T(8,128)(2,1)S(1)}, bf16[128,5,128]{0,2,1:T(8,128)(2,1)S(1)}, u32[]{:S(2)}, u32[]{:S(2)}) collective-permute-start(bf16[128,5,128]{0,2,1:T(8,128)(2,1)S(1)} %pad_maximum_fusion.2), channel_id=1, source_target_pairs={{0,1},{1,0},{2,3},{3,2},{4,5},{5,4},{6,7},{7,6},{8,9},{9,8},{10,11... | collective-permute-start | bytes 491528 | tf_op jit(solution)/shard_map/ppermute | solution.py:52
  47.4 20.5 %all-to-all-start.1 = ((bf16[64,24,128]{2,1,0:T(8,128)(2,1)}), bf16[64,24,128]{2,1,0:T(8,128)(2,1)S(1)}, u32[]{:S(2)}, u32[]{:S(2)}) async-start(bf16[64,24,128]{2,1,0:T(8,128)(2,1)} %bitcast.18), calls=%async_computation.1 | async-start | bytes 786432 | tf_op jit(solution)/shard_map/all_to_all | solution.py:80
  69.4 2.0 %copy-start.4 = (bf16[448,1,32,128]{3,2,1,0:T(8,128)(2,1)S(1)}, bf16[448,1,32,128]{3,2,1,0:T(8,128)(2,1)}, u32[]{:S(2)}) copy-start(bf16[448,1,32,128]{3,2,1,0:T(8,128)(2,1)} %param.5) | copy-start | bytes 11010052
  70.6 2.4 %copy-start = (f32[448,128]{1,0:T(8,128)}, f32[448,128]{1,0:T(8,128)S(1)}, u32[]{:S(2)}) copy-start(f32[448,128]{1,0:T(8,128)S(1)} %constant_dynamic-slice_fusion) | copy-start | bytes 688132
  89.8 30.6 %copy-start.3 = (f32[128,1,1,128]{3,2,1,0:T(1,128)S(1)}, f32[128,1,1,128]{3,2,1,0:T(1,128)}, u32[]{:S(2)}) copy-start(f32[128,1,1,128]{3,2,1,0:T(1,128)} %param.8) | copy-start | bytes 196612
  89.8 30.9 %copy-start.2 = (f32[128,256]{1,0:T(8,128)S(1)}, f32[128,256]{1,0:T(8,128)}, u32[]{:S(2)}) copy-start(f32[128,256]{1,0:T(8,128)} %param.7) | copy-start | bytes 393220
  120.7 13.0 %copy-start.1 = (f32[128,256]{1,0:T(8,128)}, f32[128,256]{1,0:T(8,128)S(1)}, u32[]{:S(2)}) copy-start(f32[128,256]{1,0:T(8,128)S(1)} %maximum_add_fusion) | copy-start | bytes 393220
  121.0 11.6 %collective-permute-start.4 = (bf16[128,128]{0,1:T(8,128)(2,1)S(1)}, bf16[128,128]{0,1:T(8,128)(2,1)S(1)}, u32[]{:S(2)}, u32[]{:S(2)}) collective-permute-start(bf16[128,128]{0,1:T(8,128)(2,1)S(1)} %get-tuple-element.65), channel_id=1, source_target_pairs={{2,0},{4,2},{6,4},{8,6},{10,8},{12,10},{14,12},{16,14},{18,16},{20... | collective-permute-start | bytes 98312 | tf_op jit(solution)/shard_map/ppermute | solution.py:142
  122.3 10.3 %collective-permute-start.3 = (bf16[128,128]{0,1:T(8,128)(2,1)S(1)}, bf16[128,128]{0,1:T(8,128)(2,1)S(1)}, u32[]{:S(2)}, u32[]{:S(2)}) collective-permute-start(bf16[128,128]{0,1:T(8,128)(2,1)S(1)} %get-tuple-element.65), channel_id=1, source_target_pairs={{0,2},{2,4},{4,6},{6,8},{8,10},{10,12},{12,14},{14,16},{16,18},{18... | collective-permute-start | bytes 98312 | tf_op jit(solution)/shard_map/ppermute | solution.py:141
  126.3 6.4 %collective-permute-start.2 = (bf16[128,128]{0,1:T(8,128)(2,1)S(1)}, bf16[128,128]{0,1:T(8,128)(2,1)S(1)}, u32[]{:S(2)}, u32[]{:S(2)}) collective-permute-start(bf16[128,128]{0,1:T(8,128)(2,1)S(1)} %get-tuple-element.65), channel_id=1, source_target_pairs={{64,0},{128,64},{192,128},{256,192},{320,256},{384,320},{448,384},... | collective-permute-start | bytes 98312 | tf_op jit(solution)/shard_map/ppermute | solution.py:142
  129.7 3.3 %collective-permute-start.1 = (bf16[128,128]{0,1:T(8,128)(2,1)S(1)}, bf16[128,128]{0,1:T(8,128)(2,1)S(1)}, u32[]{:S(2)}, u32[]{:S(2)}) collective-permute-start(bf16[128,128]{0,1:T(8,128)(2,1)S(1)} %get-tuple-element.65), channel_id=1, source_target_pairs={{0,64},{64,128},{128,192},{192,256},{256,320},{320,384},{384,448},... | collective-permute-start | bytes 98312 | tf_op jit(solution)/shard_map/ppermute | solution.py:141

commit v3 on v2

v3 whole, which is shorter than its diff:
```python
import math

import jax
import jax.numpy as jnp
from jax import lax
from jax.sharding import PartitionSpec as P

COMPONENTS = 256
ITERS = 12
X_SIZE = 4
Y_SIZE = 8
LOW = jnp.bfloat16
WIDE = jnp.float32


def power_sum(gram):
    dot = lambda a, b: jnp.dot(a, b, precision=lax.Precision.HIGHEST)
    eye = jnp.eye(COMPONENTS, dtype=WIDE)
    first = 0.98 * eye - 0.1 * gram
    second = dot(first, first)
    third = dot(second, first)
    sum3 = eye + first + second
    sum6 = sum3 + dot(third, sum3)
    sixth = dot(third, third)
    return 0.1 * (sum6 + dot(sixth, sum6))


def on_device(scans, maps, gram_old, stats_old, kept):
    highest = lax.Precision.HIGHEST
    slabs = lax.axis_size("slab")
    subjects = lax.axis_size("subj")
    volumes = scans.shape[0]
    own_count, _, lines, width = maps.shape
    voxel_total = slabs * lines * width
    total_rows = volumes * subjects
    slab, subj, comp = lax.axis_index("slab"), lax.axis_index("subj"), lax.axis_index("comp")
    half_at = (subj // Y_SIZE) % 2
    ring = slabs * 4
    ring_groups = [
        [(s * subjects + (2 * pair + h) * Y_SIZE + y) * 2 + c for s in range(slabs) for h in range(2) for c in range(2)]
        for pair in range(X_SIZE // 2)
        for y in range(Y_SIZE)
    ]
    x_groups = [[x * Y_SIZE + y for x in range(X_SIZE)] for y in range(Y_SIZE)]
    y_groups = [[x * Y_SIZE + y for y in range(Y_SIZE)] for x in range(X_SIZE)]
    whole_axes = ("slab", "subj", "comp")

    scans3 = scans.reshape(volumes, lines, width)
    maps3 = maps.reshape(own_count, lines, width)
    part = lines // 4
    own_line = lax.dynamic_slice_in_dim(maps3, subj, 1, 1)
    to_partner = lax.dynamic_slice_in_dim(maps3, half_at * 2 * part + (1 - comp) * part, part, 1)
    got = lax.ppermute(jnp.concatenate([to_partner, own_line], axis=1), "comp", [(0, 1), (1, 0)])

    proj_part = jnp.einsum("ryx,kyx->rk", scans3, maps3, preferred_element_type=WIDE)
    proj_part = (proj_part * (1.0 / math.sqrt(voxel_total))).astype(LOW)

    own_lines = lax.dynamic_slice_in_dim(maps3, half_at * 2 * part, 2 * part, 1)
    own_half = lax.dynamic_slice_in_dim(maps3, half_at * 2 * part + comp * part, part, 1)
    gram_own = jnp.einsum("ayx,byx->ab", own_lines, own_lines, preferred_element_type=WIDE)
    first = jnp.where(comp == 0, own_half, got[:, :part])
    second = jnp.where(comp == 0, got[:, :part], own_half)
    gram_cross = jnp.einsum("ayx,byx->ab", first, second, preferred_element_type=WIDE)
    gram_parts = jnp.concatenate(
        [gram_own.reshape(ring, -1, own_count), gram_cross.reshape(ring, -1, own_count)], axis=1
    )
    gram_parts = (gram_parts * (1.0 / voxel_total)).astype(LOW)

    rows = 16
    pieces = volumes // rows
    few = own_count // ring
    proj_sent = jnp.pad(proj_part.reshape(pieces, rows, own_count), ((0, ring - pieces), (0, 0), (0, 0)))
    sent = jnp.concatenate([proj_sent, gram_parts], axis=1)
    taken = lax.all_to_all(sent, whole_axes, 0, 0, axis_index_groups=ring_groups)
    taken = taken.reshape(slabs, 2, 2, rows + 2 * few, own_count).astype(WIDE)
    slab_sum = taken.sum(0)
    proj_rows = slab_sum[:, :, :rows].reshape(2, 2 * rows, own_count)
    gram_rows = slab_sum[:, :, rows:].sum(0)
    shared = jnp.concatenate([gram_rows[:, :few].reshape(2 * few, own_count), gram_rows[:, few:].sum(0)], axis=0)
    shared = jnp.pad(shared, ((0, few), (0, 0)))
    back = jnp.concatenate([proj_rows, jnp.broadcast_to(shared, (2,) + shared.shape)], axis=1).astype(LOW)
    height = back.shape[1]
    back = jnp.broadcast_to(back[None, :, None], (slabs, 2, 2, height, own_count)).reshape(ring, height, own_count)
    back = lax.all_to_all(back, whole_axes, 0, 0, axis_index_groups=ring_groups)
    back, kept, scans3 = lax.optimization_barrier((back, kept, scans3))
    proj = jnp.concatenate(
        [back[:pieces, i * rows : (i + 1) * rows].reshape(volumes, own_count) for i in range(2)], axis=1
    )
    low_block, high_block, cross = [
        back[:, 2 * rows + i * few : 2 * rows + (i + 1) * few].reshape(own_count, own_count) for i in range(3)
    ]
    gram = jnp.concatenate(
        [jnp.concatenate([low_block, cross], axis=1), jnp.concatenate([cross.T, high_block], axis=1)], axis=0
    ).astype(WIDE)

    whole = jnp.dot(proj.astype(WIDE), power_sum(gram), precision=highest)
    codes = lax.dynamic_slice_in_dim(whole, comp * own_count, own_count, 1)
    live = (lax.iota(jnp.int32, volumes) < kept[0]).astype(WIDE)
    weighted_low = (codes * live[:, None]).astype(LOW)

    term = jnp.einsum("rk,ryx->ykx", weighted_low, scans3, preferred_element_type=WIDE)
    term = (term * (0.5 / math.sqrt(total_rows))).astype(LOW).reshape(X_SIZE, Y_SIZE * own_count, width)
    product = jnp.dot(weighted_low.T, whole.astype(LOW), preferred_element_type=WIDE) * (0.5 / total_rows)
    product = jnp.concatenate([product[:, :own_count], product[:, own_count:]], axis=0).astype(LOW)
    sent = jnp.concatenate([term, jnp.broadcast_to(product, (X_SIZE,) + product.shape)], axis=1)
    taken = lax.all_to_all(sent, "subj", 0, 0, axis_index_groups=x_groups).astype(WIDE).sum(0).astype(LOW)
    split = Y_SIZE * own_count
    sent = jnp.concatenate(
        [
            taken[:split].reshape(Y_SIZE, own_count, width),
            jnp.broadcast_to(taken[split:], (Y_SIZE, 2 * own_count, width)),
        ],
        axis=1,
    )
    summed = lax.all_to_all(sent, "subj", 0, 0, axis_index_groups=y_groups)
    summed, stats_old, gram_old, got, own_line = lax.optimization_barrier((summed, stats_old, gram_old, got, own_line))
    summed = summed.astype(WIDE).sum(0)
    product = jnp.concatenate([summed[own_count : 2 * own_count], summed[2 * own_count :]], axis=1)
    gram_new = 0.5 * gram_old + product
    stats_line = 0.5 * stats_old.reshape(own_count, width) + summed[:own_count]

    own_piece = own_line.reshape(own_count, width)
    other_piece = got[:, part]
    piece = jnp.where(
        comp == 0,
        jnp.concatenate([own_piece, other_piece], axis=0),
        jnp.concatenate([other_piece, own_piece], axis=0),
    ).astype(WIDE)
    block = lax.dynamic_slice_in_dim(gram_new, comp * own_count, own_count, 1)
    diag = jnp.sum(block * jnp.eye(own_count, dtype=WIDE), axis=1, keepdims=True)
    coupled = jnp.dot(gram_new, piece, precision=highest)
    updated = own_piece.astype(WIDE) + (stats_line - coupled) / diag
    edge = updated.astype(LOW)
    sides = []
    for axis in ("slab", "subj"):
        count = lax.axis_size(axis)
        up = [(i, i + 1) for i in range(count - 1)]
        sides.append(lax.ppermute(edge, axis, up) + 0.0)
        sides.append(lax.ppermute(edge, axis, [(b, a) for a, b in up]) + 0.0)
    z_low, z_high, y_low, y_high = [side.astype(WIDE) for side in sides]
    side_x = jnp.pad(updated, ((0, 0), (1, 1)))
    lap_x = side_x[:, 2:] + side_x[:, :-2] - 2.0 * updated
    lap_z = z_low + z_high - 2.0 * updated
    lap_y = y_low + y_high - 2.0 * updated
    maps_new = (updated + 0.24 * lap_z + 0.18 * lap_y + 0.12 * lap_x).astype(LOW)
    return (
        maps_new.reshape(own_count, 1, 1, width),
        stats_line.reshape(own_count, 1, 1, width),
        gram_new,
        codes,
    )


def solution(mesh):
    in_specs = (
        P("subj", "slab", None, None),
        P("comp", "slab", None, None),
        P("comp", None),
        P("comp", "slab", "subj", None),
        P("subj"),
    )
    out_specs = (
        P("comp", "slab", "subj", None),
        P("comp", "slab", "subj", None),
        P("comp", None),
        P("subj", "comp"),
    )
    return jax.shard_map(
        on_device, mesh=mesh, in_specs=in_specs, out_specs=out_specs, check_vma=False
    )
```

time: 134 us -> 137 us (1.022)
  blocking collectives: 73 us -> 76.9 us
    all_to_all x1 -> x0, blocking collectives: 13.7 us -> none  [on_device(): product = lax.all_to_all(mine, 'slab', 0, 0)]
    all_to_all x1, blocking collectives: 16.5 us -> 28.4 us  [on_device(): summed = lax.all_to_all(sent, 'subj', 0, 0, axis_index_groups=y_groups)]
    all_to_all x1, blocking collectives: 16.7 us -> 21.8 us  [on_device(): lax.all_to_all(sent, 'subj', 0, 0, axis_index_groups=x_groups).astype(WIDE)]
    all_to_all x1, starting transfers between devices: 5.38 us -> 3.78 us  [on_device(): back = lax.all_to_all(back, whole_axes, 0, 0, axis_index_groups=ring_groups)]
    ppermute x1, waiting for transfers between devices: 0.01 us -> 1.57 us  [on_device(): lax.ppermute(jnp.concatenate([to_partner, own_line], axis=1), 'comp', [(0...]
    ppermute x2, starting transfers between devices: 4.61 us -> 6.03 us  [on_device(): sides.append(lax.ppermute(edge, axis, [(b, a) for a, b in up]) + 0.0)]
  transfers between devices with their start and end apart: 6 -> 6, of which waited for: 2 -> 3; matrix products, arithmetic and copies ran while one was open for 4% -> 4% of each run, Pallas kernels for 0% -> 0%
where the time goes in v3:
time: 137 us
  blocking collectives  76.9 us (56%)
  starting transfers between devices  27.2 us (20%)
  waiting for transfers between devices  15.6 us (11%)
  matrix products  8.48 us (6%)
  local copies, waits for them, and re-layouts  5.8 us (4%)
  between operations  1.83 us (1%)
    all_to_all x1, blocking collectives, on_device(): summed = lax.all_to_all(sent, 'subj', 0, 0, axis_index_groups=y_groups)  28.4 us
    all_to_all x1, blocking collectives, on_device(): lax.all_to_all(sent, whole_axes, 0, 0, axis_index_groups=ring_groups)  26.7 us
    all_to_all x1, blocking collectives, on_device(): lax.all_to_all(sent, 'subj', 0, 0, axis_index_groups=x_groups).astype(WIDE)  21.8 us
    all_to_all x1, waiting for transfers between devices, on_device(): back = lax.all_to_all(back, whole_axes, 0, 0, axis_index_groups=ring_groups)  13.7 us
    ppermute x1, starting transfers between devices, on_device(): lax.ppermute(jnp.concatenate([to_partner, own_line], axis=1), 'comp', [(0...  11.5 us
    ppermute x2, starting transfers between devices, on_device(): sides.append(lax.ppermute(edge, axis, [(b, a) for a, b in up]) + 0.0)  6.03 us
    ppermute x2, starting transfers between devices, on_device(): sides.append(lax.ppermute(edge, axis, up) + 0.0)  5.91 us
    all_to_all x1, starting transfers between devices, on_device(): back = lax.all_to_all(back, whole_axes, 0, 0, axis_index_groups=ring_groups)  3.78 us
  transfers between devices with their start and end apart: 6, of which 3 were waited for; matrix products, arithmetic and copies ran while one was open for 4% of the time, Pallas kernels for 0%

profile of v3, /device:TPU:1, one launch (start us, length us, event | category | flops | bytes accessed | tf_op | source)
XLA Modules:
  0.0 136.8 jit_solution(12562960036024788106)
XLA Ops:
  0.7 1.1 constant_dynamic-slice_fusion.1
  1.9 1.1 constant_dynamic-slice_fusion.2
  3.0 0.2 copy.51
  3.3 11.5 %collective-permute-start = (bf16[128,9,128]{0,2,1:T(8,128)(2,1)S(1)}, bf16[128,9,128]{0,2,1:T(8,128)(2,1)S(1)}, u32[]{:S(2)}, u32[]{:S(2)}) collective-permute-start(bf16[128,9,128]{0,2,1:T(8,128)(2,1)S(1)} %pad_maximum_fusion.2), channel_id=1, source_target_pairs={{0,1},{1,0},{2,3},{3,2},{4,5},{5,4},{6,7},{7,6},{8,9},{9,8},{10,11... | collective-permute-start | bytes 884744 | tf_op jit(solution)/shard_map/ppermute | solution.py:53
  14.8 0.2 copy.50
  15.2 0.3 convolution_bitcast_fusion
  15.5 3.4 %fusion.13 = bf16[448,128]{1,0:T(8,128)(2,1)S(1)} fusion(bf16[448,32,128]{2,1,0:T(8,128)(2,1)} %bitcast.98, bf16[128,32,128]{2,1,0:T(8,128)(2,1)S(1)} %bitcast.71), kind=kOutput, calls=%fused_computation.12 | convolution fusion | flops 469876736 | bytes 4833280 | tf_op jit(solution)/shard_map/ryx,kyx->rk/dot_general | solution.py:55
  18.9 1.6 %collective-permute-done = bf16[128,9,128]{0,2,1:T(8,128)(2,1)S(1)} collective-permute-done((bf16[128,9,128]{0,2,1:T(8,128)(2,1)S(1)}, bf16[128,9,128]{0,2,1:T(8,128)(2,1)S(1)}, u32[]{:S(2)}, u32[]{:S(2)}) %collective-permute-start) | collective-permute-done | bytes 294944 | tf_op jit(solution)/shard_map/ppermute | solution.py:53
  20.5 0.3 fusion.22
  20.9 26.7 %all_to_all.20 = bf16[32,24,128]{2,1,0:T(8,128)(2,1)S(1)} all-to-all(bf16[32,24,128]{2,1,0:T(8,128)(2,1)S(1)} %fusion.35), channel_id=1, replica_groups={{0,1,16,17,64,65,80,81,128,129,144,145,192,193,208,209,256,257,272,273,..., dimensions={0} | all-to-all | bytes 393216 | tf_op jit(solution)/shard_map/all_to_all | solution.py:74
  47.7 0.8 broadcast_in_dim.18
  48.5 3.8 %all-to-all-start.1 = ((bf16[32,48,128]{2,1,0:T(8,128)(2,1)}), bf16[32,48,128]{2,1,0:T(8,128)(2,1)S(1)}, u32[]{:S(2)}, u32[]{:S(2)}) async-start(bf16[32,48,128]{2,1,0:T(8,128)(2,1)} %bitcast.18), calls=%async_computation.1 | async-start | bytes 786432 | tf_op jit(solution)/shard_map/all_to_all | solution.py:84
  52.9 13.7 %all-to-all-done.1 = bf16[32,48,128]{2,1,0:T(8,128)(2,1)S(1)} async-done(((bf16[32,48,128]{2,1,0:T(8,128)(2,1)}), bf16[32,48,128]{2,1,0:T(8,128)(2,1)S(1)}, u32[]{:S(2)}, u32[]{:S(2)}) %all-to-all-start.1) | async-done | bytes 393248 | tf_op jit(solution)/shard_map/all_to_all | solution.py:84
  66.7 0.4 fusion.28
  67.2 0.4 fusion.27
  67.6 0.4 convolution_add_fusion.1
  68.1 0.4 fusion.79
  68.4 0.4 fusion.6
  68.8 0.4 fusion.30
  69.3 0.3 fusion.16
  69.6 1.5 %multiply_convert_fusion = bf16[32,128,128]{1,2,0:T(8,128)(2,1)S(1)} fusion(bf16[448,32,128]{2,1,0:T(8,128)(2,1)S(1)} %bitcast.99, f32[448,128]{1,0:T(8,128)S(1)} %constant_dynamic-slice_fusion, f32[448]{0:T(512)S(1)} %fusion.61), kind=kOutput, calls=%fused_computation.4 | convolution fusion | flops 470925312 | bytes 4949760 | tf_op jit(solution)/shard_map/rk,ryx->ykx/dot_general | solution.py:101
  71.3 21.8 %all_to_all.21 = bf16[4,1280,128]{2,1,0:T(8,128)(2,1)S(1)} all-to-all(bf16[4,1280,128]{2,1,0:T(8,128)(2,1)S(1)} %pad_maximum_fusion), channel_id=1, replica_groups={{0,16,32,48},{2,18,34,50},{4,20,36,52},{6,22,38,54},{8,24,40,56},{10,26..., dimensions={0} | all-to-all | bytes 2621440 | tf_op jit(solution)/shard_map/all_to_all | solution.py:106
  93.1 0.4 reduce_sum.60
  93.7 28.4 %all_to_all.22 = bf16[8,384,128]{2,1,0:T(8,128)(2,1)S(1)} all-to-all(bf16[8,384,128]{2,1,0:T(8,128)(2,1)S(1)} %pad_maximum_fusion.1), channel_id=1, replica_groups={{0,2,4,6,8,10,12,14},{16,18,20,22,24,26,28,30},{32,34,36,38,40,42,44,46..., dimensions={0} | all-to-all | bytes 1572864 | tf_op jit(solution)/shard_map/all_to_all | solution.py:115
  122.6 0.2 fusion.78
  122.9 1.3 collective-permute-start.4
  124.2 4.0 %collective-permute-start.3 = (bf16[128,128]{0,1:T(8,128)(2,1)S(1)}, bf16[128,128]{0,1:T(8,128)(2,1)S(1)}, u32[]{:S(2)}, u32[]{:S(2)}) collective-permute-start(bf16[128,128]{0,1:T(8,128)(2,1)S(1)} %get-tuple-element.44), channel_id=1, source_target_pairs={{0,2},{2,4},{4,6},{6,8},{8,10},{10,12},{12,14},{14,16},{16,18},{18... | collective-permute-start | bytes 98312 | tf_op jit(solution)/shard_map/ppermute | solution.py:138
  128.2 4.7 %collective-permute-start.2 = (bf16[128,128]{0,1:T(8,128)(2,1)S(1)}, bf16[128,128]{0,1:T(8,128)(2,1)S(1)}, u32[]{:S(2)}, u32[]{:S(2)}) collective-permute-start(bf16[128,128]{0,1:T(8,128)(2,1)S(1)} %get-tuple-element.44), channel_id=1, source_target_pairs={{64,0},{128,64},{192,128},{256,192},{320,256},{384,320},{448,384},... | collective-permute-start | bytes 98312 | tf_op jit(solution)/shard_map/ppermute | solution.py:139
  132.9 1.9 %collective-permute-start.1 = (bf16[128,128]{0,1:T(8,128)(2,1)S(1)}, bf16[128,128]{0,1:T(8,128)(2,1)S(1)}, u32[]{:S(2)}, u32[]{:S(2)}) collective-permute-start(bf16[128,128]{0,1:T(8,128)(2,1)S(1)} %get-tuple-element.44), channel_id=1, source_target_pairs={{0,64},{64,128},{128,192},{192,256},{256,320},{320,384},{384,448},... | collective-permute-start | bytes 98312 | tf_op jit(solution)/shard_map/ppermute | solution.py:138
  134.9 0.7 copy.62
  135.6 0.4 collective-permute-done.1
  136.1 0.7 copy.61
  (53 shorter events, 1.5 us)
Async XLA Ops:
  0.6 14.4 %copy-start = (bf16[128,1,32,128]{3,2,1,0:T(8,128)(2,1)S(1)}, bf16[128,1,32,128]{3,2,1,0:T(8,128)(2,1)}, u32[]{:S(2)}) copy-start(bf16[128,1,32,128]{3,2,1,0:T(8,128)(2,1)} %param.6) | copy-start | bytes 3145732
  3.3 17.2 %collective-permute-start = (bf16[128,9,128]{0,2,1:T(8,128)(2,1)S(1)}, bf16[128,9,128]{0,2,1:T(8,128)(2,1)S(1)}, u32[]{:S(2)}, u32[]{:S(2)}) collective-permute-start(bf16[128,9,128]{0,2,1:T(8,128)(2,1)S(1)} %pad_maximum_fusion.2), channel_id=1, source_target_pairs={{0,1},{1,0},{2,3},{3,2},{4,5},{5,4},{6,7},{7,6},{8,9},{9,8},{10,11... | collective-permute-start | bytes 884744 | tf_op jit(solution)/shard_map/ppermute | solution.py:53
  48.5 18.1 %all-to-all-start.1 = ((bf16[32,48,128]{2,1,0:T(8,128)(2,1)}), bf16[32,48,128]{2,1,0:T(8,128)(2,1)S(1)}, u32[]{:S(2)}, u32[]{:S(2)}) async-start(bf16[32,48,128]{2,1,0:T(8,128)(2,1)} %bitcast.18), calls=%async_computation.1 | async-start | bytes 786432 | tf_op jit(solution)/shard_map/all_to_all | solution.py:84
  67.6 2.0 %copy-start.5 = (bf16[448,1,32,128]{3,2,1,0:T(8,128)(2,1)S(1)}, bf16[448,1,32,128]{3,2,1,0:T(8,128)(2,1)}, u32[]{:S(2)}) copy-start(bf16[448,1,32,128]{3,2,1,0:T(8,128)(2,1)} %param.5) | copy-start | bytes 11010052
  69.2 1.9 %copy-start.1 = (f32[448,128]{1,0:T(8,128)}, f32[448,128]{1,0:T(8,128)S(1)}, u32[]{:S(2)}) copy-start(f32[448,128]{1,0:T(8,128)S(1)} %constant_dynamic-slice_fusion) | copy-start | bytes 688132
  93.5 28.6 %copy-start.4 = (f32[128,1,1,128]{3,2,1,0:T(1,128)S(1)}, f32[128,1,1,128]{3,2,1,0:T(1,128)}, u32[]{:S(2)}) copy-start(f32[128,1,1,128]{3,2,1,0:T(1,128)} %param.8) | copy-start | bytes 196612
  93.6 28.9 %copy-start.3 = (f32[128,256]{1,0:T(8,128)S(1)}, f32[128,256]{1,0:T(8,128)}, u32[]{:S(2)}) copy-start(f32[128,256]{1,0:T(8,128)} %param.7) | copy-start | bytes 393220
  122.5 14.3 %copy-start.2 = (f32[128,256]{1,0:T(8,128)}, f32[128,256]{1,0:T(8,128)S(1)}, u32[]{:S(2)}) copy-start(f32[128,256]{1,0:T(8,128)S(1)} %maximum_add_fusion) | copy-start | bytes 393220
  122.9 12.7 %collective-permute-start.4 = (bf16[128,128]{0,1:T(8,128)(2,1)S(1)}, bf16[128,128]{0,1:T(8,128)(2,1)S(1)}, u32[]{:S(2)}, u32[]{:S(2)}) collective-permute-start(bf16[128,128]{0,1:T(8,128)(2,1)S(1)} %get-tuple-element.44), channel_id=1, source_target_pairs={{2,0},{4,2},{6,4},{8,6},{10,8},{12,10},{14,12},{16,14},{18,16},{20... | collective-permute-start | bytes 98312 | tf_op jit(solution)/shard_map/ppermute | solution.py:139
  124.2 11.4 %collective-permute-start.3 = (bf16[128,128]{0,1:T(8,128)(2,1)S(1)}, bf16[128,128]{0,1:T(8,128)(2,1)S(1)}, u32[]{:S(2)}, u32[]{:S(2)}) collective-permute-start(bf16[128,128]{0,1:T(8,128)(2,1)S(1)} %get-tuple-element.44), channel_id=1, source_target_pairs={{0,2},{2,4},{4,6},{6,8},{8,10},{10,12},{12,14},{14,16},{16,18},{18... | collective-permute-start | bytes 98312 | tf_op jit(solution)/shard_map/ppermute | solution.py:138
  128.2 7.4 %collective-permute-start.2 = (bf16[128,128]{0,1:T(8,128)(2,1)S(1)}, bf16[128,128]{0,1:T(8,128)(2,1)S(1)}, u32[]{:S(2)}, u32[]{:S(2)}) collective-permute-start(bf16[128,128]{0,1:T(8,128)(2,1)S(1)} %get-tuple-element.44), channel_id=1, source_target_pairs={{64,0},{128,64},{192,128},{256,192},{320,256},{384,320},{448,384},... | collective-permute-start | bytes 98312 | tf_op jit(solution)/shard_map/ppermute | solution.py:139
  132.9 3.1 %collective-permute-start.1 = (bf16[128,128]{0,1:T(8,128)(2,1)S(1)}, bf16[128,128]{0,1:T(8,128)(2,1)S(1)}, u32[]{:S(2)}, u32[]{:S(2)}) collective-permute-start(bf16[128,128]{0,1:T(8,128)(2,1)S(1)} %get-tuple-element.44), channel_id=1, source_target_pairs={{0,64},{64,128},{128,192},{192,256},{256,320},{320,384},{384,448},... | collective-permute-start | bytes 98312 | tf_op jit(solution)/shard_map/ppermute | solution.py:138

commit v4 on v3

--- a/solution.py
+++ b/solution.py
@@ -101,21 +101,29 @@
     term = jnp.einsum("rk,ryx->ykx", weighted_low, scans3, preferred_element_type=WIDE)
     term = (term * (0.5 / math.sqrt(total_rows))).astype(LOW).reshape(X_SIZE, Y_SIZE * own_count, width)
     product = jnp.dot(weighted_low.T, whole.astype(LOW), preferred_element_type=WIDE) * (0.5 / total_rows)
-    product = jnp.concatenate([product[:, :own_count], product[:, own_count:]], axis=0).astype(LOW)
-    sent = jnp.concatenate([term, jnp.broadcast_to(product, (X_SIZE,) + product.shape)], axis=1)
+    share = own_count // slabs
+    mine = lax.dynamic_slice_in_dim(product, slab * share, share, 0).astype(LOW)
+    mine = jnp.concatenate([mine[:, :own_count], mine[:, own_count:]], axis=0)
+    sent = jnp.concatenate([term, jnp.broadcast_to(mine, (X_SIZE, 2 * share, width))], axis=1)
     taken = lax.all_to_all(sent, "subj", 0, 0, axis_index_groups=x_groups).astype(WIDE).sum(0).astype(LOW)
     split = Y_SIZE * own_count
     sent = jnp.concatenate(
         [
             taken[:split].reshape(Y_SIZE, own_count, width),
-            jnp.broadcast_to(taken[split:], (Y_SIZE, 2 * own_count, width)),
+            jnp.broadcast_to(taken[split:], (Y_SIZE, 2 * share, width)),
         ],
         axis=1,
     )
     summed = lax.all_to_all(sent, "subj", 0, 0, axis_index_groups=y_groups)
-    summed, stats_old, gram_old, got, own_line = lax.optimization_barrier((summed, stats_old, gram_old, got, own_line))
+    summed, stats_old, gram_old = lax.optimization_barrier((summed, stats_old, gram_old))
     summed = summed.astype(WIDE).sum(0)
-    product = jnp.concatenate([summed[own_count : 2 * own_count], summed[2 * own_count :]], axis=1)
+    mine = jnp.broadcast_to(summed[own_count:].astype(LOW), (slabs, 2 * share, width))
+    product = lax.all_to_all(mine, "slab", 0, 0)
+    product, summed, stats_old, got, own_line = lax.optimization_barrier((product, summed, stats_old, got, own_line))
+    product = product.astype(WIDE)
+    product = jnp.concatenate(
+        [product[:, :share].reshape(own_count, own_count), product[:, share:].reshape(own_count, own_count)], axis=1
+    )
     gram_new = 0.5 * gram_old + product
     stats_line = 0.5 * stats_old.reshape(own_count, width) + summed[:own_count]
 

time: 137 us -> 134 us (0.978)
  blocking collectives: 76.9 us -> 74.3 us
    all_to_all x1, blocking collectives: 28.4 us -> 19 us  [on_device(): summed = lax.all_to_all(sent, 'subj', 0, 0, axis_index_groups=y_groups)]
    all_to_all x0 -> x1, blocking collectives: none -> 9.36 us  [on_device(): product = lax.all_to_all(mine, 'slab', 0, 0)]
    all_to_all x1, blocking collectives: 21.8 us -> 19.3 us  [on_device(): lax.all_to_all(sent, 'subj', 0, 0, axis_index_groups=x_groups).astype(WIDE)]
    ppermute x2, starting transfers between devices: 6.03 us -> 4.61 us  [on_device(): sides.append(lax.ppermute(edge, axis, [(b, a) for a, b in up]) + 0.0)]
where the time goes in v4:
time: 134 us; the launch traced here: 133 us
  blocking collectives  74.3 us (55%)
  starting transfers between devices  26.1 us (19%)
  waiting for transfers between devices  15.5 us (12%)
  matrix products  8.48 us (6%)
  local copies, waits for them, and re-layouts  6.15 us (5%)
  between operations  1.84 us (1%)
    all_to_all x1, blocking collectives, on_device(): lax.all_to_all(sent, whole_axes, 0, 0, axis_index_groups=ring_groups)  26.7 us
    all_to_all x1, blocking collectives, on_device(): lax.all_to_all(sent, 'subj', 0, 0, axis_index_groups=x_groups).astype(WIDE)  19.3 us
    all_to_all x1, blocking collectives, on_device(): summed = lax.all_to_all(sent, 'subj', 0, 0, axis_index_groups=y_groups)  19 us
    all_to_all x1, waiting for transfers between devices, on_device(): back = lax.all_to_all(back, whole_axes, 0, 0, axis_index_groups=ring_groups)  13.7 us
    ppermute x1, starting transfers between devices, on_device(): lax.ppermute(jnp.concatenate([to_partner, own_line], axis=1), 'comp', [(0...  11.5 us
    all_to_all x1, blocking collectives, on_device(): product = lax.all_to_all(mine, 'slab', 0, 0)  9.36 us
    ppermute x2, starting transfers between devices, on_device(): sides.append(lax.ppermute(edge, axis, up) + 0.0)  6.25 us
    ppermute x2, starting transfers between devices, on_device(): sides.append(lax.ppermute(edge, axis, [(b, a) for a, b in up]) + 0.0)  4.61 us
  transfers between devices with their start and end apart: 6, of which 3 were waited for; matrix products, arithmetic and copies ran while one was open for 4% of the time, Pallas kernels for 0%

profile of v4, /device:TPU:1, one launch (start us, length us, event | category | flops | bytes accessed | tf_op | source)
XLA Modules:
  0.0 133.2 jit_solution(17726528707224393976)
XLA Ops:
  0.7 1.1 constant_dynamic-slice_fusion.1
  1.9 1.1 constant_dynamic-slice_fusion.2
  3.3 11.5 %collective-permute-start = (bf16[128,9,128]{0,2,1:T(8,128)(2,1)S(1)}, bf16[128,9,128]{0,2,1:T(8,128)(2,1)S(1)}, u32[]{:S(2)}, u32[]{:S(2)}) collective-permute-start(bf16[128,9,128]{0,2,1:T(8,128)(2,1)S(1)} %pad_maximum_fusion.2), channel_id=1, source_target_pairs={{0,1},{1,0},{2,3},{3,2},{4,5},{5,4},{6,7},{7,6},{8,9},{9,8},{10,11... | collective-permute-start | bytes 884744 | tf_op jit(solution)/shard_map/ppermute | solution.py:53
  15.2 0.3 convolution_bitcast_fusion
  15.5 3.4 %fusion.13 = bf16[448,128]{1,0:T(8,128)(2,1)S(1)} fusion(bf16[448,32,128]{2,1,0:T(8,128)(2,1)} %bitcast.102, bf16[128,32,128]{2,1,0:T(8,128)(2,1)S(1)} %bitcast.73), kind=kOutput, calls=%fused_computation.10 | convolution fusion | flops 469876736 | bytes 4833280 | tf_op jit(solution)/shard_map/ryx,kyx->rk/dot_general | solution.py:55
  18.9 1.6 %collective-permute-done = bf16[128,9,128]{0,2,1:T(8,128)(2,1)S(1)} collective-permute-done((bf16[128,9,128]{0,2,1:T(8,128)(2,1)S(1)}, bf16[128,9,128]{0,2,1:T(8,128)(2,1)S(1)}, u32[]{:S(2)}, u32[]{:S(2)}) %collective-permute-start) | collective-permute-done | bytes 294944 | tf_op jit(solution)/shard_map/ppermute | solution.py:53
  20.5 0.3 fusion.21
  20.9 26.7 %all_to_all.25 = bf16[32,24,128]{2,1,0:T(8,128)(2,1)S(1)} all-to-all(bf16[32,24,128]{2,1,0:T(8,128)(2,1)S(1)} %fusion.35), channel_id=1, replica_groups={{0,1,16,17,64,65,80,81,128,129,144,145,192,193,208,209,256,257,272,273,..., dimensions={0} | all-to-all | bytes 393216 | tf_op jit(solution)/shard_map/all_to_all | solution.py:74
  47.7 0.8 broadcast_in_dim.21
  48.5 3.8 %all-to-all-start.1 = ((bf16[32,48,128]{2,1,0:T(8,128)(2,1)}), bf16[32,48,128]{2,1,0:T(8,128)(2,1)S(1)}, u32[]{:S(2)}, u32[]{:S(2)}) async-start(bf16[32,48,128]{2,1,0:T(8,128)(2,1)} %bitcast.18), calls=%async_computation.1 | async-start | bytes 786432 | tf_op jit(solution)/shard_map/all_to_all | solution.py:84
  52.9 13.7 %all-to-all-done.1 = bf16[32,48,128]{2,1,0:T(8,128)(2,1)S(1)} async-done(((bf16[32,48,128]{2,1,0:T(8,128)(2,1)}), bf16[32,48,128]{2,1,0:T(8,128)(2,1)S(1)}, u32[]{:S(2)}, u32[]{:S(2)}) %all-to-all-start.1) | async-done | bytes 393248 | tf_op jit(solution)/shard_map/all_to_all | solution.py:84
  66.7 0.4 fusion.27
  67.2 0.4 fusion.26
  67.6 0.4 convolution_add_fusion.1
  68.1 0.4 fusion.80
  68.4 0.4 fusion.6
  68.8 0.4 fusion.29
  69.3 0.3 fusion.33
  69.6 0.5 copy-done.5
  70.1 1.5 %multiply_convert_fusion = bf16[32,128,128]{1,2,0:T(8,128)(2,1)S(1)} fusion(bf16[448,32,128]{2,1,0:T(8,128)(2,1)S(1)} %bitcast.103, f32[448,128]{1,0:T(8,128)S(1)} %constant_dynamic-slice_fusion, f32[448]{0:T(512)S(1)} %fusion.62), kind=kOutput, calls=%fused_computation.4 | convolution fusion | flops 470925312 | bytes 4949760 | tf_op jit(solution)/shard_map/rk,ryx->ykx/dot_general | solution.py:101
  71.7 19.3 %all_to_all.26 = bf16[4,1056,128]{2,1,0:T(8,128)(2,1)S(1)} all-to-all(bf16[4,1056,128]{2,1,0:T(8,128)(2,1)S(1)} %pad_maximum_fusion), channel_id=1, replica_groups={{0,16,32,48},{2,18,34,50},{4,20,36,52},{6,22,38,54},{8,24,40,56},{10,26..., dimensions={0} | all-to-all | bytes 2162688 | tf_op jit(solution)/shard_map/all_to_all | solution.py:108
  91.1 0.3 reduce_sum.60
  91.4 19.0 %all_to_all.27 = bf16[8,160,128]{2,1,0:T(8,128)(2,1)S(1)} all-to-all(bf16[8,160,128]{2,1,0:T(8,128)(2,1)S(1)} %pad_maximum_fusion.1), channel_id=1, replica_groups={{0,2,4,6,8,10,12,14},{16,18,20,22,24,26,28,30},{32,34,36,38,40,42,44,46..., dimensions={0} | all-to-all | bytes 655360 | tf_op jit(solution)/shard_map/all_to_all | solution.py:117
  110.5 9.4 %all_to_all.28 = bf16[8,32,128]{2,1,0:T(8,128)(2,1)S(1)} all-to-all(bf16[8,32,128]{2,1,0:T(8,128)(2,1)S(1)} %broadcast_in_dim.24), channel_id=1, replica_groups=mesh['slab'=8,'subj'=32,'comp'=2] {'slab'}, dimensions={0} | all-to-all | bytes 131072 | tf_op jit(solution)/shard_map/all_to_all | solution.py:121
  120.2 0.2 fusion.79
  120.5 1.3 collective-permute-start.4
  121.8 4.0 %collective-permute-start.3 = (bf16[128,128]{0,1:T(8,128)(2,1)S(1)}, bf16[128,128]{0,1:T(8,128)(2,1)S(1)}, u32[]{:S(2)}, u32[]{:S(2)}) collective-permute-start(bf16[128,128]{0,1:T(8,128)(2,1)S(1)} %get-tuple-element.49), channel_id=1, source_target_pairs={{0,2},{2,4},{4,6},{6,8},{8,10},{10,12},{12,14},{14,16},{16,18},{18... | collective-permute-start | bytes 98312 | tf_op jit(solution)/shard_map/ppermute | solution.py:146
  125.8 3.3 %collective-permute-start.2 = (bf16[128,128]{0,1:T(8,128)(2,1)S(1)}, bf16[128,128]{0,1:T(8,128)(2,1)S(1)}, u32[]{:S(2)}, u32[]{:S(2)}) collective-permute-start(bf16[128,128]{0,1:T(8,128)(2,1)S(1)} %get-tuple-element.49), channel_id=1, source_target_pairs={{64,0},{128,64},{192,128},{256,192},{320,256},{384,320},{448,384},... | collective-permute-start | bytes 98312 | tf_op jit(solution)/shard_map/ppermute | solution.py:147
  129.1 2.3 %collective-permute-start.1 = (bf16[128,128]{0,1:T(8,128)(2,1)S(1)}, bf16[128,128]{0,1:T(8,128)(2,1)S(1)}, u32[]{:S(2)}, u32[]{:S(2)}) collective-permute-start(bf16[128,128]{0,1:T(8,128)(2,1)S(1)} %get-tuple-element.49), channel_id=1, source_target_pairs={{0,64},{64,128},{128,192},{192,256},{256,320},{320,384},{384,448},... | collective-permute-start | bytes 98312 | tf_op jit(solution)/shard_map/ppermute | solution.py:146
  131.4 0.7 copy.60
  132.1 0.2 collective-permute-done.1
  132.4 0.7 copy.59
  (57 shorter events, 1.8 us)
Async XLA Ops:
  0.6 14.4 %copy-start = (bf16[128,1,32,128]{3,2,1,0:T(8,128)(2,1)S(1)}, bf16[128,1,32,128]{3,2,1,0:T(8,128)(2,1)}, u32[]{:S(2)}) copy-start(bf16[128,1,32,128]{3,2,1,0:T(8,128)(2,1)} %param.6) | copy-start | bytes 3145732
  3.3 17.2 %collective-permute-start = (bf16[128,9,128]{0,2,1:T(8,128)(2,1)S(1)}, bf16[128,9,128]{0,2,1:T(8,128)(2,1)S(1)}, u32[]{:S(2)}, u32[]{:S(2)}) collective-permute-start(bf16[128,9,128]{0,2,1:T(8,128)(2,1)S(1)} %pad_maximum_fusion.2), channel_id=1, source_target_pairs={{0,1},{1,0},{2,3},{3,2},{4,5},{5,4},{6,7},{7,6},{8,9},{9,8},{10,11... | collective-permute-start | bytes 884744 | tf_op jit(solution)/shard_map/ppermute | solution.py:53
  48.5 18.1 %all-to-all-start.1 = ((bf16[32,48,128]{2,1,0:T(8,128)(2,1)}), bf16[32,48,128]{2,1,0:T(8,128)(2,1)S(1)}, u32[]{:S(2)}, u32[]{:S(2)}) async-start(bf16[32,48,128]{2,1,0:T(8,128)(2,1)} %bitcast.18), calls=%async_computation.1 | async-start | bytes 786432 | tf_op jit(solution)/shard_map/all_to_all | solution.py:84
  68.0 2.0 %copy-start.5 = (bf16[448,1,32,128]{3,2,1,0:T(8,128)(2,1)S(1)}, bf16[448,1,32,128]{3,2,1,0:T(8,128)(2,1)}, u32[]{:S(2)}) copy-start(bf16[448,1,32,128]{3,2,1,0:T(8,128)(2,1)} %param.5) | copy-start | bytes 11010052
  69.2 2.4 %copy-start.1 = (f32[448,128]{1,0:T(8,128)}, f32[448,128]{1,0:T(8,128)S(1)}, u32[]{:S(2)}) copy-start(f32[448,128]{1,0:T(8,128)S(1)} %constant_dynamic-slice_fusion) | copy-start | bytes 688132
  91.1 28.8 %copy-start.4 = (f32[128,1,1,128]{3,2,1,0:T(1,128)S(1)}, f32[128,1,1,128]{3,2,1,0:T(1,128)}, u32[]{:S(2)}) copy-start(f32[128,1,1,128]{3,2,1,0:T(1,128)} %param.8) | copy-start | bytes 196612
  91.1 29.0 %copy-start.3 = (f32[128,256]{1,0:T(8,128)S(1)}, f32[128,256]{1,0:T(8,128)}, u32[]{:S(2)}) copy-start(f32[128,256]{1,0:T(8,128)} %param.7) | copy-start | bytes 393220
  120.1 13.0 %copy-start.2 = (f32[128,256]{1,0:T(8,128)}, f32[128,256]{1,0:T(8,128)S(1)}, u32[]{:S(2)}) copy-start(f32[128,256]{1,0:T(8,128)S(1)} %maximum_add_fusion) | copy-start | bytes 393220
  120.5 11.6 %collective-permute-start.4 = (bf16[128,128]{0,1:T(8,128)(2,1)S(1)}, bf16[128,128]{0,1:T(8,128)(2,1)S(1)}, u32[]{:S(2)}, u32[]{:S(2)}) collective-permute-start(bf16[128,128]{0,1:T(8,128)(2,1)S(1)} %get-tuple-element.49), channel_id=1, source_target_pairs={{2,0},{4,2},{6,4},{8,6},{10,8},{12,10},{14,12},{16,14},{18,16},{20... | collective-permute-start | bytes 98312 | tf_op jit(solution)/shard_map/ppermute | solution.py:147
  121.8 10.3 %collective-permute-start.3 = (bf16[128,128]{0,1:T(8,128)(2,1)S(1)}, bf16[128,128]{0,1:T(8,128)(2,1)S(1)}, u32[]{:S(2)}, u32[]{:S(2)}) collective-permute-start(bf16[128,128]{0,1:T(8,128)(2,1)S(1)} %get-tuple-element.49), channel_id=1, source_target_pairs={{0,2},{2,4},{4,6},{6,8},{8,10},{10,12},{12,14},{14,16},{16,18},{18... | collective-permute-start | bytes 98312 | tf_op jit(solution)/shard_map/ppermute | solution.py:146
  125.8 6.4 %collective-permute-start.2 = (bf16[128,128]{0,1:T(8,128)(2,1)S(1)}, bf16[128,128]{0,1:T(8,128)(2,1)S(1)}, u32[]{:S(2)}, u32[]{:S(2)}) collective-permute-start(bf16[128,128]{0,1:T(8,128)(2,1)S(1)} %get-tuple-element.49), channel_id=1, source_target_pairs={{64,0},{128,64},{192,128},{256,192},{320,256},{384,320},{448,384},... | collective-permute-start | bytes 98312 | tf_op jit(solution)/shard_map/ppermute | solution.py:147
  129.1 3.3 %collective-permute-start.1 = (bf16[128,128]{0,1:T(8,128)(2,1)S(1)}, bf16[128,128]{0,1:T(8,128)(2,1)S(1)}, u32[]{:S(2)}, u32[]{:S(2)}) collective-permute-start(bf16[128,128]{0,1:T(8,128)(2,1)S(1)} %get-tuple-element.49), channel_id=1, source_target_pairs={{0,64},{64,128},{128,192},{192,256},{256,320},{320,384},{384,448},... | collective-permute-start | bytes 98312 | tf_op jit(solution)/shard_map/ppermute | solution.py:146

commit v5 on v3

v5 whole, which is shorter than its diff:
```python
import math

import jax
import jax.numpy as jnp
from jax import lax
from jax.sharding import PartitionSpec as P

COMPONENTS = 256
ITERS = 12
X_SIZE = 4
Y_SIZE = 8
LOW = jnp.bfloat16
WIDE = jnp.float32
SWAP = [(0, 1), (1, 0)]


def power_sum(gram):
    dot = lambda a, b: jnp.dot(a, b, precision=lax.Precision.HIGHEST)
    eye = jnp.eye(COMPONENTS, dtype=WIDE)
    first = 0.98 * eye - 0.1 * gram
    second = dot(first, first)
    third = dot(second, first)
    sum3 = eye + first + second
    sum6 = sum3 + dot(third, sum3)
    sixth = dot(third, third)
    return 0.1 * (sum6 + dot(sixth, sum6))


def on_device(scans, maps, gram_old, stats_old, kept):
    highest = lax.Precision.HIGHEST
    slabs = lax.axis_size("slab")
    subjects = lax.axis_size("subj")
    volumes = scans.shape[0]
    own_count, _, lines, width = maps.shape
    voxel_total = slabs * lines * width
    total_rows = volumes * subjects
    slab, subj, comp = lax.axis_index("slab"), lax.axis_index("subj"), lax.axis_index("comp")
    at_x = subj // Y_SIZE
    ring = slabs * 2
    ring_axes = ("slab", "comp")
    x_groups = [[x * Y_SIZE + y for x in range(X_SIZE)] for y in range(Y_SIZE)]
    y_groups = [[x * Y_SIZE + y for y in range(Y_SIZE)] for x in range(X_SIZE)]

    scans3 = scans.reshape(volumes, lines, width)
    maps3 = maps.reshape(own_count, lines, width)
    part = lines // (2 * X_SIZE)
    own_line = lax.dynamic_slice_in_dim(maps3, subj, 1, 1)
    to_partner = lax.dynamic_slice_in_dim(maps3, (2 * at_x + 1 - comp) * part, part, 1)
    got = lax.ppermute(jnp.concatenate([to_partner, own_line], axis=1), "comp", SWAP)

    proj_part = jnp.einsum("ryx,kyx->rk", scans3, maps3, preferred_element_type=WIDE)
    proj_part = (proj_part * (1.0 / math.sqrt(voxel_total))).astype(LOW)
    rows = 32
    pieces = volumes // rows
    few = own_count // ring
    sent = jnp.pad(proj_part.reshape(pieces, rows, own_count), ((0, ring - pieces), (0, 0), (0, 0)))
    taken = lax.all_to_all(sent, ring_axes, 0, 0)
    proj_rows = taken.reshape(slabs, 2, rows, own_count).astype(WIDE).sum(0).astype(LOW)

    own_lines = lax.dynamic_slice_in_dim(maps3, at_x * 2 * part, 2 * part, 1)
    own_half = lax.dynamic_slice_in_dim(maps3, (2 * at_x + comp) * part, part, 1)
    gram_own = jnp.einsum("ayx,byx->ab", own_lines, own_lines, preferred_element_type=WIDE)
    first = jnp.where(comp == 0, own_half, got[:, :part])
    second = jnp.where(comp == 0, got[:, :part], own_half)
    gram_cross = jnp.einsum("ayx,byx->ab", first, second, preferred_element_type=WIDE)
    gram_parts = jnp.concatenate(
        [gram_own.reshape(ring, few, own_count), gram_cross.reshape(ring, few, own_count)], axis=1
    )
    gram_parts = (gram_parts * (1.0 / voxel_total)).astype(LOW)
    proj_rows = jnp.broadcast_to(proj_rows.reshape(2 * rows, own_count), (ring, 2 * rows, own_count))
    back = lax.all_to_all(jnp.concatenate([proj_rows, gram_parts], axis=1), ring_axes, 0, 0)
    proj_pair = [back[:pieces, i * rows : (i + 1) * rows].reshape(volumes, own_count) for i in range(2)]
    proj = jnp.concatenate(proj_pair, axis=1)
    gram_rows = back[:, 2 * rows :].astype(WIDE).reshape(slabs, 2, 2 * few, own_count).sum(0)
    gram_rows = jnp.concatenate(
        [gram_rows[:, :few].reshape(2 * few, own_count), gram_rows[:, few:].sum(0)], axis=0
    ).astype(LOW)

    live = (lax.iota(jnp.int32, volumes) < kept[0]).astype(LOW)
    live_proj = jnp.where(comp == 0, proj_pair[0], proj_pair[1]) * live[:, None]
    term = jnp.einsum("rk,ryx->ykx", live_proj, scans3, preferred_element_type=WIDE)
    term = (term * (0.5 / math.sqrt(total_rows))).astype(LOW).reshape(X_SIZE, Y_SIZE * own_count, width)
    product = jnp.dot(live_proj.T, proj, preferred_element_type=WIDE) * (0.5 / total_rows)
    share = own_count // slabs
    mine = lax.dynamic_slice_in_dim(product, slab * share, share, 0).astype(LOW)
    mine = jnp.concatenate([mine[:, :own_count], mine[:, own_count:], gram_rows], axis=0)
    sent = jnp.concatenate([term, jnp.broadcast_to(mine, (X_SIZE,) + mine.shape)], axis=1)
    taken = lax.all_to_all(sent, "subj", 0, 0, axis_index_groups=x_groups).astype(WIDE).sum(0).astype(LOW)
    split = Y_SIZE * own_count
    gram_rows = taken[split + 2 * share :]
    mine = taken[split : split + 2 * share]
    sent = jnp.concatenate(
        [
            taken[:split].reshape(Y_SIZE, own_count, width),
            jnp.broadcast_to(mine, (Y_SIZE,) + mine.shape),
        ],
        axis=1,
    )
    summed = lax.all_to_all(sent, "subj", 0, 0, axis_index_groups=y_groups)
    summed = summed.astype(WIDE).sum(0).astype(LOW)
    own_stats = summed[:own_count]
    other_stats = lax.ppermute(own_stats, "comp", SWAP)
    mine = jnp.concatenate([summed[own_count:], gram_rows], axis=0)
    shared = lax.all_to_all(jnp.broadcast_to(mine, (ring,) + mine.shape), ring_axes, 0, 0)

    gram_at = 2 * share
    low_block, high_block, cross = [
        shared[:, gram_at + i * few : gram_at + (i + 1) * few].reshape(own_count, own_count) for i in range(3)
    ]
    gram = jnp.concatenate(
        [jnp.concatenate([low_block, cross], axis=1), jnp.concatenate([cross.T, high_block], axis=1)], axis=0
    ).astype(WIDE)
    coding = power_sum(gram)
    own_coding = lax.dynamic_slice_in_dim(coding, comp * own_count, own_count, 1)
    product = jnp.transpose(shared[:, :gram_at].reshape(slabs, 2, 2, share, own_count), (1, 0, 3, 2, 4))
    product = product.reshape(COMPONENTS, COMPONENTS).astype(WIDE)
    product = jnp.dot(jnp.dot(own_coding.T, product, precision=highest), coding, precision=highest)
    codes = jnp.dot(proj.astype(WIDE), own_coding, precision=highest)
    both_stats = jnp.where(
        comp == 0,
        jnp.concatenate([own_stats, other_stats], axis=0),
        jnp.concatenate([other_stats, own_stats], axis=0),
    ).astype(WIDE)
    stats_line = 0.5 * stats_old.reshape(own_count, width) + jnp.dot(own_coding.T, both_stats, precision=highest)
    gram_new = 0.5 * gram_old + product
    own_piece = own_line.reshape(own_count, width)
    other_piece = got[:, part]
    piece = jnp.where(
        comp == 0,
        jnp.concatenate([own_piece, other_piece], axis=0),
        jnp.concatenate([other_piece, own_piece], axis=0),
    ).astype(WIDE)
    block = lax.dynamic_slice_in_dim(gram_new, comp * own_count, own_count, 1)
    diag = jnp.sum(block * jnp.eye(own_count, dtype=WIDE), axis=1, keepdims=True)
    coupled = jnp.dot(gram_new, piece, precision=highest)
    updated = own_piece.astype(WIDE) + (stats_line - coupled) / diag
    edge = updated.astype(LOW)
    sides = []
    for axis in ("slab", "subj"):
        count = lax.axis_size(axis)
        up = [(i, i + 1) for i in range(count - 1)]
        sides.append(lax.ppermute(edge, axis, up) + 0.0)
        sides.append(lax.ppermute(edge, axis, [(b, a) for a, b in up]) + 0.0)
    z_low, z_high, y_low, y_high = [side.astype(WIDE) for side in sides]
    side_x = jnp.pad(updated, ((0, 0), (1, 1)))
    lap_x = side_x[:, 2:] + side_x[:, :-2] - 2.0 * updated
    lap_z = z_low + z_high - 2.0 * updated
    lap_y = y_low + y_high - 2.0 * updated
    maps_new = (updated + 0.24 * lap_z + 0.18 * lap_y + 0.12 * lap_x).astype(LOW)
    return (
        maps_new.reshape(own_count, 1, 1, width),
        stats_line.reshape(own_count, 1, 1, width),
        gram_new,
        codes,
    )


def solution(mesh):
    in_specs = (
        P("subj", "slab", None, None),
        P("comp", "slab", None, None),
        P("comp", None),
        P("comp", "slab", "subj", None),
        P("subj"),
    )
    out_specs = (
        P("comp", "slab", "subj", None),
        P("comp", "slab", "subj", None),
        P("comp", None),
        P("subj", "comp"),
    )
    return jax.shard_map(
        on_device, mesh=mesh, in_specs=in_specs, out_specs=out_specs, check_vma=False
    )
```

time: 137 us -> 132 us (0.964)
  blocking collectives: 76.9 us -> 18.2 us
  starting transfers between devices: 27.2 us -> 60.3 us
  waiting for transfers between devices: 15.6 us -> 32.3 us
  matrix products: 8.48 us -> 12.2 us
  local copies, waits for them, and re-layouts: 5.8 us -> 4.07 us
  other arithmetic: 0.94 us -> 2.31 us
    all_to_all x2 -> x0, blocking collectives: 55.1 us -> none  [the longest x1 28.4 us: on_device(): summed = lax.all_to_all(sent, 'subj', 0, 0, axis_index_groups=y_groups)]
    all_to_all x1 -> x4, starting transfers between devices: 3.78 us -> 34.4 us  [the longest x1 11.8 us: on_device(): taken = lax.all_to_all(sent, ring_axes, 0, 0)]
    all_to_all x1 -> x4, waiting for transfers between devices: 13.7 us -> 25.6 us  [the longest x1 11.9 us: on_device(): lax.all_to_all(jnp.concatenate([proj_rows, gram_parts], axis=1), ring_axe...]
    ppermute x1 -> x2, waiting for transfers between devices: 1.57 us -> 6.74 us  [the longest x1 6.74 us: on_device(): lax.ppermute(jnp.concatenate([to_partner, own_line], axis=1), 'comp', SWAP)]
    all_to_all x1, blocking collectives: 21.8 us -> 18.2 us  [on_device(): lax.all_to_all(sent, 'subj', 0, 0, axis_index_groups=x_groups).astype(WIDE)]
    dot_general x3 -> x6, matrix products: 2.26 us -> 5.75 us  [the longest x1 3.56 us: on_device(): jnp.einsum('rk,ryx->ykx', live_proj, scans3, preferred_element_type=WIDE)]
    ppermute x1 -> x2, starting transfers between devices: 11.5 us -> 14.4 us  [the longest x1 7.2 us: on_device(): lax.ppermute(jnp.concatenate([to_partner, own_line], axis=1), 'comp', SWAP)]
  transfers between devices with their start and end apart: 6 -> 10, of which waited for: 3 -> 4; matrix products, arithmetic and copies ran while one was open for 4% -> 5% of each run, Pallas kernels for 0% -> 0%
where the time goes in v5:
time: 132 us; the launch traced here: 131 us
  starting transfers between devices  60.3 us (46%)
  waiting for transfers between devices  32.3 us (24%)
  blocking collectives  18.2 us (14%)
  matrix products  12.2 us (9%)
  local copies, waits for them, and re-layouts  4.07 us (3%)
  other arithmetic  2.31 us (2%)
  between operations  1.78 us (1%)
    all_to_all x1, blocking collectives, on_device(): lax.all_to_all(sent, 'subj', 0, 0, axis_index_groups=x_groups).astype(WIDE)  18.2 us
    all_to_all x1, waiting for transfers between devices, on_device(): lax.all_to_all(jnp.concatenate([proj_rows, gram_parts], axis=1), ring_axe...  11.9 us
    all_to_all x1, starting transfers between devices, on_device(): taken = lax.all_to_all(sent, ring_axes, 0, 0)  11.8 us
    all_to_all x1, waiting for transfers between devices, on_device(): summed = lax.all_to_all(sent, 'subj', 0, 0, axis_index_groups=y_groups)  10.1 us
    all_to_all x1, starting transfers between devices, on_device(): lax.all_to_all(jnp.broadcast_to(mine, (ring,) + mine.shape), ring_axes, 0...  8.27 us
    all_to_all x1, starting transfers between devices, on_device(): lax.all_to_all(jnp.concatenate([proj_rows, gram_parts], axis=1), ring_axe...  7.49 us
    ppermute x1, starting transfers between devices, on_device(): lax.ppermute(jnp.concatenate([to_partner, own_line], axis=1), 'comp', SWAP)  7.2 us
    ppermute x1, starting transfers between devices, on_device(): other_stats = lax.ppermute(own_stats, 'comp', SWAP)  7.2 us
  transfers between devices with their start and end apart: 10, of which 4 were waited for; matrix products, arithmetic and copies ran while one was open for 5% of the time, Pallas kernels for 0%

profile of v5, /device:TPU:1, one launch (start us, length us, event | category | flops | bytes accessed | tf_op | source)
XLA Modules:
  0.0 131.2 jit_solution(2267214307324585398)
XLA Ops:
  0.6 3.8 %fusion.13 = bf16[448,128]{1,0:T(8,128)(2,1)S(1)} fusion(bf16[448,32,128]{2,1,0:T(8,128)(2,1)} %bitcast.85, bf16[128,32,128]{2,1,0:T(8,128)(2,1)} %bitcast.97), kind=kOutput, calls=%fused_computation.10 | convolution fusion | flops 469876736 | bytes 4833280 | tf_op jit(solution)/shard_map/ryx,kyx->rk/dot_general | solution.py:51
  4.4 0.7 pad.8
  5.1 11.8 %all-to-all-start = ((bf16[16,32,128]{2,1,0:T(8,128)(2,1)}), bf16[16,32,128]{2,1,0:T(8,128)(2,1)S(1)}, u32[]{:S(2)}, u32[]{:S(2)}) async-start(bf16[16,32,128]{2,1,0:T(8,128)(2,1)} %pad.8), calls=%async_computation | async-start | bytes 262144 | tf_op jit(solution)/shard_map/all_to_all | solution.py:57
  17.4 7.2 %collective-permute-start = (bf16[128,5,128]{0,2,1:T(8,128)(2,1)S(1)}, bf16[128,5,128]{0,2,1:T(8,128)(2,1)S(1)}, u32[]{:S(2)}, u32[]{:S(2)}) collective-permute-start(bf16[128,5,128]{0,2,1:T(8,128)(2,1)S(1)} %pad_maximum_fusion.4), channel_id=1, source_target_pairs={{0,1},{1,0},{2,3},{3,2},{4,5},{5,4},{6,7},{7,6},{8,9},{9,8},{10,11... | collective-permute-start | bytes 491528 | tf_op jit(solution)/shard_map/ppermute | solution.py:49
  25.1 6.7 %collective-permute-done = bf16[128,5,128]{0,2,1:T(8,128)(2,1)S(1)} collective-permute-done((bf16[128,5,128]{0,2,1:T(8,128)(2,1)S(1)}, bf16[128,5,128]{0,2,1:T(8,128)(2,1)S(1)}, u32[]{:S(2)}, u32[]{:S(2)}) %collective-permute-start) | collective-permute-done | bytes 163872 | tf_op jit(solution)/shard_map/ppermute | solution.py:49
  32.2 0.7 pad_maximum_fusion.1
  32.9 7.5 %all-to-all-start.1 = ((bf16[16,80,128]{2,1,0:T(8,128)(2,1)}), bf16[16,80,128]{2,1,0:T(8,128)(2,1)S(1)}, u32[]{:S(2)}, u32[]{:S(2)}) async-start(bf16[16,80,128]{2,1,0:T(8,128)(2,1)} %pad_maximum_fusion.1), calls=%async_computation.1 | async-start | bytes 655360 | tf_op jit(solution)/shard_map/all_to_all | solution.py:71
  41.1 11.9 %all-to-all-done.1 = bf16[16,80,128]{2,1,0:T(8,128)(2,1)S(1)} async-done(((bf16[16,80,128]{2,1,0:T(8,128)(2,1)}), bf16[16,80,128]{2,1,0:T(8,128)(2,1)S(1)}, u32[]{:S(2)}, u32[]{:S(2)}) %all-to-all-start.1) | async-done | bytes 327712 | tf_op jit(solution)/shard_map/all_to_all | solution.py:71
  53.2 0.3 fusion.28
  53.5 3.6 %multiply_convert_fusion = bf16[128,32,128]{2,0,1:T(8,128)(2,1)S(1)} fusion(bf16[448,128,1]{1,0,2:T(8,128)(2,1)S(1)} %bitcast.96, bf16[448,32,128]{2,1,0:T(8,128)(2,1)} %bitcast.86), kind=kOutput, calls=%fused_computation.4 | convolution fusion | flops 470810624 | bytes 4833280 | tf_op jit(solution)/shard_map/rk,ryx->ykx/dot_general | solution.py:81
  57.2 18.2 %all_to_all.25 = bf16[4,1080,128]{2,1,0:T(8,128)(2,1)S(1)} all-to-all(bf16[4,1080,128]{2,1,0:T(8,128)(2,1)S(1)} %pad_maximum_fusion), channel_id=1, replica_groups={{0,16,32,48},{2,18,34,50},{4,20,36,52},{6,22,38,54},{8,24,40,56},{10,26..., dimensions={0} | all-to-all | bytes 2211840 | tf_op jit(solution)/shard_map/all_to_all | solution.py:88
  75.4 0.3 reduce_sum.66
  75.8 0.7 pad_maximum_fusion.2
  76.5 6.8 %all-to-all-start.3 = ((bf16[8,160,128]{2,1,0:T(8,128)(2,1)}), bf16[8,160,128]{2,1,0:T(8,128)(2,1)S(1)}, u32[]{:S(2)}, u32[]{:S(2)}) async-start(bf16[8,160,128]{2,1,0:T(8,128)(2,1)} %pad_maximum_fusion.2), calls=%async_computation.3 | async-start | bytes 655360 | tf_op jit(solution)/shard_map/all_to_all | solution.py:99
  83.3 10.1 %all-to-all-done.3 = bf16[8,160,128]{2,1,0:T(8,128)(2,1)S(1)} async-done(((bf16[8,160,128]{2,1,0:T(8,128)(2,1)}), bf16[8,160,128]{2,1,0:T(8,128)(2,1)S(1)}, u32[]{:S(2)}, u32[]{:S(2)}) %all-to-all-start.3) | async-done | bytes 327712 | tf_op jit(solution)/shard_map/all_to_all | solution.py:99
  93.5 0.7 broadcast_in_dim.17
  94.2 8.3 %all-to-all-start.4 = ((bf16[16,56,128]{2,1,0:T(8,128)(2,1)}), bf16[16,56,128]{2,1,0:T(8,128)(2,1)S(1)}, u32[]{:S(2)}, u32[]{:S(2)}) async-start(bf16[16,56,128]{2,1,0:T(8,128)(2,1)} %broadcast_in_dim.17), calls=%async_computation.4 | async-start | bytes 458752 | tf_op jit(solution)/shard_map/all_to_all | solution.py:104
  102.7 7.2 %collective-permute-start.1 = (bf16[128,128]{0,1:T(8,128)(2,1)S(1)}, bf16[128,128]{0,1:T(8,128)(2,1)S(1)}, u32[]{:S(2)}, u32[]{:S(2)}) collective-permute-start(bf16[128,128]{0,1:T(8,128)(2,1)S(1)} %copy.79), channel_id=1, source_target_pairs={{0,1},{1,0},{2,3},{3,2},{4,5},{5,4},{6,7},{7,6},{8,9},{9,8},{10,11... | collective-permute-start | bytes 98312 | tf_op jit(solution)/shard_map/ppermute | solution.py:102
  109.9 3.6 %all-to-all-done.4 = bf16[16,56,128]{2,1,0:T(8,128)(2,1)S(1)} async-done(((bf16[16,56,128]{2,1,0:T(8,128)(2,1)}), bf16[16,56,128]{2,1,0:T(8,128)(2,1)S(1)}, u32[]{:S(2)}, u32[]{:S(2)}) %all-to-all-start.4) | async-done | bytes 229408 | tf_op jit(solution)/shard_map/all_to_all | solution.py:104
  113.7 0.4 fusion.26
  114.1 0.4 fusion.25
  114.5 0.4 convolution_add_fusion.1
  115.0 0.4 fusion.91
  115.5 0.4 fusion.6
  115.9 0.3 fusion.29
  117.1 1.3 collective-permute-start.5
  118.4 4.0 %collective-permute-start.4 = (bf16[128,128]{0,1:T(8,128)(2,1)S(1)}, bf16[128,128]{0,1:T(8,128)(2,1)S(1)}, u32[]{:S(2)}, u32[]{:S(2)}) collective-permute-start(bf16[128,128]{0,1:T(8,128)(2,1)S(1)} %get-tuple-element.30), channel_id=1, source_target_pairs={{0,2},{2,4},{4,6},{6,8},{8,10},{10,12},{12,14},{14,16},{16,18},{18... | collective-permute-start | bytes 98312 | tf_op jit(solution)/shard_map/ppermute | solution.py:142
  122.4 3.8 %collective-permute-start.3 = (bf16[128,128]{0,1:T(8,128)(2,1)S(1)}, bf16[128,128]{0,1:T(8,128)(2,1)S(1)}, u32[]{:S(2)}, u32[]{:S(2)}) collective-permute-start(bf16[128,128]{0,1:T(8,128)(2,1)S(1)} %get-tuple-element.30), channel_id=1, source_target_pairs={{64,0},{128,64},{192,128},{256,192},{320,256},{384,320},{448,384},... | collective-permute-start | bytes 98312 | tf_op jit(solution)/shard_map/ppermute | solution.py:143
  126.2 2.5 %collective-permute-start.2 = (bf16[128,128]{0,1:T(8,128)(2,1)S(1)}, bf16[128,128]{0,1:T(8,128)(2,1)S(1)}, u32[]{:S(2)}, u32[]{:S(2)}) collective-permute-start(bf16[128,128]{0,1:T(8,128)(2,1)S(1)} %get-tuple-element.30), channel_id=1, source_target_pairs={{0,64},{64,128},{128,192},{192,256},{256,320},{320,384},{384,448},... | collective-permute-start | bytes 98312 | tf_op jit(solution)/shard_map/ppermute | solution.py:142
  128.6 1.1 fusion.27
  129.7 0.7 copy.75
  130.5 0.7 copy.74
  (58 shorter events, 3.0 us)
Async XLA Ops:
  0.6 16.3 %copy-start = (bf16[128,1,32,128]{3,2,1,0:T(8,128)(2,1)S(1)}, bf16[128,1,32,128]{3,2,1,0:T(8,128)(2,1)}, u32[]{:S(2)}) copy-start(bf16[128,1,32,128]{3,2,1,0:T(8,128)(2,1)} %param.6) | copy-start | bytes 3145732
  5.1 27.0 %all-to-all-start = ((bf16[16,32,128]{2,1,0:T(8,128)(2,1)}), bf16[16,32,128]{2,1,0:T(8,128)(2,1)S(1)}, u32[]{:S(2)}, u32[]{:S(2)}) async-start(bf16[16,32,128]{2,1,0:T(8,128)(2,1)} %pad.8), calls=%async_computation | async-start | bytes 262144 | tf_op jit(solution)/shard_map/all_to_all | solution.py:57
  17.4 14.4 %collective-permute-start = (bf16[128,5,128]{0,2,1:T(8,128)(2,1)S(1)}, bf16[128,5,128]{0,2,1:T(8,128)(2,1)S(1)}, u32[]{:S(2)}, u32[]{:S(2)}) collective-permute-start(bf16[128,5,128]{0,2,1:T(8,128)(2,1)S(1)} %pad_maximum_fusion.4), channel_id=1, source_target_pairs={{0,1},{1,0},{2,3},{3,2},{4,5},{5,4},{6,7},{7,6},{8,9},{9,8},{10,11... | collective-permute-start | bytes 491528 | tf_op jit(solution)/shard_map/ppermute | solution.py:49
  32.9 20.0 %all-to-all-start.1 = ((bf16[16,80,128]{2,1,0:T(8,128)(2,1)}), bf16[16,80,128]{2,1,0:T(8,128)(2,1)S(1)}, u32[]{:S(2)}, u32[]{:S(2)}) async-start(bf16[16,80,128]{2,1,0:T(8,128)(2,1)} %pad_maximum_fusion.1), calls=%async_computation.1 | async-start | bytes 655360 | tf_op jit(solution)/shard_map/all_to_all | solution.py:71
  75.4 27.1 %copy-start.3 = (f32[128,1,1,128]{3,2,1,0:T(1,128)S(1)}, f32[128,1,1,128]{3,2,1,0:T(1,128)}, u32[]{:S(2)}) copy-start(f32[128,1,1,128]{3,2,1,0:T(1,128)} %param.8) | copy-start | bytes 196612
  76.5 16.9 %all-to-all-start.3 = ((bf16[8,160,128]{2,1,0:T(8,128)(2,1)}), bf16[8,160,128]{2,1,0:T(8,128)(2,1)S(1)}, u32[]{:S(2)}, u32[]{:S(2)}) async-start(bf16[8,160,128]{2,1,0:T(8,128)(2,1)} %pad_maximum_fusion.2), calls=%async_computation.3 | async-start | bytes 655360 | tf_op jit(solution)/shard_map/all_to_all | solution.py:99
  94.2 19.3 %all-to-all-start.4 = ((bf16[16,56,128]{2,1,0:T(8,128)(2,1)}), bf16[16,56,128]{2,1,0:T(8,128)(2,1)S(1)}, u32[]{:S(2)}, u32[]{:S(2)}) async-start(bf16[16,56,128]{2,1,0:T(8,128)(2,1)} %broadcast_in_dim.17), calls=%async_computation.4 | async-start | bytes 458752 | tf_op jit(solution)/shard_map/all_to_all | solution.py:104
  102.7 13.9 %collective-permute-start.1 = (bf16[128,128]{0,1:T(8,128)(2,1)S(1)}, bf16[128,128]{0,1:T(8,128)(2,1)S(1)}, u32[]{:S(2)}, u32[]{:S(2)}) collective-permute-start(bf16[128,128]{0,1:T(8,128)(2,1)S(1)} %copy.79), channel_id=1, source_target_pairs={{0,1},{1,0},{2,3},{3,2},{4,5},{5,4},{6,7},{7,6},{8,9},{9,8},{10,11... | collective-permute-start | bytes 98312 | tf_op jit(solution)/shard_map/ppermute | solution.py:102
  114.1 2.1 %copy-start.2 = (f32[128,256]{1,0:T(8,128)S(1)}, f32[128,256]{1,0:T(8,128)}, u32[]{:S(2)}) copy-start(f32[128,256]{1,0:T(8,128)} %param.7) | copy-start | bytes 393220
  116.5 14.7 %copy-start.1 = (f32[128,256]{1,0:T(8,128)}, f32[128,256]{1,0:T(8,128)S(1)}, u32[]{:S(2)}) copy-start(f32[128,256]{1,0:T(8,128)S(1)} %convolution_add_fusion.2) | copy-start | bytes 393220
  117.1 13.3 %collective-permute-start.5 = (bf16[128,128]{0,1:T(8,128)(2,1)S(1)}, bf16[128,128]{0,1:T(8,128)(2,1)S(1)}, u32[]{:S(2)}, u32[]{:S(2)}) collective-permute-start(bf16[128,128]{0,1:T(8,128)(2,1)S(1)} %get-tuple-element.30), channel_id=1, source_target_pairs={{2,0},{4,2},{6,4},{8,6},{10,8},{12,10},{14,12},{16,14},{18,16},{20... | collective-permute-start | bytes 98312 | tf_op jit(solution)/shard_map/ppermute | solution.py:143
  118.4 12.0 %collective-permute-start.4 = (bf16[128,128]{0,1:T(8,128)(2,1)S(1)}, bf16[128,128]{0,1:T(8,128)(2,1)S(1)}, u32[]{:S(2)}, u32[]{:S(2)}) collective-permute-start(bf16[128,128]{0,1:T(8,128)(2,1)S(1)} %get-tuple-element.30), channel_id=1, source_target_pairs={{0,2},{2,4},{4,6},{6,8},{8,10},{10,12},{12,14},{14,16},{16,18},{18... | collective-permute-start | bytes 98312 | tf_op jit(solution)/shard_map/ppermute | solution.py:142
  122.4 8.0 %collective-permute-start.3 = (bf16[128,128]{0,1:T(8,128)(2,1)S(1)}, bf16[128,128]{0,1:T(8,128)(2,1)S(1)}, u32[]{:S(2)}, u32[]{:S(2)}) collective-permute-start(bf16[128,128]{0,1:T(8,128)(2,1)S(1)} %get-tuple-element.30), channel_id=1, source_target_pairs={{64,0},{128,64},{192,128},{256,192},{320,256},{384,320},{448,384},... | collective-permute-start | bytes 98312 | tf_op jit(solution)/shard_map/ppermute | solution.py:143
  126.2 4.3 %collective-permute-start.2 = (bf16[128,128]{0,1:T(8,128)(2,1)S(1)}, bf16[128,128]{0,1:T(8,128)(2,1)S(1)}, u32[]{:S(2)}, u32[]{:S(2)}) collective-permute-start(bf16[128,128]{0,1:T(8,128)(2,1)S(1)} %get-tuple-element.30), channel_id=1, source_target_pairs={{0,64},{64,128},{128,192},{192,256},{256,320},{320,384},{384,448},... | collective-permute-start | bytes 98312 | tf_op jit(solution)/shard_map/ppermute | solution.py:142

commit v6 on v5

--- a/solution.py
+++ b/solution.py
@@ -15,7 +15,7 @@
 
 
 def power_sum(gram):
-    dot = lambda a, b: jnp.dot(a, b, precision=lax.Precision.HIGHEST)
+    dot = lambda a, b: jnp.dot(a, b, precision=lax.Precision.HIGH)
     eye = jnp.eye(COMPONENTS, dtype=WIDE)
     first = 0.98 * eye - 0.1 * gram
     second = dot(first, first)
@@ -27,7 +27,7 @@
 
 
 def on_device(scans, maps, gram_old, stats_old, kept):
-    highest = lax.Precision.HIGHEST
+    fine = lax.Precision.HIGH
     slabs = lax.axis_size("slab")
     subjects = lax.axis_size("subj")
     volumes = scans.shape[0]
@@ -35,7 +35,6 @@
     voxel_total = slabs * lines * width
     total_rows = volumes * subjects
     slab, subj, comp = lax.axis_index("slab"), lax.axis_index("subj"), lax.axis_index("comp")
-    at_x = subj // Y_SIZE
     ring = slabs * 2
     ring_axes = ("slab", "comp")
     x_groups = [[x * Y_SIZE + y for x in range(X_SIZE)] for y in range(Y_SIZE)]
@@ -43,38 +42,29 @@
 
     scans3 = scans.reshape(volumes, lines, width)
     maps3 = maps.reshape(own_count, lines, width)
-    part = lines // (2 * X_SIZE)
-    own_line = lax.dynamic_slice_in_dim(maps3, subj, 1, 1)
-    to_partner = lax.dynamic_slice_in_dim(maps3, (2 * at_x + 1 - comp) * part, part, 1)
-    got = lax.ppermute(jnp.concatenate([to_partner, own_line], axis=1), "comp", SWAP)
-
+    own_piece = lax.dynamic_slice_in_dim(maps3, subj, 1, 1).reshape(own_count, width)
     proj_part = jnp.einsum("ryx,kyx->rk", scans3, maps3, preferred_element_type=WIDE)
     proj_part = (proj_part * (1.0 / math.sqrt(voxel_total))).astype(LOW)
+
     rows = 32
     pieces = volumes // rows
     few = own_count // ring
     sent = jnp.pad(proj_part.reshape(pieces, rows, own_count), ((0, ring - pieces), (0, 0), (0, 0)))
+    sent = jnp.concatenate([sent, own_piece.T.reshape(ring, few, own_count)], axis=1)
     taken = lax.all_to_all(sent, ring_axes, 0, 0)
-    proj_rows = taken.reshape(slabs, 2, rows, own_count).astype(WIDE).sum(0).astype(LOW)
-
-    own_lines = lax.dynamic_slice_in_dim(maps3, at_x * 2 * part, 2 * part, 1)
-    own_half = lax.dynamic_slice_in_dim(maps3, (2 * at_x + comp) * part, part, 1)
-    gram_own = jnp.einsum("ayx,byx->ab", own_lines, own_lines, preferred_element_type=WIDE)
-    first = jnp.where(comp == 0, own_half, got[:, :part])
-    second = jnp.where(comp == 0, got[:, :part], own_half)
-    gram_cross = jnp.einsum("ayx,byx->ab", first, second, preferred_element_type=WIDE)
-    gram_parts = jnp.concatenate(
-        [gram_own.reshape(ring, few, own_count), gram_cross.reshape(ring, few, own_count)], axis=1
-    )
-    gram_parts = (gram_parts * (1.0 / voxel_total)).astype(LOW)
+    proj_rows = taken[:, :rows].reshape(slabs, 2, rows, own_count).astype(WIDE).sum(0).astype(LOW)
+    voxels = taken[:, rows:].reshape(slabs, 2, few, own_count)
+    low_part, high_part = [voxels[:, i].reshape(slabs * few, own_count) for i in range(2)]
+    gram_parts = [
+        jnp.dot(one.T, two, preferred_element_type=WIDE).reshape(ring, few, own_count)
+        for one, two in ((low_part, low_part), (high_part, high_part), (low_part, high_part))
+    ]
+    gram_parts = (jnp.concatenate(gram_parts, axis=1) * (1.0 / voxel_total)).astype(LOW)
     proj_rows = jnp.broadcast_to(proj_rows.reshape(2 * rows, own_count), (ring, 2 * rows, own_count))
     back = lax.all_to_all(jnp.concatenate([proj_rows, gram_parts], axis=1), ring_axes, 0, 0)
     proj_pair = [back[:pieces, i * rows : (i + 1) * rows].reshape(volumes, own_count) for i in range(2)]
     proj = jnp.concatenate(proj_pair, axis=1)
-    gram_rows = back[:, 2 * rows :].astype(WIDE).reshape(slabs, 2, 2 * few, own_count).sum(0)
-    gram_rows = jnp.concatenate(
-        [gram_rows[:, :few].reshape(2 * few, own_count), gram_rows[:, few:].sum(0)], axis=0
-    ).astype(LOW)
+    gram_rows = back[:, 2 * rows :].astype(WIDE).sum(0).astype(LOW)
 
     live = (lax.iota(jnp.int32, volumes) < kept[0]).astype(LOW)
     live_proj = jnp.where(comp == 0, proj_pair[0], proj_pair[1]) * live[:, None]
@@ -87,8 +77,7 @@
     sent = jnp.concatenate([term, jnp.broadcast_to(mine, (X_SIZE,) + mine.shape)], axis=1)
     taken = lax.all_to_all(sent, "subj", 0, 0, axis_index_groups=x_groups).astype(WIDE).sum(0).astype(LOW)
     split = Y_SIZE * own_count
-    gram_rows = taken[split + 2 * share :]
-    mine = taken[split : split + 2 * share]
+    mine = taken[split:]
     sent = jnp.concatenate(
         [
             taken[:split].reshape(Y_SIZE, own_count, width),
@@ -99,8 +88,9 @@
     summed = lax.all_to_all(sent, "subj", 0, 0, axis_index_groups=y_groups)
     summed = summed.astype(WIDE).sum(0).astype(LOW)
     own_stats = summed[:own_count]
-    other_stats = lax.ppermute(own_stats, "comp", SWAP)
-    mine = jnp.concatenate([summed[own_count:], gram_rows], axis=0)
+    other = lax.ppermute(jnp.concatenate([own_stats, own_piece], axis=0), "comp", SWAP)
+    other_stats, other_piece = other[:own_count], other[own_count:]
+    mine = summed[own_count:]
     shared = lax.all_to_all(jnp.broadcast_to(mine, (ring,) + mine.shape), ring_axes, 0, 0)
 
     gram_at = 2 * share
@@ -114,17 +104,15 @@
     own_coding = lax.dynamic_slice_in_dim(coding, comp * own_count, own_count, 1)
     product = jnp.transpose(shared[:, :gram_at].reshape(slabs, 2, 2, share, own_count), (1, 0, 3, 2, 4))
     product = product.reshape(COMPONENTS, COMPONENTS).astype(WIDE)
-    product = jnp.dot(jnp.dot(own_coding.T, product, precision=highest), coding, precision=highest)
-    codes = jnp.dot(proj.astype(WIDE), own_coding, precision=highest)
+    product = jnp.dot(jnp.dot(own_coding.T, product, precision=fine), coding, precision=fine)
+    codes = jnp.dot(proj.astype(WIDE), own_coding, precision=fine)
     both_stats = jnp.where(
         comp == 0,
         jnp.concatenate([own_stats, other_stats], axis=0),
         jnp.concatenate([other_stats, own_stats], axis=0),
     ).astype(WIDE)
-    stats_line = 0.5 * stats_old.reshape(own_count, width) + jnp.dot(own_coding.T, both_stats, precision=highest)
+    stats_line = 0.5 * stats_old.reshape(own_count, width) + jnp.dot(own_coding.T, both_stats, precision=fine)
     gram_new = 0.5 * gram_old + product
-    own_piece = own_line.reshape(own_count, width)
-    other_piece = got[:, part]
     piece = jnp.where(
         comp == 0,
         jnp.concatenate([own_piece, other_piece], axis=0),
@@ -132,7 +120,7 @@
     ).astype(WIDE)
     block = lax.dynamic_slice_in_dim(gram_new, comp * own_count, own_count, 1)
     diag = jnp.sum(block * jnp.eye(own_count, dtype=WIDE), axis=1, keepdims=True)
-    coupled = jnp.dot(gram_new, piece, precision=highest)
+    coupled = jnp.dot(gram_new, piece, precision=fine)
     updated = own_piece.astype(WIDE) + (stats_line - coupled) / diag
     edge = updated.astype(LOW)
     sides = []

time: 132 us -> 126 us (0.955)
  blocking collectives: 18.2 us -> 57.2 us
  starting transfers between devices: 60.3 us -> 28.1 us
  waiting for transfers between devices: 32.3 us -> 20.8 us
    all_to_all x0 -> x2, blocking collectives: none -> 39 us  [the longest x1 21.2 us: on_device(): taken = lax.all_to_all(sent, ring_axes, 0, 0)]
    all_to_all x2 -> x0, starting transfers between devices: 18.6 us -> none  [the longest x1 11.8 us: on_device(): taken = lax.all_to_all(sent, ring_axes, 0, 0)]
    all_to_all x2 -> x0, waiting for transfers between devices: 10.1 us -> none  [the longest x1 10.1 us: on_device(): summed = lax.all_to_all(sent, 'subj', 0, 0, axis_index_groups=y_groups)]
    ppermute x2 -> x1, starting transfers between devices: 14.4 us -> 7.2 us  [on_device(): lax.ppermute(jnp.concatenate([own_stats, own_piece], axis=0), 'comp', SWAP)]
    all_to_all x1, waiting for transfers between devices: 3.61 us -> 0.01 us  [on_device(): lax.all_to_all(jnp.broadcast_to(mine, (ring,) + mine.shape), ring_axes, 0...]
    all_to_all x1, starting transfers between devices: 7.49 us -> 4.15 us  [on_device(): lax.all_to_all(jnp.concatenate([proj_rows, gram_parts], axis=1), ring_axe...]
    ppermute x2, starting transfers between devices: 5.07 us -> 3.21 us  [on_device(): sides.append(lax.ppermute(edge, axis, [(b, a) for a, b in up]) + 0.0)]
    ppermute x2, waiting for transfers between devices: 0.01 us -> 1.71 us  [on_device(): sides.append(lax.ppermute(edge, axis, [(b, a) for a, b in up]) + 0.0)]
  transfers between devices with their start and end apart: 10 -> 7, of which waited for: 4 -> 3; matrix products, arithmetic and copies ran while one was open for 5% -> 2% of each run, Pallas kernels for 0% -> 0%
where the time goes in v6:
time: 126 us; the launch traced here: 125 us
  blocking collectives  57.2 us (45%)
  starting transfers between devices  28.1 us (22%)
  waiting for transfers between devices  20.8 us (17%)
  matrix products  11 us (9%)
  local copies, waits for them, and re-layouts  4.4 us (3%)
  between operations  1.7 us (1%)
  other arithmetic  1.63 us (1%)
    all_to_all x1, blocking collectives, on_device(): taken = lax.all_to_all(sent, ring_axes, 0, 0)  21.2 us
    all_to_all x1, blocking collectives, on_device(): lax.all_to_all(sent, 'subj', 0, 0, axis_index_groups=x_groups).astype(WIDE)  18.2 us
    all_to_all x1, blocking collectives, on_device(): summed = lax.all_to_all(sent, 'subj', 0, 0, axis_index_groups=y_groups)  17.8 us
    all_to_all x1, waiting for transfers between devices, on_device(): lax.all_to_all(jnp.concatenate([proj_rows, gram_parts], axis=1), ring_axe...  12.4 us
    all_to_all x1, starting transfers between devices, on_device(): lax.all_to_all(jnp.broadcast_to(mine, (ring,) + mine.shape), ring_axes, 0...  8.55 us
    ppermute x1, starting transfers between devices, on_device(): lax.ppermute(jnp.concatenate([own_stats, own_piece], axis=0), 'comp', SWAP)  7.2 us
    ppermute x1, waiting for transfers between devices, on_device(): lax.ppermute(jnp.concatenate([own_stats, own_piece], axis=0), 'comp', SWAP)  6.67 us
    ppermute x2, starting transfers between devices, on_device(): sides.append(lax.ppermute(edge, axis, up) + 0.0)  4.99 us
  transfers between devices with their start and end apart: 7, of which 3 were waited for; matrix products, arithmetic and copies ran while one was open for 2% of the time, Pallas kernels for 0%

profile of v6, /device:TPU:1, one launch (start us, length us, event | category | flops | bytes accessed | tf_op | source)
XLA Modules:
  0.0 124.9 jit_solution(6349239559703255354)
XLA Ops:
  0.7 1.2 copy-done
  2.1 3.4 %fusion.13 = bf16[448,128]{1,0:T(8,128)(2,1)S(1)} fusion(bf16[448,32,128]{2,1,0:T(8,128)(2,1)} %bitcast.92, bf16[128,32,128]{2,1,0:T(8,128)(2,1)S(1)} %bitcast.90), kind=kOutput, calls=%fused_computation.10 | convolution fusion | flops 469876736 | bytes 4833280 | tf_op jit(solution)/shard_map/ryx,kyx->rk/dot_general | solution.py:46
  5.5 21.2 %all_to_all.25 = bf16[16,40,128]{2,1,0:T(8,128)(2,1)S(1)} all-to-all(bf16[16,40,128]{2,1,0:T(8,128)(2,1)S(1)} %fusion.26), channel_id=1, replica_groups=mesh['slab'=8,'subj'=32,'comp'=2] {'slab','comp'}, dimensions={0} | all-to-all | bytes 327680 | tf_op jit(solution)/shard_map/all_to_all | solution.py:54
  27.5 0.8 pad_maximum_fusion.2
  28.3 4.1 %all-to-all-start.1 = ((bf16[16,88,128]{2,1,0:T(8,128)(2,1)}), bf16[16,88,128]{2,1,0:T(8,128)(2,1)S(1)}, u32[]{:S(2)}, u32[]{:S(2)}) async-start(bf16[16,88,128]{2,1,0:T(8,128)(2,1)} %pad_maximum_fusion.2), calls=%async_computation.1 | async-start | bytes 720896 | tf_op jit(solution)/shard_map/all_to_all | solution.py:64
  33.1 12.4 %all-to-all-done.1 = bf16[16,88,128]{2,1,0:T(8,128)(2,1)S(1)} async-done(((bf16[16,88,128]{2,1,0:T(8,128)(2,1)}), bf16[16,88,128]{2,1,0:T(8,128)(2,1)S(1)}, u32[]{:S(2)}, u32[]{:S(2)}) %all-to-all-start.1) | async-done | bytes 360480 | tf_op jit(solution)/shard_map/all_to_all | solution.py:64
  45.7 0.3 fusion.28
  46.0 3.6 %multiply_convert_fusion = bf16[128,32,128]{2,0,1:T(8,128)(2,1)S(1)} fusion(bf16[448,128,1]{1,0,2:T(8,128)(2,1)S(1)} %bitcast.102, bf16[448,32,128]{2,1,0:T(8,128)(2,1)} %bitcast.93), kind=kOutput, calls=%fused_computation.4 | convolution fusion | flops 470810624 | bytes 4833280 | tf_op jit(solution)/shard_map/rk,ryx->ykx/dot_general | solution.py:71
  49.8 18.2 %all_to_all.26 = bf16[4,1080,128]{2,1,0:T(8,128)(2,1)S(1)} all-to-all(bf16[4,1080,128]{2,1,0:T(8,128)(2,1)S(1)} %pad_maximum_fusion), channel_id=1, replica_groups={{0,16,32,48},{2,18,34,50},{4,20,36,52},{6,22,38,54},{8,24,40,56},{10,26..., dimensions={0} | all-to-all | bytes 2211840 | tf_op jit(solution)/shard_map/all_to_all | solution.py:78
  67.9 0.3 reduce_sum.59
  68.3 17.8 %all_to_all.27 = bf16[8,184,128]{2,1,0:T(8,128)(2,1)S(1)} all-to-all(bf16[8,184,128]{2,1,0:T(8,128)(2,1)S(1)} %pad_maximum_fusion.1), channel_id=1, replica_groups={{0,2,4,6,8,10,12,14},{16,18,20,22,24,26,28,30},{32,34,36,38,40,42,44,46..., dimensions={0} | all-to-all | bytes 753664 | tf_op jit(solution)/shard_map/all_to_all | solution.py:88
  86.2 0.7 broadcast_in_dim.17
  86.9 8.6 %all-to-all-start.4 = ((bf16[16,56,128]{2,1,0:T(8,128)(2,1)}), bf16[16,56,128]{2,1,0:T(8,128)(2,1)S(1)}, u32[]{:S(2)}, u32[]{:S(2)}) async-start(bf16[16,56,128]{2,1,0:T(8,128)(2,1)} %broadcast_in_dim.17), calls=%async_computation.4 | async-start | bytes 458752 | tf_op jit(solution)/shard_map/all_to_all | solution.py:94
  95.6 7.2 %collective-permute-start = (bf16[256,128]{0,1:T(8,128)(2,1)S(1)}, bf16[256,128]{0,1:T(8,128)(2,1)S(1)}, u32[]{:S(2)}, u32[]{:S(2)}) collective-permute-start(bf16[256,128]{0,1:T(8,128)(2,1)S(1)} %pad_maximum_fusion.7), channel_id=1, source_target_pairs={{0,1},{1,0},{2,3},{3,2},{4,5},{5,4},{6,7},{7,6},{8,9},{9,8},{10,11... | collective-permute-start | bytes 196616 | tf_op jit(solution)/shard_map/ppermute | solution.py:91
  102.9 6.7 %collective-permute-done = bf16[256,128]{0,1:T(8,128)(2,1)S(1)} collective-permute-done((bf16[256,128]{0,1:T(8,128)(2,1)S(1)}, bf16[256,128]{0,1:T(8,128)(2,1)S(1)}, u32[]{:S(2)}, u32[]{:S(2)}) %collective-permute-start) | collective-permute-done | bytes 65568 | tf_op jit(solution)/shard_map/ppermute | solution.py:91
  109.7 0.3 fusion.24
  110.0 0.3 fusion.23
  110.4 0.3 convolution_add_fusion.1
  110.7 0.3 fusion.102
  111.1 0.3 fusion.6
  111.4 0.3 fusion.29
  111.6 0.2 convolution_add_fusion.2
  112.0 0.2 convolution_add_fusion.3
  112.2 0.2 fusion.101
  112.4 2.8 %collective-permute-start.1 = (bf16[128,128]{0,1:T(8,128)(2,1)S(1)}, bf16[128,128]{0,1:T(8,128)(2,1)S(1)}, u32[]{:S(2)}, u32[]{:S(2)}) collective-permute-start(bf16[128,128]{0,1:T(8,128)(2,1)S(1)} %get-tuple-element.28), channel_id=1, source_target_pairs={{0,64},{64,128},{128,192},{192,256},{256,320},{320,384},{384,448},... | collective-permute-start | bytes 98312 | tf_op jit(solution)/shard_map/ppermute | solution.py:130
  115.2 1.9 %collective-permute-start.2 = (bf16[128,128]{0,1:T(8,128)(2,1)S(1)}, bf16[128,128]{0,1:T(8,128)(2,1)S(1)}, u32[]{:S(2)}, u32[]{:S(2)}) collective-permute-start(bf16[128,128]{0,1:T(8,128)(2,1)S(1)} %get-tuple-element.28), channel_id=1, source_target_pairs={{64,0},{128,64},{192,128},{256,192},{320,256},{384,320},{448,384},... | collective-permute-start | bytes 98312 | tf_op jit(solution)/shard_map/ppermute | solution.py:131
  117.1 2.2 %collective-permute-start.3 = (bf16[128,128]{0,1:T(8,128)(2,1)S(1)}, bf16[128,128]{0,1:T(8,128)(2,1)S(1)}, u32[]{:S(2)}, u32[]{:S(2)}) collective-permute-start(bf16[128,128]{0,1:T(8,128)(2,1)S(1)} %get-tuple-element.28), channel_id=1, source_target_pairs={{0,2},{2,4},{4,6},{6,8},{8,10},{10,12},{12,14},{14,16},{16,18},{18... | collective-permute-start | bytes 98312 | tf_op jit(solution)/shard_map/ppermute | solution.py:130
  119.4 1.3 %collective-permute-start.4 = (bf16[128,128]{0,1:T(8,128)(2,1)S(1)}, bf16[128,128]{0,1:T(8,128)(2,1)S(1)}, u32[]{:S(2)}, u32[]{:S(2)}) collective-permute-start(bf16[128,128]{0,1:T(8,128)(2,1)S(1)} %get-tuple-element.28), channel_id=1, source_target_pairs={{2,0},{4,2},{6,4},{8,6},{10,8},{12,10},{14,12},{16,14},{18,16},{20... | collective-permute-start | bytes 98312 | tf_op jit(solution)/shard_map/ppermute | solution.py:131
  120.7 1.0 fusion.27
  121.6 0.7 copy.52
  122.4 1.7 %collective-permute-done.4 = bf16[128,128]{0,1:T(8,128)(2,1)S(1)} collective-permute-done((bf16[128,128]{0,1:T(8,128)(2,1)S(1)}, bf16[128,128]{0,1:T(8,128)(2,1)S(1)}, u32[]{:S(2)}, u32[]{:S(2)}) %collective-permute-start.4) | collective-permute-done | bytes 32800 | tf_op jit(solution)/shard_map/ppermute | solution.py:131
  124.1 0.7 copy.51
  (51 shorter events, 2.0 us)
Async XLA Ops:
  0.6 1.2 copy-start
  28.3 17.3 %all-to-all-start.1 = ((bf16[16,88,128]{2,1,0:T(8,128)(2,1)}), bf16[16,88,128]{2,1,0:T(8,128)(2,1)S(1)}, u32[]{:S(2)}, u32[]{:S(2)}) async-start(bf16[16,88,128]{2,1,0:T(8,128)(2,1)} %pad_maximum_fusion.2), calls=%async_computation.1 | async-start | bytes 720896 | tf_op jit(solution)/shard_map/all_to_all | solution.py:64
  67.9 34.9 %copy-start.3 = (f32[128,1,1,128]{3,2,1,0:T(1,128)S(1)}, f32[128,1,1,128]{3,2,1,0:T(1,128)}, u32[]{:S(2)}) copy-start(f32[128,1,1,128]{3,2,1,0:T(1,128)} %param.8) | copy-start | bytes 196612
  86.9 22.7 %all-to-all-start.4 = ((bf16[16,56,128]{2,1,0:T(8,128)(2,1)}), bf16[16,56,128]{2,1,0:T(8,128)(2,1)S(1)}, u32[]{:S(2)}, u32[]{:S(2)}) async-start(bf16[16,56,128]{2,1,0:T(8,128)(2,1)} %broadcast_in_dim.17), calls=%async_computation.4 | async-start | bytes 458752 | tf_op jit(solution)/shard_map/all_to_all | solution.py:94
  95.6 14.0 %collective-permute-start = (bf16[256,128]{0,1:T(8,128)(2,1)S(1)}, bf16[256,128]{0,1:T(8,128)(2,1)S(1)}, u32[]{:S(2)}, u32[]{:S(2)}) collective-permute-start(bf16[256,128]{0,1:T(8,128)(2,1)S(1)} %pad_maximum_fusion.7), channel_id=1, source_target_pairs={{0,1},{1,0},{2,3},{3,2},{4,5},{5,4},{6,7},{7,6},{8,9},{9,8},{10,11... | collective-permute-start | bytes 196616 | tf_op jit(solution)/shard_map/ppermute | solution.py:91
  110.0 1.6 %copy-start.2 = (f32[128,256]{1,0:T(8,128)S(1)}, f32[128,256]{1,0:T(8,128)}, u32[]{:S(2)}) copy-start(f32[128,256]{1,0:T(8,128)} %param.7) | copy-start | bytes 393220
  111.9 13.0 %copy-start.1 = (f32[128,256]{1,0:T(8,128)}, f32[128,256]{1,0:T(8,128)S(1)}, u32[]{:S(2)}) copy-start(f32[128,256]{1,0:T(8,128)S(1)} %convolution_add_fusion.2) | copy-start | bytes 393220
  112.4 10.0 %collective-permute-start.1 = (bf16[128,128]{0,1:T(8,128)(2,1)S(1)}, bf16[128,128]{0,1:T(8,128)(2,1)S(1)}, u32[]{:S(2)}, u32[]{:S(2)}) collective-permute-start(bf16[128,128]{0,1:T(8,128)(2,1)S(1)} %get-tuple-element.28), channel_id=1, source_target_pairs={{0,64},{64,128},{128,192},{192,256},{256,320},{320,384},{384,448},... | collective-permute-start | bytes 98312 | tf_op jit(solution)/shard_map/ppermute | solution.py:130
  115.2 7.2 %collective-permute-start.2 = (bf16[128,128]{0,1:T(8,128)(2,1)S(1)}, bf16[128,128]{0,1:T(8,128)(2,1)S(1)}, u32[]{:S(2)}, u32[]{:S(2)}) collective-permute-start(bf16[128,128]{0,1:T(8,128)(2,1)S(1)} %get-tuple-element.28), channel_id=1, source_target_pairs={{64,0},{128,64},{192,128},{256,192},{320,256},{384,320},{448,384},... | collective-permute-start | bytes 98312 | tf_op jit(solution)/shard_map/ppermute | solution.py:131
  117.1 5.2 %collective-permute-start.3 = (bf16[128,128]{0,1:T(8,128)(2,1)S(1)}, bf16[128,128]{0,1:T(8,128)(2,1)S(1)}, u32[]{:S(2)}, u32[]{:S(2)}) collective-permute-start(bf16[128,128]{0,1:T(8,128)(2,1)S(1)} %get-tuple-element.28), channel_id=1, source_target_pairs={{0,2},{2,4},{4,6},{6,8},{8,10},{10,12},{12,14},{14,16},{16,18},{18... | collective-permute-start | bytes 98312 | tf_op jit(solution)/shard_map/ppermute | solution.py:130
  119.4 4.7 %collective-permute-start.4 = (bf16[128,128]{0,1:T(8,128)(2,1)S(1)}, bf16[128,128]{0,1:T(8,128)(2,1)S(1)}, u32[]{:S(2)}, u32[]{:S(2)}) collective-permute-start(bf16[128,128]{0,1:T(8,128)(2,1)S(1)} %get-tuple-element.28), channel_id=1, source_target_pairs={{2,0},{4,2},{6,4},{8,6},{10,8},{12,10},{14,12},{16,14},{18,16},{20... | collective-permute-start | bytes 98312 | tf_op jit(solution)/shard_map/ppermute | solution.py:131

commit v7 on v6

--- a/solution.py
+++ b/solution.py
@@ -3,6 +3,8 @@
 import jax
 import jax.numpy as jnp
 from jax import lax
+from jax.experimental import pallas as pl
+from jax.experimental.pallas import tpu as pltpu
 from jax.sharding import PartitionSpec as P
 
 COMPONENTS = 256
@@ -26,6 +28,23 @@
     return 0.1 * (sum6 + dot(sixth, sum6))
 
 
+def keep_near(array):
+    def copy(source, target, sem):
+        moved = pltpu.make_async_copy(source, target, sem)
+        moved.start()
+        moved.wait()
+
+    return pl.pallas_call(
+        copy,
+        out_shape=pltpu.VMEM(array.shape, array.dtype),
+        in_specs=[pl.BlockSpec(memory_space=pltpu.HBM)],
+        out_specs=pl.BlockSpec(memory_space=pltpu.VMEM),
+        scratch_shapes=[pltpu.SemaphoreType.DMA(())],
+        compiler_params=pltpu.CompilerParams(vmem_limit_bytes=1 << 20),
+        cost_estimate=pl.CostEstimate(flops=0, bytes_accessed=2 * array.size * 2, transcendentals=0),
+    )(array)
+
+
 def on_device(scans, maps, gram_old, stats_old, kept):
     fine = lax.Precision.HIGH
     slabs = lax.axis_size("slab")
@@ -40,7 +59,7 @@
     x_groups = [[x * Y_SIZE + y for x in range(X_SIZE)] for y in range(Y_SIZE)]
     y_groups = [[x * Y_SIZE + y for y in range(Y_SIZE)] for x in range(X_SIZE)]
 
-    scans3 = scans.reshape(volumes, lines, width)
+    scans3 = keep_near(scans.reshape(volumes, lines, width))
     maps3 = maps.reshape(own_count, lines, width)
     own_piece = lax.dynamic_slice_in_dim(maps3, subj, 1, 1).reshape(own_count, width)
     proj_part = jnp.einsum("ryx,kyx->rk", scans3, maps3, preferred_element_type=WIDE)

time: 126 us -> 129 us (1.024)
  local copies, waits for them, and re-layouts: 4.4 us -> 7.11 us
  starting transfers between devices: 28.1 us -> 30.7 us
  waiting for transfers between devices: 20.8 us -> 19.1 us
    unnamed x12 -> x16, local copies, waits for them, and re-layouts: 2.88 us -> 5.58 us
    ppermute x2, waiting for transfers between devices: 1.71 us -> 0.01 us  [on_device(): sides.append(lax.ppermute(edge, axis, [(b, a) for a, b in up]) + 0.0)]
    ppermute x2, starting transfers between devices: 4.99 us -> 6.36 us  [on_device(): sides.append(lax.ppermute(edge, axis, up) + 0.0)]
  transfers between devices with their start and end apart: 7 -> 7, of which waited for: 3 -> 2; matrix products, arithmetic and copies ran while one was open for 2% -> 2% of each run, Pallas kernels for 0% -> 0%
where the time goes in v7:
time: 129 us
  blocking collectives  57.2 us (44%)
  starting transfers between devices  30.7 us (24%)
  waiting for transfers between devices  19.1 us (15%)
  matrix products  11 us (9%)
  local copies, waits for them, and re-layouts  7.11 us (6%)
  between operations  1.72 us (1%)
  other arithmetic  1.52 us (1%)
    all_to_all x1, blocking collectives, on_device(): taken = lax.all_to_all(sent, ring_axes, 0, 0)  21.2 us
    all_to_all x1, blocking collectives, on_device(): lax.all_to_all(sent, 'subj', 0, 0, axis_index_groups=x_groups).astype(WIDE)  18.2 us
    all_to_all x1, blocking collectives, on_device(): summed = lax.all_to_all(sent, 'subj', 0, 0, axis_index_groups=y_groups)  17.8 us
    all_to_all x1, waiting for transfers between devices, on_device(): lax.all_to_all(jnp.concatenate([proj_rows, gram_parts], axis=1), ring_axe...  12.4 us
    all_to_all x1, starting transfers between devices, on_device(): lax.all_to_all(jnp.broadcast_to(mine, (ring,) + mine.shape), ring_axes, 0...  8.53 us
    ppermute x1, starting transfers between devices, on_device(): lax.ppermute(jnp.concatenate([own_stats, own_piece], axis=0), 'comp', SWAP)  7.2 us
    ppermute x1, waiting for transfers between devices, on_device(): lax.ppermute(jnp.concatenate([own_stats, own_piece], axis=0), 'comp', SWAP)  6.67 us
    ppermute x2, starting transfers between devices, on_device(): sides.append(lax.ppermute(edge, axis, up) + 0.0)  6.36 us
  transfers between devices with their start and end apart: 7, of which 2 were waited for; matrix products, arithmetic and copies ran while one was open for 2% of the time, Pallas kernels for 0%

profile of v7, /device:TPU:1, one launch (start us, length us, event | category | flops | bytes accessed | tf_op | source)
XLA Modules:
  0.0 128.7 jit_solution(248665887633383643)
XLA Ops:
  0.7 2.1 %copy-done.1 = bf16[448,1,32,128]{3,2,1,0:T(8,128)(2,1)S(1)} copy-done((bf16[448,1,32,128]{3,2,1,0:T(8,128)(2,1)S(1)}, bf16[448,1,32,128]{3,2,1,0:T(8,128)(2,1)}, u32[]{:S(2)}) %copy-start.1) | copy-done | bytes 3670040
  2.8 0.3 shard_map.84
  3.0 1.8 %copy-done.2 = bf16[448,32,128]{2,1,0:T(8,128)(2,1)} copy-done((bf16[448,32,128]{2,1,0:T(8,128)(2,1)}, bf16[448,32,128]{2,1,0:T(8,128)(2,1)S(1)}, u32[]{:S(2)}) %copy-start.2) | copy-done | bytes 3670040
  5.0 3.4 %fusion.13 = bf16[448,128]{1,0:T(8,128)(2,1)S(1)} fusion(bf16[448,32,128]{2,1,0:T(8,128)(2,1)} %copy-done.2, bf16[128,32,128]{2,1,0:T(8,128)(2,1)S(1)} %bitcast.88), kind=kOutput, calls=%fused_computation.10 | convolution fusion | flops 469876736 | bytes 4833280 | tf_op jit(solution)/shard_map/ryx,kyx->rk/dot_general | solution.py:65
  8.4 21.2 %all_to_all.25 = bf16[16,40,128]{2,1,0:T(8,128)(2,1)S(1)} all-to-all(bf16[16,40,128]{2,1,0:T(8,128)(2,1)S(1)} %fusion.26), channel_id=1, replica_groups=mesh['slab'=8,'subj'=32,'comp'=2] {'slab','comp'}, dimensions={0} | all-to-all | bytes 327680 | tf_op jit(solution)/shard_map/all_to_all | solution.py:73
  30.5 0.8 pad_maximum_fusion.2
  31.3 4.1 %all-to-all-start.1 = ((bf16[16,88,128]{2,1,0:T(8,128)(2,1)}), bf16[16,88,128]{2,1,0:T(8,128)(2,1)S(1)}, u32[]{:S(2)}, u32[]{:S(2)}) async-start(bf16[16,88,128]{2,1,0:T(8,128)(2,1)} %pad_maximum_fusion.2), calls=%async_computation.1 | async-start | bytes 720896 | tf_op jit(solution)/shard_map/all_to_all | solution.py:83
  36.1 12.4 %all-to-all-done.1 = bf16[16,88,128]{2,1,0:T(8,128)(2,1)S(1)} async-done(((bf16[16,88,128]{2,1,0:T(8,128)(2,1)}), bf16[16,88,128]{2,1,0:T(8,128)(2,1)S(1)}, u32[]{:S(2)}, u32[]{:S(2)}) %all-to-all-start.1) | async-done | bytes 360480 | tf_op jit(solution)/shard_map/all_to_all | solution.py:83
  48.5 0.3 fusion.28
  48.9 3.6 %multiply_convert_fusion = bf16[128,32,128]{2,0,1:T(8,128)(2,1)S(1)} fusion(bf16[448,32,128]{2,1,0:T(8,128)(2,1)} %copy-done.2, bf16[448,128]{1,0:T(8,128)(2,1)S(1)} %bitcast.96, bf16[448,128]{1,0:T(8,128)(2,1)S(1)} %bitcast.99, pred[]{:T(512)S(6)} %eq.14, bf16[448]{0:T(512)(128)(2,1)S(1)} %fusion.82), kind=kOutput, calls=%fused_computation.4 | convolution fusion | flops 471097344 | bytes 4948865 | tf_op jit(solution)/shard_map/rk,ryx->ykx/dot_general | solution.py:90
  52.6 18.2 %all_to_all.26 = bf16[4,1080,128]{2,1,0:T(8,128)(2,1)S(1)} all-to-all(bf16[4,1080,128]{2,1,0:T(8,128)(2,1)S(1)} %pad_maximum_fusion), channel_id=1, replica_groups={{0,16,32,48},{2,18,34,50},{4,20,36,52},{6,22,38,54},{8,24,40,56},{10,26..., dimensions={0} | all-to-all | bytes 2211840 | tf_op jit(solution)/shard_map/all_to_all | solution.py:97
  70.8 0.3 reduce_sum.59
  71.2 17.8 %all_to_all.27 = bf16[8,184,128]{2,1,0:T(8,128)(2,1)S(1)} all-to-all(bf16[8,184,128]{2,1,0:T(8,128)(2,1)S(1)} %pad_maximum_fusion.1), channel_id=1, replica_groups={{0,2,4,6,8,10,12,14},{16,18,20,22,24,26,28,30},{32,34,36,38,40,42,44,46..., dimensions={0} | all-to-all | bytes 753664 | tf_op jit(solution)/shard_map/all_to_all | solution.py:107
  89.1 0.7 broadcast_in_dim.17
  89.8 8.5 %all-to-all-start.4 = ((bf16[16,56,128]{2,1,0:T(8,128)(2,1)}), bf16[16,56,128]{2,1,0:T(8,128)(2,1)S(1)}, u32[]{:S(2)}, u32[]{:S(2)}) async-start(bf16[16,56,128]{2,1,0:T(8,128)(2,1)} %broadcast_in_dim.17), calls=%async_computation.4 | async-start | bytes 458752 | tf_op jit(solution)/shard_map/all_to_all | solution.py:113
  98.5 7.2 %collective-permute-start = (bf16[256,128]{0,1:T(8,128)(2,1)S(1)}, bf16[256,128]{0,1:T(8,128)(2,1)S(1)}, u32[]{:S(2)}, u32[]{:S(2)}) collective-permute-start(bf16[256,128]{0,1:T(8,128)(2,1)S(1)} %pad_maximum_fusion.7), channel_id=1, source_target_pairs={{0,1},{1,0},{2,3},{3,2},{4,5},{5,4},{6,7},{7,6},{8,9},{9,8},{10,11... | collective-permute-start | bytes 196616 | tf_op jit(solution)/shard_map/ppermute | solution.py:110
  105.8 6.7 %collective-permute-done = bf16[256,128]{0,1:T(8,128)(2,1)S(1)} collective-permute-done((bf16[256,128]{0,1:T(8,128)(2,1)S(1)}, bf16[256,128]{0,1:T(8,128)(2,1)S(1)}, u32[]{:S(2)}, u32[]{:S(2)}) %collective-permute-start) | collective-permute-done | bytes 65568 | tf_op jit(solution)/shard_map/ppermute | solution.py:110
  112.6 0.3 fusion.24
  112.9 0.3 fusion.23
  113.2 0.3 convolution_add_fusion.1
  113.6 0.3 fusion.103
  114.0 0.3 fusion.6
  114.3 0.3 fusion.29
  114.5 0.2 convolution_add_fusion.2
  115.1 0.2 fusion.102
  115.3 1.3 %collective-permute-start.4 = (bf16[128,128]{0,1:T(8,128)(2,1)S(1)}, bf16[128,128]{0,1:T(8,128)(2,1)S(1)}, u32[]{:S(2)}, u32[]{:S(2)}) collective-permute-start(bf16[128,128]{0,1:T(8,128)(2,1)S(1)} %get-tuple-element.27), channel_id=1, source_target_pairs={{2,0},{4,2},{6,4},{8,6},{10,8},{12,10},{14,12},{16,14},{18,16},{20... | collective-permute-start | bytes 98312 | tf_op jit(solution)/shard_map/ppermute | solution.py:150
  116.6 4.0 %collective-permute-start.3 = (bf16[128,128]{0,1:T(8,128)(2,1)S(1)}, bf16[128,128]{0,1:T(8,128)(2,1)S(1)}, u32[]{:S(2)}, u32[]{:S(2)}) collective-permute-start(bf16[128,128]{0,1:T(8,128)(2,1)S(1)} %get-tuple-element.27), channel_id=1, source_target_pairs={{0,2},{2,4},{4,6},{6,8},{8,10},{10,12},{12,14},{14,16},{16,18},{18... | collective-permute-start | bytes 98312 | tf_op jit(solution)/shard_map/ppermute | solution.py:149
  120.6 3.2 %collective-permute-start.2 = (bf16[128,128]{0,1:T(8,128)(2,1)S(1)}, bf16[128,128]{0,1:T(8,128)(2,1)S(1)}, u32[]{:S(2)}, u32[]{:S(2)}) collective-permute-start(bf16[128,128]{0,1:T(8,128)(2,1)S(1)} %get-tuple-element.27), channel_id=1, source_target_pairs={{64,0},{128,64},{192,128},{256,192},{320,256},{384,320},{448,384},... | collective-permute-start | bytes 98312 | tf_op jit(solution)/shard_map/ppermute | solution.py:150
  123.8 2.4 %collective-permute-start.1 = (bf16[128,128]{0,1:T(8,128)(2,1)S(1)}, bf16[128,128]{0,1:T(8,128)(2,1)S(1)}, u32[]{:S(2)}, u32[]{:S(2)}) collective-permute-start(bf16[128,128]{0,1:T(8,128)(2,1)S(1)} %get-tuple-element.27), channel_id=1, source_target_pairs={{0,64},{64,128},{128,192},{192,256},{256,320},{320,384},{384,448},... | collective-permute-start | bytes 98312 | tf_op jit(solution)/shard_map/ppermute | solution.py:149
  126.2 1.0 fusion.27
  127.2 0.7 copy.52
  128.0 0.7 copy.51
  (55 shorter events, 2.1 us)
Async XLA Ops:
  0.6 4.2 %copy-start = (bf16[128,1,32,128]{3,2,1,0:T(8,128)(2,1)S(1)}, bf16[128,1,32,128]{3,2,1,0:T(8,128)(2,1)}, u32[]{:S(2)}) copy-start(bf16[128,1,32,128]{3,2,1,0:T(8,128)(2,1)} %param.6) | copy-start | bytes 3145732
  0.6 2.1 %copy-start.1 = (bf16[448,1,32,128]{3,2,1,0:T(8,128)(2,1)S(1)}, bf16[448,1,32,128]{3,2,1,0:T(8,128)(2,1)}, u32[]{:S(2)}) copy-start(bf16[448,1,32,128]{3,2,1,0:T(8,128)(2,1)} %param.5) | copy-start | bytes 11010052
  3.0 1.8 %copy-start.2 = (bf16[448,32,128]{2,1,0:T(8,128)(2,1)}, bf16[448,32,128]{2,1,0:T(8,128)(2,1)S(1)}, u32[]{:S(2)}) copy-start(bf16[448,32,128]{2,1,0:T(8,128)(2,1)S(1)} %shard_map.84) | copy-start | bytes 11010052
  31.3 17.3 %all-to-all-start.1 = ((bf16[16,88,128]{2,1,0:T(8,128)(2,1)}), bf16[16,88,128]{2,1,0:T(8,128)(2,1)S(1)}, u32[]{:S(2)}, u32[]{:S(2)}) async-start(bf16[16,88,128]{2,1,0:T(8,128)(2,1)} %pad_maximum_fusion.2), calls=%async_computation.1 | async-start | bytes 720896 | tf_op jit(solution)/shard_map/all_to_all | solution.py:83
  70.8 34.9 %copy-start.5 = (f32[128,1,1,128]{3,2,1,0:T(1,128)S(1)}, f32[128,1,1,128]{3,2,1,0:T(1,128)}, u32[]{:S(2)}) copy-start(f32[128,1,1,128]{3,2,1,0:T(1,128)} %param.8) | copy-start | bytes 196612
  89.8 22.7 %all-to-all-start.4 = ((bf16[16,56,128]{2,1,0:T(8,128)(2,1)}), bf16[16,56,128]{2,1,0:T(8,128)(2,1)S(1)}, u32[]{:S(2)}, u32[]{:S(2)}) async-start(bf16[16,56,128]{2,1,0:T(8,128)(2,1)} %broadcast_in_dim.17), calls=%async_computation.4 | async-start | bytes 458752 | tf_op jit(solution)/shard_map/all_to_all | solution.py:113
  98.5 14.0 %collective-permute-start = (bf16[256,128]{0,1:T(8,128)(2,1)S(1)}, bf16[256,128]{0,1:T(8,128)(2,1)S(1)}, u32[]{:S(2)}, u32[]{:S(2)}) collective-permute-start(bf16[256,128]{0,1:T(8,128)(2,1)S(1)} %pad_maximum_fusion.7), channel_id=1, source_target_pairs={{0,1},{1,0},{2,3},{3,2},{4,5},{5,4},{6,7},{7,6},{8,9},{9,8},{10,11... | collective-permute-start | bytes 196616 | tf_op jit(solution)/shard_map/ppermute | solution.py:110
  112.9 1.6 %copy-start.4 = (f32[128,256]{1,0:T(8,128)S(1)}, f32[128,256]{1,0:T(8,128)}, u32[]{:S(2)}) copy-start(f32[128,256]{1,0:T(8,128)} %param.7) | copy-start | bytes 393220
  114.8 13.9 %copy-start.3 = (f32[128,256]{1,0:T(8,128)}, f32[128,256]{1,0:T(8,128)S(1)}, u32[]{:S(2)}) copy-start(f32[128,256]{1,0:T(8,128)S(1)} %convolution_add_fusion.2) | copy-start | bytes 393220
  115.3 12.6 %collective-permute-start.4 = (bf16[128,128]{0,1:T(8,128)(2,1)S(1)}, bf16[128,128]{0,1:T(8,128)(2,1)S(1)}, u32[]{:S(2)}, u32[]{:S(2)}) collective-permute-start(bf16[128,128]{0,1:T(8,128)(2,1)S(1)} %get-tuple-element.27), channel_id=1, source_target_pairs={{2,0},{4,2},{6,4},{8,6},{10,8},{12,10},{14,12},{16,14},{18,16},{20... | collective-permute-start | bytes 98312 | tf_op jit(solution)/shard_map/ppermute | solution.py:150
  116.6 11.3 %collective-permute-start.3 = (bf16[128,128]{0,1:T(8,128)(2,1)S(1)}, bf16[128,128]{0,1:T(8,128)(2,1)S(1)}, u32[]{:S(2)}, u32[]{:S(2)}) collective-permute-start(bf16[128,128]{0,1:T(8,128)(2,1)S(1)} %get-tuple-element.27), channel_id=1, source_target_pairs={{0,2},{2,4},{4,6},{6,8},{8,10},{10,12},{12,14},{14,16},{16,18},{18... | collective-permute-start | bytes 98312 | tf_op jit(solution)/shard_map/ppermute | solution.py:149
  120.6 7.3 %collective-permute-start.2 = (bf16[128,128]{0,1:T(8,128)(2,1)S(1)}, bf16[128,128]{0,1:T(8,128)(2,1)S(1)}, u32[]{:S(2)}, u32[]{:S(2)}) collective-permute-start(bf16[128,128]{0,1:T(8,128)(2,1)S(1)} %get-tuple-element.27), channel_id=1, source_target_pairs={{64,0},{128,64},{192,128},{256,192},{320,256},{384,320},{448,384},... | collective-permute-start | bytes 98312 | tf_op jit(solution)/shard_map/ppermute | solution.py:150
  123.8 4.1 %collective-permute-start.1 = (bf16[128,128]{0,1:T(8,128)(2,1)S(1)}, bf16[128,128]{0,1:T(8,128)(2,1)S(1)}, u32[]{:S(2)}, u32[]{:S(2)}) collective-permute-start(bf16[128,128]{0,1:T(8,128)(2,1)S(1)} %get-tuple-element.27), channel_id=1, source_target_pairs={{0,64},{64,128},{128,192},{192,256},{256,320},{320,384},{384,448},... | collective-permute-start | bytes 98312 | tf_op jit(solution)/shard_map/ppermute | solution.py:149

commit v8 on v6

--- a/solution.py
+++ b/solution.py
@@ -24,6 +24,11 @@
     sum6 = sum3 + dot(third, sum3)
     sixth = dot(third, third)
     return 0.1 * (sum6 + dot(sixth, sum6))
+
+
+def symmetric(low, cross, high):
+    top = jnp.concatenate([low, cross], axis=1)
+    return jnp.concatenate([top, jnp.concatenate([cross.T, high], axis=1)], axis=0).astype(WIDE)
 
 
 def on_device(scans, maps, gram_old, stats_old, kept):
@@ -55,25 +60,30 @@
     proj_rows = taken[:, :rows].reshape(slabs, 2, rows, own_count).astype(WIDE).sum(0).astype(LOW)
     voxels = taken[:, rows:].reshape(slabs, 2, few, own_count)
     low_part, high_part = [voxels[:, i].reshape(slabs * few, own_count) for i in range(2)]
-    gram_parts = [
-        jnp.dot(one.T, two, preferred_element_type=WIDE).reshape(ring, few, own_count)
+    shares = [
+        jnp.dot(one.T, two, preferred_element_type=WIDE) * (1.0 / voxel_total)
         for one, two in ((low_part, low_part), (high_part, high_part), (low_part, high_part))
     ]
-    gram_parts = (jnp.concatenate(gram_parts, axis=1) * (1.0 / voxel_total)).astype(LOW)
-    proj_rows = jnp.broadcast_to(proj_rows.reshape(2 * rows, own_count), (ring, 2 * rows, own_count))
-    back = lax.all_to_all(jnp.concatenate([proj_rows, gram_parts], axis=1), ring_axes, 0, 0)
-    proj_pair = [back[:pieces, i * rows : (i + 1) * rows].reshape(volumes, own_count) for i in range(2)]
-    proj = jnp.concatenate(proj_pair, axis=1)
-    gram_rows = back[:, 2 * rows :].astype(WIDE).sum(0).astype(LOW)
+    product_scale = 0.5 / total_rows
+    first_row = (2 * slab + comp) * rows
+    live = (first_row + lax.iota(jnp.int32, rows) < kept[0]).astype(LOW)
+    shares.append(
+        jnp.dot((proj_rows[0] * live[:, None]).T, proj_rows[1], preferred_element_type=WIDE) * product_scale
+    )
+    shares = jnp.concatenate([share.reshape(ring, few, own_count) for share in shares], axis=1).astype(LOW)
+    to_owner = jnp.broadcast_to(proj_rows, (slabs, 2, rows, own_count)).reshape(ring, rows, own_count)
+    back = lax.all_to_all(jnp.concatenate([to_owner, shares], axis=1), ring_axes, 0, 0)
+    proj_own = back[:pieces, :rows].reshape(volumes, own_count)
+    shares = back[:, rows:].astype(WIDE).sum(0).astype(LOW)
 
     live = (lax.iota(jnp.int32, volumes) < kept[0]).astype(LOW)
-    live_proj = jnp.where(comp == 0, proj_pair[0], proj_pair[1]) * live[:, None]
+    live_proj = proj_own * live[:, None]
     term = jnp.einsum("rk,ryx->ykx", live_proj, scans3, preferred_element_type=WIDE)
     term = (term * (0.5 / math.sqrt(total_rows))).astype(LOW).reshape(X_SIZE, Y_SIZE * own_count, width)
-    product = jnp.dot(live_proj.T, proj, preferred_element_type=WIDE) * (0.5 / total_rows)
-    share = own_count // slabs
-    mine = lax.dynamic_slice_in_dim(product, slab * share, share, 0).astype(LOW)
-    mine = jnp.concatenate([mine[:, :own_count], mine[:, own_count:], gram_rows], axis=0)
+    product = jnp.dot(live_proj.T, proj_own, preferred_element_type=WIDE) * product_scale
+    square = own_count // slabs
+    mine = lax.dynamic_slice_in_dim(product, slab * square, square, 0).astype(LOW)
+    mine = jnp.concatenate([mine, shares], axis=0)
     sent = jnp.concatenate([term, jnp.broadcast_to(mine, (X_SIZE,) + mine.shape)], axis=1)
     taken = lax.all_to_all(sent, "subj", 0, 0, axis_index_groups=x_groups).astype(WIDE).sum(0).astype(LOW)
     split = Y_SIZE * own_count
@@ -90,37 +100,34 @@
     own_stats = summed[:own_count]
     other = lax.ppermute(jnp.concatenate([own_stats, own_piece], axis=0), "comp", SWAP)
     other_stats, other_piece = other[:own_count], other[own_count:]
-    mine = summed[own_count:]
-    shared = lax.all_to_all(jnp.broadcast_to(mine, (ring,) + mine.shape), ring_axes, 0, 0)
+    mine = jnp.broadcast_to(summed[own_count:], (slabs, 2, square + 4 * few, own_count))
+    to_other = jnp.broadcast_to(proj_rows[::-1], (slabs, 2, rows, own_count))
+    shared = jnp.concatenate([mine, to_other], axis=2).reshape(ring, -1, own_count)
+    shared = lax.all_to_all(shared, ring_axes, 0, 0)
 
-    gram_at = 2 * share
-    low_block, high_block, cross = [
-        shared[:, gram_at + i * few : gram_at + (i + 1) * few].reshape(own_count, own_count) for i in range(3)
+    squares = shared[:, :square].reshape(slabs, 2, square, own_count)
+    low_block, high_block, cross, product_cross = [
+        shared[:, square + i * few : square + (i + 1) * few].reshape(own_count, own_count) for i in range(4)
     ]
-    gram = jnp.concatenate(
-        [jnp.concatenate([low_block, cross], axis=1), jnp.concatenate([cross.T, high_block], axis=1)], axis=0
-    ).astype(WIDE)
+    proj_other = shared[:pieces, square + 4 * few :].reshape(volumes, own_count)
+    gram = symmetric(low_block, cross, high_block)
+    product = symmetric(squares[:, 0].reshape(own_count, own_count), product_cross, squares[:, 1].reshape(own_count, own_count))
     coding = power_sum(gram)
     own_coding = lax.dynamic_slice_in_dim(coding, comp * own_count, own_count, 1)
-    product = jnp.transpose(shared[:, :gram_at].reshape(slabs, 2, 2, share, own_count), (1, 0, 3, 2, 4))
-    product = product.reshape(COMPONENTS, COMPONENTS).astype(WIDE)
     product = jnp.dot(jnp.dot(own_coding.T, product, precision=fine), coding, precision=fine)
-    codes = jnp.dot(proj.astype(WIDE), own_coding, precision=fine)
-    both_stats = jnp.where(
-        comp == 0,
-        jnp.concatenate([own_stats, other_stats], axis=0),
-        jnp.concatenate([other_stats, own_stats], axis=0),
-    ).astype(WIDE)
-    stats_line = 0.5 * stats_old.reshape(own_count, width) + jnp.dot(own_coding.T, both_stats, precision=fine)
+    from_own = lax.dynamic_slice_in_dim(own_coding, comp * own_count, own_count, 0)
+    from_other = lax.dynamic_slice_in_dim(own_coding, (1 - comp) * own_count, own_count, 0)
+    codes = jnp.dot(proj_own.astype(WIDE), from_own, precision=fine)
+    codes = codes + jnp.dot(proj_other.astype(WIDE), from_other, precision=fine)
+    added = jnp.dot(from_own.T, own_stats.astype(WIDE), precision=fine)
+    added = added + jnp.dot(from_other.T, other_stats.astype(WIDE), precision=fine)
+    stats_line = 0.5 * stats_old.reshape(own_count, width) + added
     gram_new = 0.5 * gram_old + product
-    piece = jnp.where(
-        comp == 0,
-        jnp.concatenate([own_piece, other_piece], axis=0),
-        jnp.concatenate([other_piece, own_piece], axis=0),
-    ).astype(WIDE)
     block = lax.dynamic_slice_in_dim(gram_new, comp * own_count, own_count, 1)
+    other_block = lax.dynamic_slice_in_dim(gram_new, (1 - comp) * own_count, own_count, 1)
     diag = jnp.sum(block * jnp.eye(own_count, dtype=WIDE), axis=1, keepdims=True)
-    coupled = jnp.dot(gram_new, piece, precision=fine)
+    coupled = jnp.dot(block, own_piece.astype(WIDE), precision=fine)
+    coupled = coupled + jnp.dot(other_block, other_piece.astype(WIDE), precision=fine)
     updated = own_piece.astype(WIDE) + (stats_line - coupled) / diag
     edge = updated.astype(LOW)
     sides = []

time: 126 us -> 129 us (1.024)
  blocking collectives: 57.2 us -> 18.2 us
  starting transfers between devices: 28.1 us -> 47.9 us
  waiting for transfers between devices: 20.8 us -> 37.3 us
  matrix products: 11 us -> 14.7 us
  other arithmetic: 1.63 us -> 3 us
    all_to_all x2 -> x0, blocking collectives: 39 us -> none  [the longest x1 21.2 us: on_device(): taken = lax.all_to_all(sent, ring_axes, 0, 0)]
    all_to_all x2 -> x4, waiting for transfers between devices: 12.4 us -> 36 us  [the longest x1 11.3 us: on_device(): lax.all_to_all(jnp.concatenate([to_owner, shares], axis=1), ring_axes, 0, 0)]
    all_to_all x2 -> x4, starting transfers between devices: 12.7 us -> 30.8 us  [the longest x1 11.8 us: on_device(): taken = lax.all_to_all(sent, ring_axes, 0, 0)]
    ppermute x1, waiting for transfers between devices: 6.67 us -> 0.01 us  [on_device(): lax.ppermute(jnp.concatenate([own_stats, own_piece], axis=0), 'comp', SWAP)]
    dot_general x7 -> x11, matrix products: 2.11 us -> 5.81 us  [the longest x3 2.48 us: on_device(): jnp.dot(one.T, two, preferred_element_type=WIDE) * (1.0 / voxel_total)]
    ppermute x2, starting transfers between devices: 4.99 us -> 6.72 us  [on_device(): sides.append(lax.ppermute(edge, axis, up) + 0.0)]
    unnamed x12 -> x14, local copies, waits for them, and re-layouts: 2.88 us -> 3.58 us
  transfers between devices with their start and end apart: 7 -> 9, of which waited for: 3 -> 5; matrix products, arithmetic and copies ran while one was open for 2% -> 4% of each run, Pallas kernels for 0% -> 0%
where the time goes in v8:
time: 129 us; the launch traced here: 127 us
  starting transfers between devices  47.9 us (37%)
  waiting for transfers between devices  37.3 us (29%)
  blocking collectives  18.2 us (14%)
  matrix products  14.7 us (11%)
  local copies, waits for them, and re-layouts  4.16 us (3%)
  other arithmetic  3 us (2%)
  between operations  1.69 us (1%)
    all_to_all x1, blocking collectives, on_device(): lax.all_to_all(sent, 'subj', 0, 0, axis_index_groups=x_groups).astype(WIDE)  18.2 us
    all_to_all x1, starting transfers between devices, on_device(): taken = lax.all_to_all(sent, ring_axes, 0, 0)  11.8 us
    all_to_all x1, waiting for transfers between devices, on_device(): lax.all_to_all(jnp.concatenate([to_owner, shares], axis=1), ring_axes, 0, 0)  11.3 us
    all_to_all x1, waiting for transfers between devices, on_device(): summed = lax.all_to_all(sent, 'subj', 0, 0, axis_index_groups=y_groups)  10.5 us
    all_to_all x1, waiting for transfers between devices, on_device(): taken = lax.all_to_all(sent, ring_axes, 0, 0)  8.95 us
    all_to_all x1, starting transfers between devices, on_device(): shared = lax.all_to_all(shared, ring_axes, 0, 0)  8 us
    ppermute x1, starting transfers between devices, on_device(): lax.ppermute(jnp.concatenate([own_stats, own_piece], axis=0), 'comp', SWAP)  7.2 us
    all_to_all x1, starting transfers between devices, on_device(): summed = lax.all_to_all(sent, 'subj', 0, 0, axis_index_groups=y_groups)  6.8 us
  transfers between devices with their start and end apart: 9, of which 5 were waited for; matrix products, arithmetic and copies ran while one was open for 4% of the time, Pallas kernels for 0%

profile of v8, /device:TPU:1, one launch (start us, length us, event | category | flops | bytes accessed | tf_op | source)
XLA Modules:
  0.0 127.0 jit_solution(15768382671165707676)
XLA Ops:
  0.7 1.2 copy-done
  2.1 3.4 %fusion.13 = bf16[448,128]{1,0:T(8,128)(2,1)S(1)} fusion(bf16[448,32,128]{2,1,0:T(8,128)(2,1)} %bitcast.134, bf16[128,32,128]{2,1,0:T(8,128)(2,1)S(1)} %bitcast.132), kind=kOutput, calls=%fused_computation.11 | convolution fusion | flops 469876736 | bytes 4833280 | tf_op jit(solution)/shard_map/ryx,kyx->rk/dot_general | solution.py:51
  5.5 0.7 fusion.42
  6.1 11.8 %all-to-all-start = ((bf16[16,40,128]{2,1,0:T(8,128)(2,1)}), bf16[16,40,128]{2,1,0:T(8,128)(2,1)S(1)}, u32[]{:S(2)}, u32[]{:S(2)}) async-start(bf16[16,40,128]{2,1,0:T(8,128)(2,1)} %fusion.42), calls=%async_computation | async-start | bytes 327680 | tf_op jit(solution)/shard_map/all_to_all | solution.py:59
  18.6 8.9 %all-to-all-done = bf16[16,40,128]{2,1,0:T(8,128)(2,1)S(1)} async-done(((bf16[16,40,128]{2,1,0:T(8,128)(2,1)}), bf16[16,40,128]{2,1,0:T(8,128)(2,1)S(1)}, u32[]{:S(2)}, u32[]{:S(2)}) %all-to-all-start) | async-done | bytes 163872 | tf_op jit(solution)/shard_map/all_to_all | solution.py:59
  27.7 0.7 constant_dynamic-update-slice_fusion
  28.4 0.8 fusion.34
  29.2 0.8 fusion.32
  30.0 0.8 fusion.30
  30.8 0.9 fusion.28
  31.7 4.1 %all-to-all-start.1 = ((bf16[16,64,128]{2,1,0:T(8,128)(2,1)}), bf16[16,64,128]{2,1,0:T(8,128)(2,1)S(1)}, u32[]{:S(2)}, u32[]{:S(2)}) async-start(bf16[16,64,128]{2,1,0:T(8,128)(2,1)} %fusion.28), calls=%async_computation.1 | async-start | bytes 524288 | tf_op jit(solution)/shard_map/all_to_all | solution.py:75
  35.8 11.3 %all-to-all-done.1 = bf16[16,64,128]{2,1,0:T(8,128)(2,1)S(1)} async-done(((bf16[16,64,128]{2,1,0:T(8,128)(2,1)}), bf16[16,64,128]{2,1,0:T(8,128)(2,1)S(1)}, u32[]{:S(2)}, u32[]{:S(2)}) %all-to-all-start.1) | async-done | bytes 262176 | tf_op jit(solution)/shard_map/all_to_all | solution.py:75
  47.2 3.6 %multiply_convert_fusion = bf16[128,32,128]{2,0,1:T(8,128)(2,1)S(1)} fusion(bf16[448,128,1]{1,0,2:T(8,128)(2,1)S(1)} %bitcast.144, bf16[448,32,128]{2,1,0:T(8,128)(2,1)} %bitcast.135), kind=kOutput, calls=%fused_computation.4 | convolution fusion | flops 470810624 | bytes 4833280 | tf_op jit(solution)/shard_map/rk,ryx->ykx/dot_general | solution.py:81
  50.8 0.3 convolution_bitcast_fusion
  51.3 18.2 %all_to_all.25 = bf16[4,1072,128]{2,1,0:T(8,128)(2,1)S(1)} all-to-all(bf16[4,1072,128]{2,1,0:T(8,128)(2,1)S(1)} %pad_maximum_fusion), channel_id=1, replica_groups={{0,16,32,48},{2,18,34,50},{4,20,36,52},{6,22,38,54},{8,24,40,56},{10,26..., dimensions={0} | all-to-all | bytes 2195456 | tf_op jit(solution)/shard_map/all_to_all | solution.py:88
  69.8 0.8 pad_maximum_fusion.1
  70.6 6.8 %all-to-all-start.3 = ((bf16[8,176,128]{2,1,0:T(8,128)(2,1)}), bf16[8,176,128]{2,1,0:T(8,128)(2,1)S(1)}, u32[]{:S(2)}, u32[]{:S(2)}) async-start(bf16[8,176,128]{2,1,0:T(8,128)(2,1)} %pad_maximum_fusion.1), calls=%async_computation.3 | async-start | bytes 720896 | tf_op jit(solution)/shard_map/all_to_all | solution.py:98
  77.4 10.5 %all-to-all-done.3 = bf16[8,176,128]{2,1,0:T(8,128)(2,1)S(1)} async-done(((bf16[8,176,128]{2,1,0:T(8,128)(2,1)}), bf16[8,176,128]{2,1,0:T(8,128)(2,1)S(1)}, u32[]{:S(2)}, u32[]{:S(2)}) %all-to-all-start.3) | async-done | bytes 360480 | tf_op jit(solution)/shard_map/all_to_all | solution.py:98
  88.0 0.8 pad_maximum_fusion.2
  88.8 8.0 %all-to-all-start.4 = ((bf16[16,80,128]{2,1,0:T(8,128)(2,1)}), bf16[16,80,128]{2,1,0:T(8,128)(2,1)S(1)}, u32[]{:S(2)}, u32[]{:S(2)}) async-start(bf16[16,80,128]{2,1,0:T(8,128)(2,1)} %bitcast.29), calls=%async_computation.4 | async-start | bytes 655360 | tf_op jit(solution)/shard_map/all_to_all | solution.py:106
  97.0 7.2 %collective-permute-start = (bf16[256,128]{0,1:T(8,128)(2,1)S(1)}, bf16[256,128]{0,1:T(8,128)(2,1)S(1)}, u32[]{:S(2)}, u32[]{:S(2)}) collective-permute-start(bf16[256,128]{0,1:T(8,128)(2,1)S(1)} %pad_maximum_fusion.3), channel_id=1, source_target_pairs={{0,1},{1,0},{2,3},{3,2},{4,5},{5,4},{6,7},{7,6},{8,9},{9,8},{10,11... | collective-permute-start | bytes 196616 | tf_op jit(solution)/shard_map/ppermute | solution.py:101
  104.2 5.3 %all-to-all-done.4 = bf16[16,80,128]{2,1,0:T(8,128)(2,1)S(1)} async-done(((bf16[16,80,128]{2,1,0:T(8,128)(2,1)}), bf16[16,80,128]{2,1,0:T(8,128)(2,1)S(1)}, u32[]{:S(2)}, u32[]{:S(2)}) %all-to-all-start.4) | async-done | bytes 327712 | tf_op jit(solution)/shard_map/all_to_all | solution.py:106
  109.7 0.3 fusion.41
  110.3 0.3 convolution_add_fusion.1
  112.9 4.5 %collective-permute-start.1 = (bf16[128,128]{0,1:T(8,128)(2,1)S(1)}, bf16[128,128]{0,1:T(8,128)(2,1)S(1)}, u32[]{:S(2)}, u32[]{:S(2)}) collective-permute-start(bf16[128,128]{0,1:T(8,128)(2,1)S(1)} %get-tuple-element.24), channel_id=1, source_target_pairs={{0,64},{64,128},{128,192},{192,256},{256,320},{320,384},{384,448},... | collective-permute-start | bytes 98312 | tf_op jit(solution)/shard_map/ppermute | solution.py:137
  117.4 1.9 %collective-permute-start.2 = (bf16[128,128]{0,1:T(8,128)(2,1)S(1)}, bf16[128,128]{0,1:T(8,128)(2,1)S(1)}, u32[]{:S(2)}, u32[]{:S(2)}) collective-permute-start(bf16[128,128]{0,1:T(8,128)(2,1)S(1)} %get-tuple-element.24), channel_id=1, source_target_pairs={{64,0},{128,64},{192,128},{256,192},{320,256},{384,320},{448,384},... | collective-permute-start | bytes 98312 | tf_op jit(solution)/shard_map/ppermute | solution.py:138
  119.3 2.2 %collective-permute-start.3 = (bf16[128,128]{0,1:T(8,128)(2,1)S(1)}, bf16[128,128]{0,1:T(8,128)(2,1)S(1)}, u32[]{:S(2)}, u32[]{:S(2)}) collective-permute-start(bf16[128,128]{0,1:T(8,128)(2,1)S(1)} %get-tuple-element.24), channel_id=1, source_target_pairs={{0,2},{2,4},{4,6},{6,8},{8,10},{10,12},{12,14},{14,16},{16,18},{18... | collective-permute-start | bytes 98312 | tf_op jit(solution)/shard_map/ppermute | solution.py:137
  121.5 1.3 %collective-permute-start.4 = (bf16[128,128]{0,1:T(8,128)(2,1)S(1)}, bf16[128,128]{0,1:T(8,128)(2,1)S(1)}, u32[]{:S(2)}, u32[]{:S(2)}) collective-permute-start(bf16[128,128]{0,1:T(8,128)(2,1)S(1)} %get-tuple-element.24), channel_id=1, source_target_pairs={{2,0},{4,2},{6,4},{8,6},{10,8},{12,10},{14,12},{16,14},{18,16},{20... | collective-permute-start | bytes 98312 | tf_op jit(solution)/shard_map/ppermute | solution.py:138
  123.2 1.0 convolution_add_fusion.2
  124.2 0.7 copy.50
  124.9 1.3 %collective-permute-done.4 = bf16[128,128]{0,1:T(8,128)(2,1)S(1)} collective-permute-done((bf16[128,128]{0,1:T(8,128)(2,1)S(1)}, bf16[128,128]{0,1:T(8,128)(2,1)S(1)}, u32[]{:S(2)}, u32[]{:S(2)}) %collective-permute-start.4) | collective-permute-done | bytes 32800 | tf_op jit(solution)/shard_map/ppermute | solution.py:138
  126.3 0.7 copy.49
  (56 shorter events, 4.1 us)
Async XLA Ops:
  0.6 1.2 copy-start
  6.1 21.4 %all-to-all-start = ((bf16[16,40,128]{2,1,0:T(8,128)(2,1)}), bf16[16,40,128]{2,1,0:T(8,128)(2,1)S(1)}, u32[]{:S(2)}, u32[]{:S(2)}) async-start(bf16[16,40,128]{2,1,0:T(8,128)(2,1)} %fusion.42), calls=%async_computation | async-start | bytes 327680 | tf_op jit(solution)/shard_map/all_to_all | solution.py:59
  31.7 15.4 %all-to-all-start.1 = ((bf16[16,64,128]{2,1,0:T(8,128)(2,1)}), bf16[16,64,128]{2,1,0:T(8,128)(2,1)S(1)}, u32[]{:S(2)}, u32[]{:S(2)}) async-start(bf16[16,64,128]{2,1,0:T(8,128)(2,1)} %fusion.28), calls=%async_computation.1 | async-start | bytes 524288 | tf_op jit(solution)/shard_map/all_to_all | solution.py:75
  69.7 27.1 %copy-start.3 = (f32[128,1,1,128]{3,2,1,0:T(1,128)S(1)}, f32[128,1,1,128]{3,2,1,0:T(1,128)}, u32[]{:S(2)}) copy-start(f32[128,1,1,128]{3,2,1,0:T(1,128)} %param.8) | copy-start | bytes 196612
  70.6 17.3 %all-to-all-start.3 = ((bf16[8,176,128]{2,1,0:T(8,128)(2,1)}), bf16[8,176,128]{2,1,0:T(8,128)(2,1)S(1)}, u32[]{:S(2)}, u32[]{:S(2)}) async-start(bf16[8,176,128]{2,1,0:T(8,128)(2,1)} %pad_maximum_fusion.1), calls=%async_computation.3 | async-start | bytes 720896 | tf_op jit(solution)/shard_map/all_to_all | solution.py:98
  88.8 20.7 %all-to-all-start.4 = ((bf16[16,80,128]{2,1,0:T(8,128)(2,1)}), bf16[16,80,128]{2,1,0:T(8,128)(2,1)S(1)}, u32[]{:S(2)}, u32[]{:S(2)}) async-start(bf16[16,80,128]{2,1,0:T(8,128)(2,1)} %bitcast.29), calls=%async_computation.4 | async-start | bytes 655360 | tf_op jit(solution)/shard_map/all_to_all | solution.py:106
  97.0 15.4 %collective-permute-start = (bf16[256,128]{0,1:T(8,128)(2,1)S(1)}, bf16[256,128]{0,1:T(8,128)(2,1)S(1)}, u32[]{:S(2)}, u32[]{:S(2)}) collective-permute-start(bf16[256,128]{0,1:T(8,128)(2,1)S(1)} %pad_maximum_fusion.3), channel_id=1, source_target_pairs={{0,1},{1,0},{2,3},{3,2},{4,5},{5,4},{6,7},{7,6},{8,9},{9,8},{10,11... | collective-permute-start | bytes 196616 | tf_op jit(solution)/shard_map/ppermute | solution.py:101
  110.0 1.9 %copy-start.2 = (f32[128,256]{1,0:T(8,128)S(1)}, f32[128,256]{1,0:T(8,128)}, u32[]{:S(2)}) copy-start(f32[128,256]{1,0:T(8,128)} %param.7) | copy-start | bytes 393220
  112.1 14.9 %copy-start.1 = (f32[128,256]{1,0:T(8,128)}, f32[128,256]{1,0:T(8,128)S(1)}, u32[]{:S(2)}) copy-start(f32[128,256]{1,0:T(8,128)S(1)} %convolution_add_fusion.3) | copy-start | bytes 393220
  112.9 12.0 %collective-permute-start.1 = (bf16[128,128]{0,1:T(8,128)(2,1)S(1)}, bf16[128,128]{0,1:T(8,128)(2,1)S(1)}, u32[]{:S(2)}, u32[]{:S(2)}) collective-permute-start(bf16[128,128]{0,1:T(8,128)(2,1)S(1)} %get-tuple-element.24), channel_id=1, source_target_pairs={{0,64},{64,128},{128,192},{192,256},{256,320},{320,384},{384,448},... | collective-permute-start | bytes 98312 | tf_op jit(solution)/shard_map/ppermute | solution.py:137
  117.4 7.5 %collective-permute-start.2 = (bf16[128,128]{0,1:T(8,128)(2,1)S(1)}, bf16[128,128]{0,1:T(8,128)(2,1)S(1)}, u32[]{:S(2)}, u32[]{:S(2)}) collective-permute-start(bf16[128,128]{0,1:T(8,128)(2,1)S(1)} %get-tuple-element.24), channel_id=1, source_target_pairs={{64,0},{128,64},{192,128},{256,192},{320,256},{384,320},{448,384},... | collective-permute-start | bytes 98312 | tf_op jit(solution)/shard_map/ppermute | solution.py:138
  119.3 5.6 %collective-permute-start.3 = (bf16[128,128]{0,1:T(8,128)(2,1)S(1)}, bf16[128,128]{0,1:T(8,128)(2,1)S(1)}, u32[]{:S(2)}, u32[]{:S(2)}) collective-permute-start(bf16[128,128]{0,1:T(8,128)(2,1)S(1)} %get-tuple-element.24), channel_id=1, source_target_pairs={{0,2},{2,4},{4,6},{6,8},{8,10},{10,12},{12,14},{14,16},{16,18},{18... | collective-permute-start | bytes 98312 | tf_op jit(solution)/shard_map/ppermute | solution.py:137
  121.5 4.7 %collective-permute-start.4 = (bf16[128,128]{0,1:T(8,128)(2,1)S(1)}, bf16[128,128]{0,1:T(8,128)(2,1)S(1)}, u32[]{:S(2)}, u32[]{:S(2)}) collective-permute-start(bf16[128,128]{0,1:T(8,128)(2,1)S(1)} %get-tuple-element.24), channel_id=1, source_target_pairs={{2,0},{4,2},{6,4},{8,6},{10,8},{12,10},{14,12},{16,14},{18,16},{20... | collective-permute-start | bytes 98312 | tf_op jit(solution)/shard_map/ppermute | solution.py:138

commit v9 on v8

--- a/solution.py
+++ b/solution.py
@@ -24,6 +24,10 @@
     sum6 = sum3 + dot(third, sum3)
     sixth = dot(third, third)
     return 0.1 * (sum6 + dot(sixth, sum6))
+
+
+def after(value, done):
+    return value + (done != done).astype(value.dtype)
 
 
 def symmetric(low, cross, high):
@@ -54,35 +58,38 @@
     rows = 32
     pieces = volumes // rows
     few = own_count // ring
-    sent = jnp.pad(proj_part.reshape(pieces, rows, own_count), ((0, ring - pieces), (0, 0), (0, 0)))
+    square = own_count // slabs
+    first_row = (2 * slab + comp) * rows
+    first_square = (slab * square).astype(jnp.uint32)
+    noted = kept[0] + first_row + first_square.astype(jnp.int32)
+    empty = jnp.broadcast_to(noted.astype(LOW), (ring - pieces, rows, own_count))
+    sent = jnp.concatenate([proj_part.reshape(pieces, rows, own_count), empty], axis=0)
     sent = jnp.concatenate([sent, own_piece.T.reshape(ring, few, own_count)], axis=1)
     taken = lax.all_to_all(sent, ring_axes, 0, 0)
     proj_rows = taken[:, :rows].reshape(slabs, 2, rows, own_count).astype(WIDE).sum(0).astype(LOW)
     voxels = taken[:, rows:].reshape(slabs, 2, few, own_count)
-    low_part, high_part = [voxels[:, i].reshape(slabs * few, own_count) for i in range(2)]
-    shares = [
-        jnp.dot(one.T, two, preferred_element_type=WIDE) * (1.0 / voxel_total)
-        for one, two in ((low_part, low_part), (high_part, high_part), (low_part, high_part))
-    ]
+    voxels = jnp.concatenate([voxels[:, i].reshape(slabs * few, own_count) for i in range(2)], axis=1)
+    gram_part = jnp.dot(voxels.T, voxels, preferred_element_type=WIDE) * (1.0 / voxel_total)
     product_scale = 0.5 / total_rows
-    first_row = (2 * slab + comp) * rows
-    live = (first_row + lax.iota(jnp.int32, rows) < kept[0]).astype(LOW)
-    shares.append(
-        jnp.dot((proj_rows[0] * live[:, None]).T, proj_rows[1], preferred_element_type=WIDE) * product_scale
-    )
-    shares = jnp.concatenate([share.reshape(ring, few, own_count) for share in shares], axis=1).astype(LOW)
+    at_row = after(lax.broadcasted_iota(jnp.int32, (rows, own_count), 0), proj_rows[0])
+    live = first_row + at_row < kept[0]
+    cross_part = jnp.dot(jnp.where(live, proj_rows[0], 0).T, proj_rows[1], preferred_element_type=WIDE)
+    shares = [gram_part[:own_count, :own_count], gram_part[own_count:, own_count:], gram_part[:own_count, own_count:]]
+    shares.append(cross_part * product_scale)
+    shares = jnp.stack(shares).astype(LOW).reshape(4, ring, few, own_count)
+    shares = jnp.transpose(shares, (1, 0, 2, 3)).reshape(ring, 4 * few, own_count)
     to_owner = jnp.broadcast_to(proj_rows, (slabs, 2, rows, own_count)).reshape(ring, rows, own_count)
     back = lax.all_to_all(jnp.concatenate([to_owner, shares], axis=1), ring_axes, 0, 0)
-    proj_own = back[:pieces, :rows].reshape(volumes, own_count)
+    proj_own = back[:pieces, :rows]
+    at_piece = after(lax.broadcasted_iota(jnp.int32, proj_own.shape, 0), proj_own)
+    left = kept[0] - rows * at_piece
+    live_proj = jnp.where(lax.broadcasted_iota(jnp.int32, proj_own.shape, 1) < left, proj_own, 0).reshape(volumes, own_count)
+    proj_own = proj_own.reshape(volumes, own_count)
     shares = back[:, rows:].astype(WIDE).sum(0).astype(LOW)
-
-    live = (lax.iota(jnp.int32, volumes) < kept[0]).astype(LOW)
-    live_proj = proj_own * live[:, None]
     term = jnp.einsum("rk,ryx->ykx", live_proj, scans3, preferred_element_type=WIDE)
     term = (term * (0.5 / math.sqrt(total_rows))).astype(LOW).reshape(X_SIZE, Y_SIZE * own_count, width)
     product = jnp.dot(live_proj.T, proj_own, preferred_element_type=WIDE) * product_scale
-    square = own_count // slabs
-    mine = lax.dynamic_slice_in_dim(product, slab * square, square, 0).astype(LOW)
+    mine = lax.dynamic_slice(product, (first_square, jnp.uint32(0)), (square, own_count)).astype(LOW)
     mine = jnp.concatenate([mine, shares], axis=0)
     sent = jnp.concatenate([term, jnp.broadcast_to(mine, (X_SIZE,) + mine.shape)], axis=1)
     taken = lax.all_to_all(sent, "subj", 0, 0, axis_index_groups=x_groups).astype(WIDE).sum(0).astype(LOW)
@@ -100,9 +107,10 @@
     own_stats = summed[:own_count]
     other = lax.ppermute(jnp.concatenate([own_stats, own_piece], axis=0), "comp", SWAP)
     other_stats, other_piece = other[:own_count], other[own_count:]
-    mine = jnp.broadcast_to(summed[own_count:], (slabs, 2, square + 4 * few, own_count))
-    to_other = jnp.broadcast_to(proj_rows[::-1], (slabs, 2, rows, own_count))
-    shared = jnp.concatenate([mine, to_other], axis=2).reshape(ring, -1, own_count)
+    mine = summed[own_count:]
+    late_rows = after(proj_rows, mine[:rows])
+    shared = jnp.concatenate([mine, late_rows[1], mine, late_rows[0]], axis=0).reshape(2, -1, own_count)
+    shared = jnp.broadcast_to(shared, (slabs,) + shared.shape).reshape(ring, -1, own_count)
     shared = lax.all_to_all(shared, ring_axes, 0, 0)
 
     squares = shared[:, :square].reshape(slabs, 2, square, own_count)

time: 129 us -> 123 us (0.953)
  blocking collectives: 18.2 us -> 71.5 us
  waiting for transfers between devices: 37.3 us -> 6.59 us
  starting transfers between devices: 47.9 us -> 24.7 us
  matrix products: 14.7 us -> 11.7 us
  other arithmetic: 3 us -> 0.84 us
    all_to_all x0 -> x3, blocking collectives: none -> 53.3 us  [the longest x1 21.2 us: on_device(): taken = lax.all_to_all(sent, ring_axes, 0, 0)]
    all_to_all x3 -> x0, waiting for transfers between devices: 30.8 us -> none  [the longest x1 11.3 us: on_device(): lax.all_to_all(jnp.concatenate([to_owner, shares], axis=1), ring_axes, 0, 0)]
    all_to_all x3 -> x0, starting transfers between devices: 22.8 us -> none  [the longest x1 11.8 us: on_device(): taken = lax.all_to_all(sent, ring_axes, 0, 0)]
    dot_general x4 -> x2, matrix products: 3.34 us -> 0.41 us  [the longest x1 0.21 us: on_device(): jnp.dot(voxels.T, voxels, preferred_element_type=WIDE) * (1.0 / voxel_total)]
    unnamed x14 -> x13, local copies, waits for them, and re-layouts: 3.58 us -> 2.89 us
  transfers between devices with their start and end apart: 9 -> 6, of which waited for: 5 -> 2; matrix products, arithmetic and copies ran while one was open for 4% -> 4% of each run, Pallas kernels for 0% -> 0%
where the time goes in v9:
time: 123 us; the launch traced here: 121 us
  blocking collectives  71.5 us (58%)
  starting transfers between devices  24.7 us (20%)
  matrix products  11.7 us (10%)
  waiting for transfers between devices  6.59 us (5%)
  local copies, waits for them, and re-layouts  4.21 us (3%)
  between operations  1.77 us (1%)
    all_to_all x1, blocking collectives, on_device(): taken = lax.all_to_all(sent, ring_axes, 0, 0)  21.2 us
    all_to_all x1, blocking collectives, on_device(): lax.all_to_all(sent, 'subj', 0, 0, axis_index_groups=x_groups).astype(WIDE)  18.2 us
    all_to_all x1, blocking collectives, on_device(): summed = lax.all_to_all(sent, 'subj', 0, 0, axis_index_groups=y_groups)  17.5 us
    all_to_all x1, blocking collectives, on_device(): lax.all_to_all(jnp.concatenate([to_owner, shares], axis=1), ring_axes, 0, 0)  14.5 us
    all_to_all x1, starting transfers between devices, on_device(): shared = lax.all_to_all(shared, ring_axes, 0, 0)  7.6 us
    ppermute x1, starting transfers between devices, on_device(): lax.ppermute(jnp.concatenate([own_stats, own_piece], axis=0), 'comp', SWAP)  7.2 us
    ppermute x2, starting transfers between devices, on_device(): sides.append(lax.ppermute(edge, axis, up) + 0.0)  6.72 us
    all_to_all x1, waiting for transfers between devices, on_device(): shared = lax.all_to_all(shared, ring_axes, 0, 0)  5.26 us
  transfers between devices with their start and end apart: 6, of which 2 were waited for; matrix products, arithmetic and copies ran while one was open for 4% of the time, Pallas kernels for 0%

profile of v9, /device:TPU:1, one launch (start us, length us, event | category | flops | bytes accessed | tf_op | source)
XLA Modules:
  0.0 121.3 jit_solution(18338647189171608164)
XLA Ops:
  0.7 1.2 copy-done
  2.7 3.4 %fusion.14 = bf16[448,128]{1,0:T(8,128)(2,1)S(1)} fusion(bf16[448,32,128]{2,1,0:T(8,128)(2,1)} %bitcast.100, bf16[128,32,128]{2,1,0:T(8,128)(2,1)S(1)} %bitcast.98), kind=kOutput, calls=%fused_computation.13 | convolution fusion | flops 469876736 | bytes 4833280 | tf_op jit(solution)/shard_map/ryx,kyx->rk/dot_general | solution.py:55
  6.1 21.2 %all_to_all.25 = bf16[16,40,128]{2,1,0:T(8,128)(2,1)S(1)} all-to-all(bf16[16,40,128]{2,1,0:T(8,128)(2,1)S(1)} %fusion.31), channel_id=1, replica_groups=mesh['slab'=8,'subj'=32,'comp'=2] {'slab','comp'}, dimensions={0} | all-to-all | bytes 327680 | tf_op jit(solution)/shard_map/all_to_all | solution.py:68
  27.4 0.2 fusion.13
  28.0 14.5 %all_to_all.26 = bf16[16,64,128]{2,1,0:T(8,128)(2,1)S(1)} all-to-all(bf16[16,64,128]{2,1,0:T(8,128)(2,1)S(1)} %pad_maximum_fusion.2), channel_id=1, replica_groups=mesh['slab'=8,'subj'=32,'comp'=2] {'slab','comp'}, dimensions={0} | all-to-all | bytes 524288 | tf_op jit(solution)/shard_map/all_to_all | solution.py:82
  42.6 3.6 %multiply_convert_fusion = bf16[128,32,128]{2,0,1:T(8,128)(2,1)S(1)} fusion(bf16[448,128,1]{1,0,2:T(8,128)(2,1)S(1)} %bitcast.110, bf16[448,32,128]{2,1,0:T(8,128)(2,1)} %bitcast.101), kind=kOutput, calls=%fused_computation.4 | convolution fusion | flops 470810624 | bytes 4833280 | tf_op jit(solution)/shard_map/rk,ryx->ykx/dot_general | solution.py:89
  46.1 0.2 convolution_bitcast_fusion
  46.6 18.2 %all_to_all.27 = bf16[4,1072,128]{2,1,0:T(8,128)(2,1)S(1)} all-to-all(bf16[4,1072,128]{2,1,0:T(8,128)(2,1)S(1)} %pad_maximum_fusion), channel_id=1, replica_groups={{0,16,32,48},{2,18,34,50},{4,20,36,52},{6,22,38,54},{8,24,40,56},{10,26..., dimensions={0} | all-to-all | bytes 2195456 | tf_op jit(solution)/shard_map/all_to_all | solution.py:95
  64.7 0.3 reduce_sum.59
  65.1 17.5 %all_to_all.28 = bf16[8,176,128]{2,1,0:T(8,128)(2,1)S(1)} all-to-all(bf16[8,176,128]{2,1,0:T(8,128)(2,1)S(1)} %pad_maximum_fusion.1), channel_id=1, replica_groups={{0,2,4,6,8,10,12,14},{16,18,20,22,24,26,28,30},{32,34,36,38,40,42,44,46..., dimensions={0} | all-to-all | bytes 720896 | tf_op jit(solution)/shard_map/all_to_all | solution.py:105
  82.8 0.8 broadcast_in_dim.28
  83.5 7.6 %all-to-all-start.4 = ((bf16[16,80,128]{2,1,0:T(8,128)(2,1)}), bf16[16,80,128]{2,1,0:T(8,128)(2,1)S(1)}, u32[]{:S(2)}, u32[]{:S(2)}) async-start(bf16[16,80,128]{2,1,0:T(8,128)(2,1)} %bitcast.31), calls=%async_computation.4 | async-start | bytes 655360 | tf_op jit(solution)/shard_map/all_to_all | solution.py:114
  91.4 7.2 %collective-permute-start = (bf16[256,128]{0,1:T(8,128)(2,1)S(1)}, bf16[256,128]{0,1:T(8,128)(2,1)S(1)}, u32[]{:S(2)}, u32[]{:S(2)}) collective-permute-start(bf16[256,128]{0,1:T(8,128)(2,1)S(1)} %pad_maximum_fusion.3), channel_id=1, source_target_pairs={{0,1},{1,0},{2,3},{3,2},{4,5},{5,4},{6,7},{7,6},{8,9},{9,8},{10,11... | collective-permute-start | bytes 196616 | tf_op jit(solution)/shard_map/ppermute | solution.py:108
  98.6 5.3 %all-to-all-done.4 = bf16[16,80,128]{2,1,0:T(8,128)(2,1)S(1)} async-done(((bf16[16,80,128]{2,1,0:T(8,128)(2,1)}), bf16[16,80,128]{2,1,0:T(8,128)(2,1)S(1)}, u32[]{:S(2)}, u32[]{:S(2)}) %all-to-all-start.4) | async-done | bytes 327712 | tf_op jit(solution)/shard_map/all_to_all | solution.py:114
  104.0 0.3 fusion.29
  104.3 0.3 fusion.28
  104.6 0.3 convolution_add_fusion.1
  104.9 0.3 fusion.100
  105.4 0.3 fusion.6
  105.7 0.3 fusion.60
  105.9 0.3 fusion.32
  106.2 0.2 convolution_add_fusion.3
  106.8 0.2 fusion.19
  107.2 4.5 %collective-permute-start.1 = (bf16[128,128]{0,1:T(8,128)(2,1)S(1)}, bf16[128,128]{0,1:T(8,128)(2,1)S(1)}, u32[]{:S(2)}, u32[]{:S(2)}) collective-permute-start(bf16[128,128]{0,1:T(8,128)(2,1)S(1)} %get-tuple-element.35), channel_id=1, source_target_pairs={{0,64},{64,128},{128,192},{192,256},{256,320},{320,384},{384,448},... | collective-permute-start | bytes 98312 | tf_op jit(solution)/shard_map/ppermute | solution.py:145
  111.7 1.9 %collective-permute-start.2 = (bf16[128,128]{0,1:T(8,128)(2,1)S(1)}, bf16[128,128]{0,1:T(8,128)(2,1)S(1)}, u32[]{:S(2)}, u32[]{:S(2)}) collective-permute-start(bf16[128,128]{0,1:T(8,128)(2,1)S(1)} %get-tuple-element.35), channel_id=1, source_target_pairs={{64,0},{128,64},{192,128},{256,192},{320,256},{384,320},{448,384},... | collective-permute-start | bytes 98312 | tf_op jit(solution)/shard_map/ppermute | solution.py:146
  113.7 2.2 %collective-permute-start.3 = (bf16[128,128]{0,1:T(8,128)(2,1)S(1)}, bf16[128,128]{0,1:T(8,128)(2,1)S(1)}, u32[]{:S(2)}, u32[]{:S(2)}) collective-permute-start(bf16[128,128]{0,1:T(8,128)(2,1)S(1)} %get-tuple-element.35), channel_id=1, source_target_pairs={{0,2},{2,4},{4,6},{6,8},{8,10},{10,12},{12,14},{14,16},{16,18},{18... | collective-permute-start | bytes 98312 | tf_op jit(solution)/shard_map/ppermute | solution.py:145
  115.9 1.3 %collective-permute-start.4 = (bf16[128,128]{0,1:T(8,128)(2,1)S(1)}, bf16[128,128]{0,1:T(8,128)(2,1)S(1)}, u32[]{:S(2)}, u32[]{:S(2)}) collective-permute-start(bf16[128,128]{0,1:T(8,128)(2,1)S(1)} %get-tuple-element.35), channel_id=1, source_target_pairs={{2,0},{4,2},{6,4},{8,6},{10,8},{12,10},{14,12},{16,14},{18,16},{20... | collective-permute-start | bytes 98312 | tf_op jit(solution)/shard_map/ppermute | solution.py:146
  117.2 0.3 fusion.58
  117.5 1.0 convolution_add_fusion.2
  118.5 0.7 copy.65
  119.2 1.3 %collective-permute-done.4 = bf16[128,128]{0,1:T(8,128)(2,1)S(1)} collective-permute-done((bf16[128,128]{0,1:T(8,128)(2,1)S(1)}, bf16[128,128]{0,1:T(8,128)(2,1)S(1)}, u32[]{:S(2)}, u32[]{:S(2)}) %collective-permute-start.4) | collective-permute-done | bytes 32800 | tf_op jit(solution)/shard_map/ppermute | solution.py:146
  120.6 0.7 copy.64
  (53 shorter events, 1.9 us)
Async XLA Ops:
  0.6 1.2 %copy-start = (bf16[128,1,32,128]{3,2,1,0:T(8,128)(2,1)S(1)}, bf16[128,1,32,128]{3,2,1,0:T(8,128)(2,1)}, u32[]{:S(2)}) copy-start(bf16[128,1,32,128]{3,2,1,0:T(8,128)(2,1)} %param.6) | copy-start | bytes 3145732
  65.0 26.1 %copy-start.3 = (f32[128,1,1,128]{3,2,1,0:T(1,128)S(1)}, f32[128,1,1,128]{3,2,1,0:T(1,128)}, u32[]{:S(2)}) copy-start(f32[128,1,1,128]{3,2,1,0:T(1,128)} %param.8) | copy-start | bytes 196612
  83.5 20.3 %all-to-all-start.4 = ((bf16[16,80,128]{2,1,0:T(8,128)(2,1)}), bf16[16,80,128]{2,1,0:T(8,128)(2,1)S(1)}, u32[]{:S(2)}, u32[]{:S(2)}) async-start(bf16[16,80,128]{2,1,0:T(8,128)(2,1)} %bitcast.31), calls=%async_computation.4 | async-start | bytes 655360 | tf_op jit(solution)/shard_map/all_to_all | solution.py:114
  91.4 15.4 %collective-permute-start = (bf16[256,128]{0,1:T(8,128)(2,1)S(1)}, bf16[256,128]{0,1:T(8,128)(2,1)S(1)}, u32[]{:S(2)}, u32[]{:S(2)}) collective-permute-start(bf16[256,128]{0,1:T(8,128)(2,1)S(1)} %pad_maximum_fusion.3), channel_id=1, source_target_pairs={{0,1},{1,0},{2,3},{3,2},{4,5},{5,4},{6,7},{7,6},{8,9},{9,8},{10,11... | collective-permute-start | bytes 196616 | tf_op jit(solution)/shard_map/ppermute | solution.py:108
  104.3 1.9 %copy-start.2 = (f32[128,256]{1,0:T(8,128)S(1)}, f32[128,256]{1,0:T(8,128)}, u32[]{:S(2)}) copy-start(f32[128,256]{1,0:T(8,128)} %param.7) | copy-start | bytes 393220
  106.4 14.9 %copy-start.1 = (f32[128,256]{1,0:T(8,128)}, f32[128,256]{1,0:T(8,128)S(1)}, u32[]{:S(2)}) copy-start(f32[128,256]{1,0:T(8,128)S(1)} %convolution_add_fusion.3) | copy-start | bytes 393220
  107.2 12.0 %collective-permute-start.1 = (bf16[128,128]{0,1:T(8,128)(2,1)S(1)}, bf16[128,128]{0,1:T(8,128)(2,1)S(1)}, u32[]{:S(2)}, u32[]{:S(2)}) collective-permute-start(bf16[128,128]{0,1:T(8,128)(2,1)S(1)} %get-tuple-element.35), channel_id=1, source_target_pairs={{0,64},{64,128},{128,192},{192,256},{256,320},{320,384},{384,448},... | collective-permute-start | bytes 98312 | tf_op jit(solution)/shard_map/ppermute | solution.py:145
  111.7 7.5 %collective-permute-start.2 = (bf16[128,128]{0,1:T(8,128)(2,1)S(1)}, bf16[128,128]{0,1:T(8,128)(2,1)S(1)}, u32[]{:S(2)}, u32[]{:S(2)}) collective-permute-start(bf16[128,128]{0,1:T(8,128)(2,1)S(1)} %get-tuple-element.35), channel_id=1, source_target_pairs={{64,0},{128,64},{192,128},{256,192},{320,256},{384,320},{448,384},... | collective-permute-start | bytes 98312 | tf_op jit(solution)/shard_map/ppermute | solution.py:146
  113.7 5.6 %collective-permute-start.3 = (bf16[128,128]{0,1:T(8,128)(2,1)S(1)}, bf16[128,128]{0,1:T(8,128)(2,1)S(1)}, u32[]{:S(2)}, u32[]{:S(2)}) collective-permute-start(bf16[128,128]{0,1:T(8,128)(2,1)S(1)} %get-tuple-element.35), channel_id=1, source_target_pairs={{0,2},{2,4},{4,6},{6,8},{8,10},{10,12},{12,14},{14,16},{16,18},{18... | collective-permute-start | bytes 98312 | tf_op jit(solution)/shard_map/ppermute | solution.py:145
  115.9 4.7 %collective-permute-start.4 = (bf16[128,128]{0,1:T(8,128)(2,1)S(1)}, bf16[128,128]{0,1:T(8,128)(2,1)S(1)}, u32[]{:S(2)}, u32[]{:S(2)}) collective-permute-start(bf16[128,128]{0,1:T(8,128)(2,1)S(1)} %get-tuple-element.35), channel_id=1, source_target_pairs={{2,0},{4,2},{6,4},{8,6},{10,8},{12,10},{14,12},{16,14},{18,16},{20... | collective-permute-start | bytes 98312 | tf_op jit(solution)/shard_map/ppermute | solution.py:146

commit v10 on v9

--- a/solution.py
+++ b/solution.py
@@ -64,7 +64,7 @@
     noted = kept[0] + first_row + first_square.astype(jnp.int32)
     empty = jnp.broadcast_to(noted.astype(LOW), (ring - pieces, rows, own_count))
     sent = jnp.concatenate([proj_part.reshape(pieces, rows, own_count), empty], axis=0)
-    sent = jnp.concatenate([sent, own_piece.T.reshape(ring, few, own_count)], axis=1)
+    sent = jnp.concatenate([sent, after(own_piece.T, proj_part[:width]).reshape(ring, few, own_count)], axis=1)
     taken = lax.all_to_all(sent, ring_axes, 0, 0)
     proj_rows = taken[:, :rows].reshape(slabs, 2, rows, own_count).astype(WIDE).sum(0).astype(LOW)
     voxels = taken[:, rows:].reshape(slabs, 2, few, own_count)
@@ -106,7 +106,10 @@
     summed = summed.astype(WIDE).sum(0).astype(LOW)
     own_stats = summed[:own_count]
     other = lax.ppermute(jnp.concatenate([own_stats, own_piece], axis=0), "comp", SWAP)
-    other_stats, other_piece = other[:own_count], other[own_count:]
+    both_stats, both_piece = [
+        jnp.where(comp == 0, jnp.concatenate([mine, far], axis=0), jnp.concatenate([far, mine], axis=0)).astype(WIDE)
+        for mine, far in ((own_stats, other[:own_count]), (own_piece, other[own_count:]))
+    ]
     mine = summed[own_count:]
     late_rows = after(proj_rows, mine[:rows])
     shared = jnp.concatenate([mine, late_rows[1], mine, late_rows[0]], axis=0).reshape(2, -1, own_count)
@@ -127,15 +130,12 @@
     from_other = lax.dynamic_slice_in_dim(own_coding, (1 - comp) * own_count, own_count, 0)
     codes = jnp.dot(proj_own.astype(WIDE), from_own, precision=fine)
     codes = codes + jnp.dot(proj_other.astype(WIDE), from_other, precision=fine)
-    added = jnp.dot(from_own.T, own_stats.astype(WIDE), precision=fine)
-    added = added + jnp.dot(from_other.T, other_stats.astype(WIDE), precision=fine)
+    added = jnp.dot(own_coding.T, both_stats, precision=fine)
     stats_line = 0.5 * stats_old.reshape(own_count, width) + added
     gram_new = 0.5 * gram_old + product
     block = lax.dynamic_slice_in_dim(gram_new, comp * own_count, own_count, 1)
-    other_block = lax.dynamic_slice_in_dim(gram_new, (1 - comp) * own_count, own_count, 1)
     diag = jnp.sum(block * jnp.eye(own_count, dtype=WIDE), axis=1, keepdims=True)
-    coupled = jnp.dot(block, own_piece.astype(WIDE), precision=fine)
-    coupled = coupled + jnp.dot(other_block, other_piece.astype(WIDE), precision=fine)
+    coupled = jnp.dot(gram_new, both_piece, precision=fine)
     updated = own_piece.astype(WIDE) + (stats_line - coupled) / diag
     edge = updated.astype(LOW)
     sides = []

time: 123 us -> 124 us (level)
  waiting for transfers between devices: 6.59 us -> 9.14 us
    ppermute x1, waiting for transfers between devices: 0.01 us -> 7.82 us  [on_device(): lax.ppermute(jnp.concatenate([own_stats, own_piece], axis=0), 'comp', SWAP)]
    all_to_all x1, waiting for transfers between devices: 5.26 us -> 0.01 us  [on_device(): shared = lax.all_to_all(shared, ring_axes, 0, 0)]
    unnamed x13 -> x12, local copies, waits for them, and re-layouts: 2.89 us -> 2.16 us
  transfers between devices with their start and end apart: 6 -> 6, of which waited for: 2 -> 2; matrix products, arithmetic and copies ran while one was open for 4% -> 2% of each run, Pallas kernels for 0% -> 0%
where the time goes in v10:
time: 124 us; the launch traced here: 122 us
  blocking collectives  71.5 us (58%)
  starting transfers between devices  23.9 us (19%)
  matrix products  11.2 us (9%)
  waiting for transfers between devices  9.14 us (7%)
  local copies, waits for them, and re-layouts  3.49 us (3%)
  between operations  1.86 us (2%)
    all_to_all x1, blocking collectives, on_device(): taken = lax.all_to_all(sent, ring_axes, 0, 0)  21.2 us
    all_to_all x1, blocking collectives, on_device(): lax.all_to_all(sent, 'subj', 0, 0, axis_index_groups=x_groups).astype(WIDE)  18.1 us
    all_to_all x1, blocking collectives, on_device(): summed = lax.all_to_all(sent, 'subj', 0, 0, axis_index_groups=y_groups)  17.6 us
    all_to_all x1, blocking collectives, on_device(): lax.all_to_all(jnp.concatenate([to_owner, shares], axis=1), ring_axes, 0, 0)  14.5 us
    ppermute x1, waiting for transfers between devices, on_device(): lax.ppermute(jnp.concatenate([own_stats, own_piece], axis=0), 'comp', SWAP)  7.82 us
    all_to_all x1, starting transfers between devices, on_device(): shared = lax.all_to_all(shared, ring_axes, 0, 0)  7.58 us
    ppermute x1, starting transfers between devices, on_device(): lax.ppermute(jnp.concatenate([own_stats, own_piece], axis=0), 'comp', SWAP)  7.2 us
    ppermute x2, starting transfers between devices, on_device(): sides.append(lax.ppermute(edge, axis, up) + 0.0)  5.94 us
  transfers between devices with their start and end apart: 6, of which 2 were waited for; matrix products, arithmetic and copies ran while one was open for 2% of the time, Pallas kernels for 0%

profile of v10, /device:TPU:1, one launch (start us, length us, event | category | flops | bytes accessed | tf_op | source)
XLA Modules:
  0.0 122.0 jit_solution(8427561789703254720)
XLA Ops:
  1.4 0.5 copy-done
  2.1 3.4 %fusion.14 = bf16[448,128]{1,0:T(8,128)(2,1)S(1)} fusion(bf16[448,32,128]{2,1,0:T(8,128)(2,1)} %bitcast.99, bf16[128,32,128]{2,1,0:T(8,128)(2,1)S(1)} %bitcast.97), kind=kOutput, calls=%fused_computation.13 | convolution fusion | flops 469876736 | bytes 4833280 | tf_op jit(solution)/shard_map/ryx,kyx->rk/dot_general | solution.py:55
  5.5 21.2 %all_to_all.25 = bf16[16,40,128]{2,1,0:T(8,128)(2,1)S(1)} all-to-all(bf16[16,40,128]{2,1,0:T(8,128)(2,1)S(1)} %fusion.29), channel_id=1, replica_groups=mesh['slab'=8,'subj'=32,'comp'=2] {'slab','comp'}, dimensions={0} | all-to-all | bytes 327680 | tf_op jit(solution)/shard_map/all_to_all | solution.py:68
  26.8 0.2 fusion.13
  27.1 0.2 fusion.20
  27.4 14.5 %all_to_all.26 = bf16[16,64,128]{2,1,0:T(8,128)(2,1)S(1)} all-to-all(bf16[16,64,128]{2,1,0:T(8,128)(2,1)S(1)} %pad_maximum_fusion.2), channel_id=1, replica_groups=mesh['slab'=8,'subj'=32,'comp'=2] {'slab','comp'}, dimensions={0} | all-to-all | bytes 524288 | tf_op jit(solution)/shard_map/all_to_all | solution.py:82
  41.9 3.6 %multiply_convert_fusion = bf16[128,32,128]{2,0,1:T(8,128)(2,1)S(1)} fusion(bf16[448,128,1]{1,0,2:T(8,128)(2,1)S(1)} %bitcast.106, bf16[448,32,128]{2,1,0:T(8,128)(2,1)} %bitcast.100), kind=kOutput, calls=%fused_computation.4 | convolution fusion | flops 470810624 | bytes 4833280 | tf_op jit(solution)/shard_map/rk,ryx->ykx/dot_general | solution.py:89
  45.5 0.2 convolution_bitcast_fusion
  45.9 18.1 %all_to_all.27 = bf16[4,1072,128]{2,1,0:T(8,128)(2,1)S(1)} all-to-all(bf16[4,1072,128]{2,1,0:T(8,128)(2,1)S(1)} %pad_maximum_fusion), channel_id=1, replica_groups={{0,16,32,48},{2,18,34,50},{4,20,36,52},{6,22,38,54},{8,24,40,56},{10,26..., dimensions={0} | all-to-all | bytes 2195456 | tf_op jit(solution)/shard_map/all_to_all | solution.py:95
  64.1 0.3 reduce_sum.59
  64.5 17.6 %all_to_all.28 = bf16[8,176,128]{2,1,0:T(8,128)(2,1)S(1)} all-to-all(bf16[8,176,128]{2,1,0:T(8,128)(2,1)S(1)} %pad_maximum_fusion.1), channel_id=1, replica_groups={{0,2,4,6,8,10,12,14},{16,18,20,22,24,26,28,30},{32,34,36,38,40,42,44,46..., dimensions={0} | all-to-all | bytes 720896 | tf_op jit(solution)/shard_map/all_to_all | solution.py:105
  82.1 0.8 broadcast_in_dim.28
  82.9 7.6 %all-to-all-start.4 = ((bf16[16,80,128]{2,1,0:T(8,128)(2,1)}), bf16[16,80,128]{2,1,0:T(8,128)(2,1)S(1)}, u32[]{:S(2)}, u32[]{:S(2)}) async-start(bf16[16,80,128]{2,1,0:T(8,128)(2,1)} %bitcast.31), calls=%async_computation.4 | async-start | bytes 655360 | tf_op jit(solution)/shard_map/all_to_all | solution.py:117
  90.6 7.2 %collective-permute-start = (bf16[256,128]{0,1:T(8,128)(2,1)S(1)}, bf16[256,128]{0,1:T(8,128)(2,1)S(1)}, u32[]{:S(2)}, u32[]{:S(2)}) collective-permute-start(bf16[256,128]{0,1:T(8,128)(2,1)S(1)} %pad_maximum_fusion.4), channel_id=1, source_target_pairs={{0,1},{1,0},{2,3},{3,2},{4,5},{5,4},{6,7},{7,6},{8,9},{9,8},{10,11... | collective-permute-start | bytes 196616 | tf_op jit(solution)/shard_map/ppermute | solution.py:108
  98.0 7.8 %collective-permute-done = bf16[256,128]{0,1:T(8,128)(2,1)S(1)} collective-permute-done((bf16[256,128]{0,1:T(8,128)(2,1)S(1)}, bf16[256,128]{0,1:T(8,128)(2,1)S(1)}, u32[]{:S(2)}, u32[]{:S(2)}) %collective-permute-start) | collective-permute-done | bytes 65568 | tf_op jit(solution)/shard_map/ppermute | solution.py:108
  105.9 0.3 fusion.27
  106.3 0.3 fusion.26
  106.6 0.3 convolution_add_fusion.1
  106.9 0.3 fusion.107
  107.3 0.3 fusion.6
  107.6 0.3 fusion.30
  107.9 0.2 convolution_add_fusion.3
  108.5 0.2 fusion.106
  108.7 3.7 %collective-permute-start.1 = (bf16[128,128]{0,1:T(8,128)(2,1)S(1)}, bf16[128,128]{0,1:T(8,128)(2,1)S(1)}, u32[]{:S(2)}, u32[]{:S(2)}) collective-permute-start(bf16[128,128]{0,1:T(8,128)(2,1)S(1)} %get-tuple-element.37), channel_id=1, source_target_pairs={{0,64},{64,128},{128,192},{192,256},{256,320},{320,384},{384,448},... | collective-permute-start | bytes 98312 | tf_op jit(solution)/shard_map/ppermute | solution.py:145
  112.4 1.9 %collective-permute-start.2 = (bf16[128,128]{0,1:T(8,128)(2,1)S(1)}, bf16[128,128]{0,1:T(8,128)(2,1)S(1)}, u32[]{:S(2)}, u32[]{:S(2)}) collective-permute-start(bf16[128,128]{0,1:T(8,128)(2,1)S(1)} %get-tuple-element.37), channel_id=1, source_target_pairs={{64,0},{128,64},{192,128},{256,192},{320,256},{384,320},{448,384},... | collective-permute-start | bytes 98312 | tf_op jit(solution)/shard_map/ppermute | solution.py:146
  114.3 2.2 %collective-permute-start.3 = (bf16[128,128]{0,1:T(8,128)(2,1)S(1)}, bf16[128,128]{0,1:T(8,128)(2,1)S(1)}, u32[]{:S(2)}, u32[]{:S(2)}) collective-permute-start(bf16[128,128]{0,1:T(8,128)(2,1)S(1)} %get-tuple-element.37), channel_id=1, source_target_pairs={{0,2},{2,4},{4,6},{6,8},{8,10},{10,12},{12,14},{14,16},{16,18},{18... | collective-permute-start | bytes 98312 | tf_op jit(solution)/shard_map/ppermute | solution.py:145
  116.5 1.3 %collective-permute-start.4 = (bf16[128,128]{0,1:T(8,128)(2,1)S(1)}, bf16[128,128]{0,1:T(8,128)(2,1)S(1)}, u32[]{:S(2)}, u32[]{:S(2)}) collective-permute-start(bf16[128,128]{0,1:T(8,128)(2,1)S(1)} %get-tuple-element.37), channel_id=1, source_target_pairs={{2,0},{4,2},{6,4},{8,6},{10,8},{12,10},{14,12},{16,14},{18,16},{20... | collective-permute-start | bytes 98312 | tf_op jit(solution)/shard_map/ppermute | solution.py:146
  117.8 0.3 fusion.67
  118.2 1.0 convolution_add_fusion.2
  119.1 0.7 copy.65
  119.9 1.3 %collective-permute-done.4 = bf16[128,128]{0,1:T(8,128)(2,1)S(1)} collective-permute-done((bf16[128,128]{0,1:T(8,128)(2,1)S(1)}, bf16[128,128]{0,1:T(8,128)(2,1)S(1)}, u32[]{:S(2)}, u32[]{:S(2)}) %collective-permute-start.4) | collective-permute-done | bytes 32800 | tf_op jit(solution)/shard_map/ppermute | solution.py:146
  121.3 0.7 copy.64
  (53 shorter events, 1.6 us)
Async XLA Ops:
  0.6 1.2 %copy-start = (bf16[128,1,32,128]{3,2,1,0:T(8,128)(2,1)S(1)}, bf16[128,1,32,128]{3,2,1,0:T(8,128)(2,1)}, u32[]{:S(2)}) copy-start(bf16[128,1,32,128]{3,2,1,0:T(8,128)(2,1)} %param.6) | copy-start | bytes 3145732
  64.4 33.5 %copy-start.3 = (f32[128,1,1,128]{3,2,1,0:T(1,128)S(1)}, f32[128,1,1,128]{3,2,1,0:T(1,128)}, u32[]{:S(2)}) copy-start(f32[128,1,1,128]{3,2,1,0:T(1,128)} %param.8) | copy-start | bytes 196612
  82.9 22.9 %all-to-all-start.4 = ((bf16[16,80,128]{2,1,0:T(8,128)(2,1)}), bf16[16,80,128]{2,1,0:T(8,128)(2,1)S(1)}, u32[]{:S(2)}, u32[]{:S(2)}) async-start(bf16[16,80,128]{2,1,0:T(8,128)(2,1)} %bitcast.31), calls=%async_computation.4 | async-start | bytes 655360 | tf_op jit(solution)/shard_map/all_to_all | solution.py:117
  90.6 15.2 %collective-permute-start = (bf16[256,128]{0,1:T(8,128)(2,1)S(1)}, bf16[256,128]{0,1:T(8,128)(2,1)S(1)}, u32[]{:S(2)}, u32[]{:S(2)}) collective-permute-start(bf16[256,128]{0,1:T(8,128)(2,1)S(1)} %pad_maximum_fusion.4), channel_id=1, source_target_pairs={{0,1},{1,0},{2,3},{3,2},{4,5},{5,4},{6,7},{7,6},{8,9},{9,8},{10,11... | collective-permute-start | bytes 196616 | tf_op jit(solution)/shard_map/ppermute | solution.py:108
  106.3 1.6 %copy-start.2 = (f32[128,256]{1,0:T(8,128)S(1)}, f32[128,256]{1,0:T(8,128)}, u32[]{:S(2)}) copy-start(f32[128,256]{1,0:T(8,128)} %param.7) | copy-start | bytes 393220
  108.1 13.9 %copy-start.1 = (f32[128,256]{1,0:T(8,128)}, f32[128,256]{1,0:T(8,128)S(1)}, u32[]{:S(2)}) copy-start(f32[128,256]{1,0:T(8,128)S(1)} %convolution_add_fusion.3) | copy-start | bytes 393220
  108.7 11.2 %collective-permute-start.1 = (bf16[128,128]{0,1:T(8,128)(2,1)S(1)}, bf16[128,128]{0,1:T(8,128)(2,1)S(1)}, u32[]{:S(2)}, u32[]{:S(2)}) collective-permute-start(bf16[128,128]{0,1:T(8,128)(2,1)S(1)} %get-tuple-element.37), channel_id=1, source_target_pairs={{0,64},{64,128},{128,192},{192,256},{256,320},{320,384},{384,448},... | collective-permute-start | bytes 98312 | tf_op jit(solution)/shard_map/ppermute | solution.py:145
  112.4 7.5 %collective-permute-start.2 = (bf16[128,128]{0,1:T(8,128)(2,1)S(1)}, bf16[128,128]{0,1:T(8,128)(2,1)S(1)}, u32[]{:S(2)}, u32[]{:S(2)}) collective-permute-start(bf16[128,128]{0,1:T(8,128)(2,1)S(1)} %get-tuple-element.37), channel_id=1, source_target_pairs={{64,0},{128,64},{192,128},{256,192},{320,256},{384,320},{448,384},... | collective-permute-start | bytes 98312 | tf_op jit(solution)/shard_map/ppermute | solution.py:146
  114.3 5.5 %collective-permute-start.3 = (bf16[128,128]{0,1:T(8,128)(2,1)S(1)}, bf16[128,128]{0,1:T(8,128)(2,1)S(1)}, u32[]{:S(2)}, u32[]{:S(2)}) collective-permute-start(bf16[128,128]{0,1:T(8,128)(2,1)S(1)} %get-tuple-element.37), channel_id=1, source_target_pairs={{0,2},{2,4},{4,6},{6,8},{8,10},{10,12},{12,14},{14,16},{16,18},{18... | collective-permute-start | bytes 98312 | tf_op jit(solution)/shard_map/ppermute | solution.py:145
  116.5 4.7 %collective-permute-start.4 = (bf16[128,128]{0,1:T(8,128)(2,1)S(1)}, bf16[128,128]{0,1:T(8,128)(2,1)S(1)}, u32[]{:S(2)}, u32[]{:S(2)}) collective-permute-start(bf16[128,128]{0,1:T(8,128)(2,1)S(1)} %get-tuple-element.37), channel_id=1, source_target_pairs={{2,0},{4,2},{6,4},{8,6},{10,8},{12,10},{14,12},{16,14},{18,16},{20... | collective-permute-start | bytes 98312 | tf_op jit(solution)/shard_map/ppermute | solution.py:146

commit v11 on v9

--- a/solution.py
+++ b/solution.py
@@ -67,8 +67,8 @@
     sent = jnp.concatenate([sent, own_piece.T.reshape(ring, few, own_count)], axis=1)
     taken = lax.all_to_all(sent, ring_axes, 0, 0)
     proj_rows = taken[:, :rows].reshape(slabs, 2, rows, own_count).astype(WIDE).sum(0).astype(LOW)
-    voxels = taken[:, rows:].reshape(slabs, 2, few, own_count)
-    voxels = jnp.concatenate([voxels[:, i].reshape(slabs * few, own_count) for i in range(2)], axis=1)
+    held = taken[:, rows:].reshape(slabs, 2, few, own_count)
+    voxels = jnp.concatenate([held[:, i].reshape(slabs * few, own_count) for i in range(2)], axis=1)
     gram_part = jnp.dot(voxels.T, voxels, preferred_element_type=WIDE) * (1.0 / voxel_total)
     product_scale = 0.5 / total_rows
     at_row = after(lax.broadcasted_iota(jnp.int32, (rows, own_count), 0), proj_rows[0])
@@ -105,19 +105,23 @@
     summed = lax.all_to_all(sent, "subj", 0, 0, axis_index_groups=y_groups)
     summed = summed.astype(WIDE).sum(0).astype(LOW)
     own_stats = summed[:own_count]
-    other = lax.ppermute(jnp.concatenate([own_stats, own_piece], axis=0), "comp", SWAP)
-    other_stats, other_piece = other[:own_count], other[own_count:]
+    other_stats = lax.ppermute(own_stats, "comp", SWAP)
     mine = summed[own_count:]
     late_rows = after(proj_rows, mine[:rows])
     shared = jnp.concatenate([mine, late_rows[1], mine, late_rows[0]], axis=0).reshape(2, -1, own_count)
-    shared = jnp.broadcast_to(shared, (slabs,) + shared.shape).reshape(ring, -1, own_count)
+    late_held = after(held, mine[:few])
+    late_held = jnp.concatenate([late_held[:, 1:], late_held[:, :1]], axis=1)
+    shared = jnp.concatenate([jnp.broadcast_to(shared, (slabs,) + shared.shape), late_held], axis=2)
+    shared = shared.reshape(ring, -1, own_count)
     shared = lax.all_to_all(shared, ring_axes, 0, 0)
 
     squares = shared[:, :square].reshape(slabs, 2, square, own_count)
     low_block, high_block, cross, product_cross = [
         shared[:, square + i * few : square + (i + 1) * few].reshape(own_count, own_count) for i in range(4)
     ]
-    proj_other = shared[:pieces, square + 4 * few :].reshape(volumes, own_count)
+    proj_at = square + 4 * few
+    proj_other = shared[:pieces, proj_at : proj_at + rows].reshape(volumes, own_count)
+    other_piece = shared[:, proj_at + rows :].reshape(width, own_count).T
     gram = symmetric(low_block, cross, high_block)
     product = symmetric(squares[:, 0].reshape(own_count, own_count), product_cross, squares[:, 1].reshape(own_count, own_count))
     coding = power_sum(gram)

time: 123 us -> 123 us (level)
  local copies, waits for them, and re-layouts: 4.21 us -> 2.66 us
    unnamed x13 -> x11, local copies, waits for them, and re-layouts: 2.89 us -> 2.05 us
where the time goes in v11:
time: 123 us; the launch traced here: 121 us
  blocking collectives  71.4 us (58%)
  starting transfers between devices  24.6 us (20%)
  matrix products  11.8 us (10%)
  waiting for transfers between devices  7.33 us (6%)
  local copies, waits for them, and re-layouts  2.66 us (2%)
  between operations  1.86 us (2%)
  other arithmetic  1.61 us (1%)
    all_to_all x1, blocking collectives, on_device(): taken = lax.all_to_all(sent, ring_axes, 0, 0)  21.2 us
    all_to_all x1, blocking collectives, on_device(): lax.all_to_all(sent, 'subj', 0, 0, axis_index_groups=x_groups).astype(WIDE)  18.2 us
    all_to_all x1, blocking collectives, on_device(): summed = lax.all_to_all(sent, 'subj', 0, 0, axis_index_groups=y_groups)  17.5 us
    all_to_all x1, blocking collectives, on_device(): lax.all_to_all(jnp.concatenate([to_owner, shares], axis=1), ring_axes, 0, 0)  14.5 us
    all_to_all x1, starting transfers between devices, on_device(): shared = lax.all_to_all(shared, ring_axes, 0, 0)  7.6 us
    ppermute x1, starting transfers between devices, on_device(): other_stats = lax.ppermute(own_stats, 'comp', SWAP)  7.2 us
    ppermute x2, starting transfers between devices, on_device(): sides.append(lax.ppermute(edge, axis, up) + 0.0)  6.62 us
    all_to_all x1, waiting for transfers between devices, on_device(): shared = lax.all_to_all(shared, ring_axes, 0, 0)  6.01 us
  transfers between devices with their start and end apart: 6, of which 2 were waited for; matrix products, arithmetic and copies ran while one was open for 4% of the time, Pallas kernels for 0%

profile of v11, /device:TPU:1, one launch (start us, length us, event | category | flops | bytes accessed | tf_op | source)
XLA Modules:
  0.0 121.3 jit_solution(16792574995011958704)
XLA Ops:
  1.4 0.5 copy-done
  2.1 3.4 %fusion.14 = bf16[448,128]{1,0:T(8,128)(2,1)S(1)} fusion(bf16[448,32,128]{2,1,0:T(8,128)(2,1)} %bitcast.106, bf16[128,32,128]{2,1,0:T(8,128)(2,1)S(1)} %bitcast.104), kind=kOutput, calls=%fused_computation.13 | convolution fusion | flops 469876736 | bytes 4833280 | tf_op jit(solution)/shard_map/ryx,kyx->rk/dot_general | solution.py:55
  5.5 21.2 %all_to_all.25 = bf16[16,40,128]{2,1,0:T(8,128)(2,1)S(1)} all-to-all(bf16[16,40,128]{2,1,0:T(8,128)(2,1)S(1)} %fusion.31), channel_id=1, replica_groups=mesh['slab'=8,'subj'=32,'comp'=2] {'slab','comp'}, dimensions={0} | all-to-all | bytes 327680 | tf_op jit(solution)/shard_map/all_to_all | solution.py:68
  26.7 0.2 fusion.13
  27.3 14.5 %all_to_all.26 = bf16[16,64,128]{2,1,0:T(8,128)(2,1)S(1)} all-to-all(bf16[16,64,128]{2,1,0:T(8,128)(2,1)S(1)} %pad_maximum_fusion.2), channel_id=1, replica_groups=mesh['slab'=8,'subj'=32,'comp'=2] {'slab','comp'}, dimensions={0} | all-to-all | bytes 524288 | tf_op jit(solution)/shard_map/all_to_all | solution.py:82
  41.9 3.6 %multiply_convert_fusion = bf16[128,32,128]{2,0,1:T(8,128)(2,1)S(1)} fusion(bf16[448,128,1]{1,0,2:T(8,128)(2,1)S(1)} %bitcast.115, bf16[448,32,128]{2,1,0:T(8,128)(2,1)} %bitcast.107), kind=kOutput, calls=%fused_computation.4 | convolution fusion | flops 470810624 | bytes 4833280 | tf_op jit(solution)/shard_map/rk,ryx->ykx/dot_general | solution.py:89
  45.5 0.2 convolution_bitcast_fusion
  45.9 18.2 %all_to_all.27 = bf16[4,1072,128]{2,1,0:T(8,128)(2,1)S(1)} all-to-all(bf16[4,1072,128]{2,1,0:T(8,128)(2,1)S(1)} %pad_maximum_fusion), channel_id=1, replica_groups={{0,16,32,48},{2,18,34,50},{4,20,36,52},{6,22,38,54},{8,24,40,56},{10,26..., dimensions={0} | all-to-all | bytes 2195456 | tf_op jit(solution)/shard_map/all_to_all | solution.py:95
  64.1 0.3 reduce_sum.59
  64.5 17.5 %all_to_all.28 = bf16[8,176,128]{2,1,0:T(8,128)(2,1)S(1)} all-to-all(bf16[8,176,128]{2,1,0:T(8,128)(2,1)S(1)} %pad_maximum_fusion.1), channel_id=1, replica_groups={{0,2,4,6,8,10,12,14},{16,18,20,22,24,26,28,30},{32,34,36,38,40,42,44,46..., dimensions={0} | all-to-all | bytes 720896 | tf_op jit(solution)/shard_map/all_to_all | solution.py:105
  82.2 0.8 maximum_maximum_fusion
  83.0 7.6 %all-to-all-start.4 = ((bf16[16,88,128]{2,1,0:T(8,128)(2,1)}), bf16[16,88,128]{2,1,0:T(8,128)(2,1)S(1)}, u32[]{:S(2)}, u32[]{:S(2)}) async-start(bf16[16,88,128]{2,1,0:T(8,128)(2,1)} %bitcast.31), calls=%async_computation.4 | async-start | bytes 720896 | tf_op jit(solution)/shard_map/all_to_all | solution.py:116
  90.7 7.2 %collective-permute-start = (bf16[128,128]{1,0:T(8,128)(2,1)S(1)}, bf16[128,128]{1,0:T(8,128)(2,1)S(1)}, u32[]{:S(2)}, u32[]{:S(2)}) collective-permute-start(bf16[128,128]{1,0:T(8,128)(2,1)S(1)} %slice.157), channel_id=1, source_target_pairs={{0,1},{1,0},{2,3},{3,2},{4,5},{5,4},{6,7},{7,6},{8,9},{9,8},{10,11... | collective-permute-start | bytes 98312 | tf_op jit(solution)/shard_map/ppermute | solution.py:108
  97.9 6.0 %all-to-all-done.4 = bf16[16,88,128]{2,1,0:T(8,128)(2,1)S(1)} async-done(((bf16[16,88,128]{2,1,0:T(8,128)(2,1)}), bf16[16,88,128]{2,1,0:T(8,128)(2,1)S(1)}, u32[]{:S(2)}, u32[]{:S(2)}) %all-to-all-start.4) | async-done | bytes 360480 | tf_op jit(solution)/shard_map/all_to_all | solution.py:116
  104.0 0.3 fusion.29
  104.4 0.3 fusion.28
  104.7 0.3 convolution_add_fusion.1
  105.0 0.3 fusion.99
  105.4 0.3 fusion.6
  105.7 0.3 fusion.60
  106.0 0.3 fusion.32
  106.3 0.2 convolution_add_fusion.3
  106.8 0.3 fusion.19
  107.3 4.4 %collective-permute-start.1 = (bf16[128,128]{0,1:T(8,128)(2,1)S(1)}, bf16[128,128]{0,1:T(8,128)(2,1)S(1)}, u32[]{:S(2)}, u32[]{:S(2)}) collective-permute-start(bf16[128,128]{0,1:T(8,128)(2,1)S(1)} %get-tuple-element.33), channel_id=1, source_target_pairs={{0,64},{64,128},{128,192},{192,256},{256,320},{320,384},{384,448},... | collective-permute-start | bytes 98312 | tf_op jit(solution)/shard_map/ppermute | solution.py:149
  111.7 1.9 %collective-permute-start.2 = (bf16[128,128]{0,1:T(8,128)(2,1)S(1)}, bf16[128,128]{0,1:T(8,128)(2,1)S(1)}, u32[]{:S(2)}, u32[]{:S(2)}) collective-permute-start(bf16[128,128]{0,1:T(8,128)(2,1)S(1)} %get-tuple-element.33), channel_id=1, source_target_pairs={{64,0},{128,64},{192,128},{256,192},{320,256},{384,320},{448,384},... | collective-permute-start | bytes 98312 | tf_op jit(solution)/shard_map/ppermute | solution.py:150
  113.7 2.2 %collective-permute-start.3 = (bf16[128,128]{0,1:T(8,128)(2,1)S(1)}, bf16[128,128]{0,1:T(8,128)(2,1)S(1)}, u32[]{:S(2)}, u32[]{:S(2)}) collective-permute-start(bf16[128,128]{0,1:T(8,128)(2,1)S(1)} %get-tuple-element.33), channel_id=1, source_target_pairs={{0,2},{2,4},{4,6},{6,8},{8,10},{10,12},{12,14},{14,16},{16,18},{18... | collective-permute-start | bytes 98312 | tf_op jit(solution)/shard_map/ppermute | solution.py:149
  115.9 1.3 %collective-permute-start.4 = (bf16[128,128]{0,1:T(8,128)(2,1)S(1)}, bf16[128,128]{0,1:T(8,128)(2,1)S(1)}, u32[]{:S(2)}, u32[]{:S(2)}) collective-permute-start(bf16[128,128]{0,1:T(8,128)(2,1)S(1)} %get-tuple-element.33), channel_id=1, source_target_pairs={{2,0},{4,2},{6,4},{8,6},{10,8},{12,10},{14,12},{16,14},{18,16},{20... | collective-permute-start | bytes 98312 | tf_op jit(solution)/shard_map/ppermute | solution.py:150
  117.2 0.3 fusion.58
  117.5 1.0 convolution_add_fusion.2
  118.5 0.7 copy.46
  119.2 1.3 %collective-permute-done.4 = bf16[128,128]{0,1:T(8,128)(2,1)S(1)} collective-permute-done((bf16[128,128]{0,1:T(8,128)(2,1)S(1)}, bf16[128,128]{0,1:T(8,128)(2,1)S(1)}, u32[]{:S(2)}, u32[]{:S(2)}) %collective-permute-start.4) | collective-permute-done | bytes 32800 | tf_op jit(solution)/shard_map/ppermute | solution.py:150
  120.6 0.7 copy.45
  (55 shorter events, 1.9 us)
Async XLA Ops:
  0.6 1.2 %copy-start = (bf16[128,1,32,128]{3,2,1,0:T(8,128)(2,1)S(1)}, bf16[128,1,32,128]{3,2,1,0:T(8,128)(2,1)}, u32[]{:S(2)}) copy-start(bf16[128,1,32,128]{3,2,1,0:T(8,128)(2,1)} %param.6) | copy-start | bytes 3145732
  64.4 26.2 %copy-start.3 = (f32[128,1,1,128]{3,2,1,0:T(1,128)S(1)}, f32[128,1,1,128]{3,2,1,0:T(1,128)}, u32[]{:S(2)}) copy-start(f32[128,1,1,128]{3,2,1,0:T(1,128)} %param.8) | copy-start | bytes 196612
  83.0 20.9 %all-to-all-start.4 = ((bf16[16,88,128]{2,1,0:T(8,128)(2,1)}), bf16[16,88,128]{2,1,0:T(8,128)(2,1)S(1)}, u32[]{:S(2)}, u32[]{:S(2)}) async-start(bf16[16,88,128]{2,1,0:T(8,128)(2,1)} %bitcast.31), calls=%async_computation.4 | async-start | bytes 720896 | tf_op jit(solution)/shard_map/all_to_all | solution.py:116
  90.7 16.1 %collective-permute-start = (bf16[128,128]{1,0:T(8,128)(2,1)S(1)}, bf16[128,128]{1,0:T(8,128)(2,1)S(1)}, u32[]{:S(2)}, u32[]{:S(2)}) collective-permute-start(bf16[128,128]{1,0:T(8,128)(2,1)S(1)} %slice.157), channel_id=1, source_target_pairs={{0,1},{1,0},{2,3},{3,2},{4,5},{5,4},{6,7},{7,6},{8,9},{9,8},{10,11... | collective-permute-start | bytes 98312 | tf_op jit(solution)/shard_map/ppermute | solution.py:108
  104.4 1.9 %copy-start.2 = (f32[128,256]{1,0:T(8,128)S(1)}, f32[128,256]{1,0:T(8,128)}, u32[]{:S(2)}) copy-start(f32[128,256]{1,0:T(8,128)} %param.7) | copy-start | bytes 393220
  106.5 14.8 %copy-start.1 = (f32[128,256]{1,0:T(8,128)}, f32[128,256]{1,0:T(8,128)S(1)}, u32[]{:S(2)}) copy-start(f32[128,256]{1,0:T(8,128)S(1)} %convolution_add_fusion.3) | copy-start | bytes 393220
  107.3 11.9 %collective-permute-start.1 = (bf16[128,128]{0,1:T(8,128)(2,1)S(1)}, bf16[128,128]{0,1:T(8,128)(2,1)S(1)}, u32[]{:S(2)}, u32[]{:S(2)}) collective-permute-start(bf16[128,128]{0,1:T(8,128)(2,1)S(1)} %get-tuple-element.33), channel_id=1, source_target_pairs={{0,64},{64,128},{128,192},{192,256},{256,320},{320,384},{384,448},... | collective-permute-start | bytes 98312 | tf_op jit(solution)/shard_map/ppermute | solution.py:149
  111.7 7.5 %collective-permute-start.2 = (bf16[128,128]{0,1:T(8,128)(2,1)S(1)}, bf16[128,128]{0,1:T(8,128)(2,1)S(1)}, u32[]{:S(2)}, u32[]{:S(2)}) collective-permute-start(bf16[128,128]{0,1:T(8,128)(2,1)S(1)} %get-tuple-element.33), channel_id=1, source_target_pairs={{64,0},{128,64},{192,128},{256,192},{320,256},{384,320},{448,384},... | collective-permute-start | bytes 98312 | tf_op jit(solution)/shard_map/ppermute | solution.py:150
  113.7 5.5 %collective-permute-start.3 = (bf16[128,128]{0,1:T(8,128)(2,1)S(1)}, bf16[128,128]{0,1:T(8,128)(2,1)S(1)}, u32[]{:S(2)}, u32[]{:S(2)}) collective-permute-start(bf16[128,128]{0,1:T(8,128)(2,1)S(1)} %get-tuple-element.33), channel_id=1, source_target_pairs={{0,2},{2,4},{4,6},{6,8},{8,10},{10,12},{12,14},{14,16},{16,18},{18... | collective-permute-start | bytes 98312 | tf_op jit(solution)/shard_map/ppermute | solution.py:149
  115.9 4.7 %collective-permute-start.4 = (bf16[128,128]{0,1:T(8,128)(2,1)S(1)}, bf16[128,128]{0,1:T(8,128)(2,1)S(1)}, u32[]{:S(2)}, u32[]{:S(2)}) collective-permute-start(bf16[128,128]{0,1:T(8,128)(2,1)S(1)} %get-tuple-element.33), channel_id=1, source_target_pairs={{2,0},{4,2},{6,4},{8,6},{10,8},{12,10},{14,12},{16,14},{18,16},{20... | collective-permute-start | bytes 98312 | tf_op jit(solution)/shard_map/ppermute | solution.py:150
